TPU v7x, 32 devices: a whole 2x2x4 slice. The times are simulated.
32 devices in a mesh: context: 8 (over z, core), tensor: 4 (over y, x).
Axes of the slice: x: 2, y: 2, z: 4, core: 2. Of those that a mesh axis runs over, the one named last changes fastest.
Arguments:
- tokens: bfloat16 [4, 2048, 2048], P(None, 'context'), may hold values from -6 to 6
- block_order: int32 [16], replicated, may hold values from 0 to 15, each once
- query_weight: bfloat16 [2048, 2048], P('context', 'tensor'), may hold values from -0.110485435 to 0.110485435
- key_weight: bfloat16 [2048, 2048], P('context', 'tensor'), may hold values from -0.110485435 to 0.110485435
- value_weight: bfloat16 [2048, 2048], P('context', 'tensor'), may hold values from -0.125 to 0.125
- output_weight: bfloat16 [2048, 2048], P('tensor', 'context'), may hold values from -0.125 to 0.125
- gate_weight: bfloat16 [2048, 8192], P('context', 'tensor'), may hold values from -0.125 to 0.125
- up_weight: bfloat16 [2048, 8192], P('context', 'tensor'), may hold values from -0.125 to 0.125
- down_weight: bfloat16 [8192, 2048], P('tensor', 'context'), may hold values from -0.0625 to 0.0625
- query_gain: bfloat16 [2048], P('tensor'), may hold values from 0.25 to 1.75
- key_gain: bfloat16 [2048], P('tensor'), may hold values from 0.25 to 1.75
- attention_gain: bfloat16 [2048], P('context'), may hold values from 0.25 to 1.75
- forward_gain: bfloat16 [2048], P('context'), may hold values from 0.25 to 1.75
- cotangent: bfloat16 [4, 2048, 2048], P(None, 'context'), may hold values from -6 to 6
Outputs:
- layer_output: bfloat16 [4, 2048, 2048], P(None, 'context')
- tokens_grad: float32 [4, 2048, 2048], P(None, 'context')
- query_weight_grad: float32 [2048, 2048], P('context', 'tensor')
- key_weight_grad: float32 [2048, 2048], P('context', 'tensor')
- value_weight_grad: float32 [2048, 2048], P('context', 'tensor')
- output_weight_grad: float32 [2048, 2048], P('tensor', 'context')
- gate_weight_grad: float32 [2048, 8192], P('context', 'tensor')
- up_weight_grad: float32 [2048, 8192], P('context', 'tensor')
- down_weight_grad: float32 [8192, 2048], P('tensor', 'context')
- query_gain_grad: float32 [2048], P('tensor')
- key_gain_grad: float32 [2048], P('tensor')
- attention_gain_grad: float32 [2048], P('context')
- forward_gain_grad: float32 [2048], P('context')
Inputs may be any that keep to these rules, and one draw needn't show every extreme that they name: `block_order`: each number once.
All inputs are finite; a program needn't handle non-finite values.
Results may differ from a plain program's by a relative error of at most 0.015.
Values may be sent and summed in bfloat16 or wider, within the bound.
A program may use at most 320 MiB of HBM per device.

v0:
```python
import jax
import jax.numpy as jnp
from jax import lax
from jax.sharding import PartitionSpec as P

HD = 128


EPS = 1e-06
THETA = 500000.0


def post_norm(branch, gain):
    factor = lax.rsqrt(jnp.mean(branch * branch, axis=-1, keepdims=True) + EPS)
    return branch * factor * gain


def swiglu(gate, up):
    return jax.nn.silu(gate) * up


def rotate(values, cosine, sine):
    half = values.shape[-1] // 2
    turned = jnp.concatenate([-values[..., half:], values[..., :half]], axis=-1)
    return values * cosine + turned * sine


def place_of(stored, block_order, piece_len):
    slots = jnp.arange(block_order.shape[0], dtype=jnp.int32)
    hits = (stored // piece_len)[:, None] == slots[None, :]
    picked = jnp.sum(jnp.where(hits, block_order[None, :], 0), axis=1)
    return picked * piece_len + stored % piece_len


def rotary_of(place, head_size):
    freq = THETA ** (-jnp.arange(0, head_size, 2, dtype=jnp.float32) / head_size)
    angle = place.astype(jnp.float32)[:, None] * freq[None, :]
    cosine = jnp.concatenate([jnp.cos(angle), jnp.cos(angle)], axis=-1)[:, None, :]
    sine = jnp.concatenate([jnp.sin(angle), jnp.sin(angle)], axis=-1)[:, None, :]
    return (cosine, sine)


def by_transpose(left, right):
    return lax.dot_general(
        left, right, (((1,), (1,)), ((), ())), preferred_element_type=jnp.float32
    )


def transpose_by(left, right):
    return lax.dot_general(
        left, right, (((0,), (0,)), ((), ())), preferred_element_type=jnp.float32
    )


def attention_scores(queries, keys, allowed):
    raw = jnp.einsum("sqhd,skhd->shqk", queries, keys, preferred_element_type=jnp.float32)
    raw = raw * queries.shape[-1] ** (-0.5)
    return jnp.where(allowed[None, None], raw, -1e30)


def local(
    tokens,
    block_order,
    query_weight,
    key_weight,
    value_weight,
    output_weight,
    gate_weight,
    up_weight,
    down_weight,
    query_gain,
    key_gain,
    attention_gain,
    forward_gain,
    cotangent,
):
    seqs, local_len, width = tokens.shape
    full_len = local_len * lax.axis_size("context")
    count = seqs * local_len
    rows = tokens.reshape(count, width)
    piece_len = full_len // block_order.shape[0]
    local_stored = lax.axis_index("context") * local_len + jnp.arange(local_len, dtype=jnp.int32)
    query_place = place_of(local_stored, block_order, piece_len)
    key_place = place_of(jnp.arange(full_len, dtype=jnp.int32), block_order, piece_len)
    allowed = query_place[:, None] >= key_place[None, :]
    cosine, sine = rotary_of(query_place, HD)
    w_query, w_key, w_value, w_output, w_gate, w_up, w_down, gain_attn, gain_feed = (
        lax.all_gather(query_weight, "context", axis=0, tiled=True),
        lax.all_gather(key_weight, "context", axis=0, tiled=True),
        lax.all_gather(value_weight, "context", axis=0, tiled=True),
        lax.all_gather(output_weight, "context", axis=1, tiled=True),
        lax.all_gather(gate_weight, "context", axis=0, tiled=True),
        lax.all_gather(up_weight, "context", axis=0, tiled=True),
        lax.all_gather(down_weight, "context", axis=1, tiled=True),
        lax.all_gather(attention_gain, "context", axis=0, tiled=True),
        lax.all_gather(forward_gain, "context", axis=0, tiled=True),
    )
    gain_attn32 = gain_attn.astype(jnp.float32)
    gain_feed32 = gain_feed.astype(jnp.float32)
    query_scaling = query_gain.astype(jnp.float32)
    key_scaling = key_gain.astype(jnp.float32)
    query_raw = jnp.dot(rows, w_query, preferred_element_type=jnp.float32)
    key_raw = jnp.dot(rows, w_key, preferred_element_type=jnp.float32)
    value_low = jnp.dot(rows, w_value, preferred_element_type=jnp.float32).astype(jnp.bfloat16)
    query_total, key_total = lax.psum(
        (jnp.sum(query_raw * query_raw, axis=1), jnp.sum(key_raw * key_raw, axis=1)), "tensor"
    )
    query_factor = lax.rsqrt(query_total / width + EPS)[:, None]
    key_factor = lax.rsqrt(key_total / width + EPS)[:, None]
    heads = query_raw.shape[1] // HD
    query_normed = (query_raw * query_factor * query_scaling).reshape(seqs, local_len, heads, HD)
    key_normed = (key_raw * key_factor * key_scaling).reshape(seqs, local_len, heads, HD)
    query_low = rotate(query_normed, cosine, sine).astype(jnp.bfloat16)
    key_low = rotate(key_normed, cosine, sine).astype(jnp.bfloat16)
    key_full, value_full = (
        lax.all_gather(key_low.reshape(seqs, local_len, heads * HD), "context", axis=1, tiled=True),
        lax.all_gather(
            value_low.reshape(seqs, local_len, heads * HD), "context", axis=1, tiled=True
        ),
    )
    keys = key_full.reshape(seqs, full_len, heads, HD)
    values = value_full.reshape(seqs, full_len, heads, HD)
    scores = attention_scores(query_low, keys, allowed)
    total_log = jax.nn.logsumexp(scores, axis=-1, keepdims=True)
    probs_low = jnp.exp(scores - total_log).astype(jnp.bfloat16)
    mixed_low = jnp.einsum("shqk,skhd->sqhd", probs_low, values, preferred_element_type=jnp.float32)
    mixed_low = mixed_low.astype(jnp.bfloat16).reshape(count, heads * HD)
    attended = lax.psum(jnp.dot(mixed_low, w_output, preferred_element_type=jnp.float32), "tensor")
    hidden = rows.astype(jnp.float32) + post_norm(attended, gain_attn32)
    hidden_low = hidden.astype(jnp.bfloat16)
    gate = jnp.dot(hidden_low, w_gate, preferred_element_type=jnp.float32)
    up = jnp.dot(hidden_low, w_up, preferred_element_type=jnp.float32)
    act_low = swiglu(gate, up).astype(jnp.bfloat16)
    fed = lax.psum(jnp.dot(act_low, w_down, preferred_element_type=jnp.float32), "tensor")
    layer_output = (
        (hidden + post_norm(fed, gain_feed32)).astype(jnp.bfloat16).reshape(seqs, local_len, width)
    )
    w_query, w_key, w_value, w_output, w_gate, w_up, w_down = (
        lax.all_gather(query_weight, "context", axis=0, tiled=True),
        lax.all_gather(key_weight, "context", axis=0, tiled=True),
        lax.all_gather(value_weight, "context", axis=0, tiled=True),
        lax.all_gather(output_weight, "context", axis=1, tiled=True),
        lax.all_gather(gate_weight, "context", axis=0, tiled=True),
        lax.all_gather(up_weight, "context", axis=0, tiled=True),
        lax.all_gather(down_weight, "context", axis=1, tiled=True),
    )
    key_full, value_full = (
        lax.all_gather(key_low.reshape(seqs, local_len, heads * HD), "context", axis=1, tiled=True),
        lax.all_gather(
            value_low.reshape(seqs, local_len, heads * HD), "context", axis=1, tiled=True
        ),
    )
    keys = key_full.reshape(seqs, full_len, heads, HD)
    values = value_full.reshape(seqs, full_len, heads, HD)
    upstream = cotangent.reshape(count, width).astype(jnp.float32)
    unused, feed_back = jax.vjp(post_norm, fed, gain_feed32)
    fed_grad, feed_gain_grad = feed_back(upstream)
    fed_low = fed_grad.astype(jnp.bfloat16)
    act_grad = by_transpose(fed_low, w_down)
    unused, glu_back = jax.vjp(swiglu, gate, up)
    gate_grad, up_grad = glu_back(act_grad)
    gate_low = gate_grad.astype(jnp.bfloat16)
    up_low = up_grad.astype(jnp.bfloat16)
    hidden_grad = upstream + lax.psum(
        by_transpose(gate_low, w_gate) + by_transpose(up_low, w_up), "tensor"
    )
    unused, attn_back = jax.vjp(post_norm, attended, gain_attn32)
    attended_grad, attn_gain_grad = attn_back(hidden_grad)
    attended_low = attended_grad.astype(jnp.bfloat16)
    mixed_grad = (
        by_transpose(attended_low, w_output)
        .astype(jnp.bfloat16)
        .reshape(seqs, local_len, heads, HD)
    )
    scores = attention_scores(query_low, keys, allowed)
    probs = jnp.exp(scores - total_log)
    prob_grad = jnp.einsum(
        "sqhd,skhd->shqk", mixed_grad, values, preferred_element_type=jnp.float32
    )
    spread = jnp.sum(probs * prob_grad, axis=-1, keepdims=True)
    score_low = (probs * (prob_grad - spread)).astype(jnp.bfloat16)
    step_scale = HD ** (-0.5)
    query_grad = (
        jnp.einsum("shqk,skhd->sqhd", score_low, keys, preferred_element_type=jnp.float32)
        * step_scale
    )
    probs_low = probs.astype(jnp.bfloat16)
    key_terms = (
        jnp.einsum("shqk,sqhd->skhd", score_low, query_low, preferred_element_type=jnp.float32)
        * step_scale
    )
    value_terms = jnp.einsum(
        "shqk,sqhd->skhd", probs_low, mixed_grad, preferred_element_type=jnp.float32
    )
    key_grad, value_grad = (
        lax.psum_scatter(
            key_terms.reshape(seqs, full_len, heads * HD),
            "context",
            scatter_dimension=1,
            tiled=True,
        ),
        lax.psum_scatter(
            value_terms.reshape(seqs, full_len, heads * HD),
            "context",
            scatter_dimension=1,
            tiled=True,
        ),
    )
    unused, query_turn = jax.vjp(lambda inner: rotate(inner, cosine, sine), query_normed)
    (query_normed_grad,) = query_turn(query_grad)
    unused, key_turn = jax.vjp(lambda inner: rotate(inner, cosine, sine), key_normed)
    (key_normed_grad,) = key_turn(key_grad.reshape(seqs, local_len, heads, HD))
    query_flat = query_normed_grad.reshape(count, heads * HD)
    key_flat = key_normed_grad.reshape(count, heads * HD)
    query_inner, key_inner = lax.psum(
        (
            jnp.sum(query_flat * query_scaling * query_raw, axis=1),
            jnp.sum(key_flat * key_scaling * key_raw, axis=1),
        ),
        "tensor",
    )
    query_raw_low = (
        query_factor * query_scaling * query_flat
        - query_raw * query_factor**3 * (query_inner / width)[:, None]
    ).astype(jnp.bfloat16)
    key_raw_low = (
        key_factor * key_scaling * key_flat - key_raw * key_factor**3 * (key_inner / width)[:, None]
    ).astype(jnp.bfloat16)
    query_gain_grad, key_gain_grad = lax.psum(
        (
            jnp.sum(query_flat * query_raw * query_factor, axis=0),
            jnp.sum(key_flat * key_raw * key_factor, axis=0),
        ),
        "context",
    )
    value_low_grad = value_grad.reshape(count, heads * HD).astype(jnp.bfloat16)
    tokens_grad = hidden_grad + lax.psum(
        by_transpose(query_raw_low, w_query)
        + by_transpose(key_raw_low, w_key)
        + by_transpose(value_low_grad, w_value),
        "tensor",
    )
    grads = (
        lax.psum_scatter(
            transpose_by(rows, query_raw_low), "context", scatter_dimension=0, tiled=True
        ),
        lax.psum_scatter(
            transpose_by(rows, key_raw_low), "context", scatter_dimension=0, tiled=True
        ),
        lax.psum_scatter(
            transpose_by(rows, value_low_grad), "context", scatter_dimension=0, tiled=True
        ),
        lax.psum_scatter(
            transpose_by(mixed_low, attended_low), "context", scatter_dimension=1, tiled=True
        ),
        lax.psum_scatter(
            transpose_by(hidden_low, gate_low), "context", scatter_dimension=0, tiled=True
        ),
        lax.psum_scatter(
            transpose_by(hidden_low, up_low), "context", scatter_dimension=0, tiled=True
        ),
        lax.psum_scatter(
            transpose_by(act_low, fed_low), "context", scatter_dimension=1, tiled=True
        ),
        lax.psum_scatter(attn_gain_grad, "context", scatter_dimension=0, tiled=True),
        lax.psum_scatter(feed_gain_grad, "context", scatter_dimension=0, tiled=True),
    )
    return (
        layer_output,
        tokens_grad.reshape(seqs, local_len, width),
        grads[0],
        grads[1],
        grads[2],
        grads[3],
        grads[4],
        grads[5],
        grads[6],
        query_gain_grad,
        key_gain_grad,
        grads[7],
        grads[8],
    )


def solution(mesh):
    return jax.shard_map(
        local,
        mesh=mesh,
        in_specs=(
            P(None, "context", None),
            P(),
            P("context", "tensor"),
            P("context", "tensor"),
            P("context", "tensor"),
            P("tensor", "context"),
            P("context", "tensor"),
            P("context", "tensor"),
            P("tensor", "context"),
            P("tensor"),
            P("tensor"),
            P("context"),
            P("context"),
            P(None, "context", None),
        ),
        out_specs=(
            P(None, "context", None),
            P(None, "context", None),
            P("context", "tensor"),
            P("context", "tensor"),
            P("context", "tensor"),
            P("tensor", "context"),
            P("context", "tensor"),
            P("context", "tensor"),
            P("tensor", "context"),
            P("tensor"),
            P("tensor"),
            P("context"),
            P("context"),
        ),
        check_vma=False,
    )
```

profile of v0, /device:TPU:9, one launch (start us, length us, event | category | flops | bytes accessed | tf_op | source)
XLA Modules:
  0.0 2457.6 jit_solution(13488351858381302621)
XLA Ops:
  12.0 28.3 %all-gather.16.cloned.1.call-done = bf16[2048,512]{1,0:T(8,128)(2,1)} async-done(((bf16[256,512]{1,0:T(8,128)(2,1)}), bf16[2048,512]{1,0:T(8,128)(2,1)}) %all-gather.16.cloned.1.call-update) | async-done | bytes 2097168 | tf_op jit(solution)/shard_map/all_gather | solution.py:88
  40.3 5.2 multiply_reduce_fusion.8
  45.6 25.0 %all-gather.18.cloned.1.call-done = bf16[2048,512]{1,0:T(8,128)(2,1)} async-done(((bf16[256,512]{1,0:T(8,128)(2,1)}), bf16[2048,512]{1,0:T(8,128)(2,1)}) %all-gather.18.cloned.1.call-update) | async-done | bytes 2097168 | tf_op jit(solution)/shard_map/all_gather | solution.py:89
  70.5 6.5 multiply_reduce_fusion.7
  77.0 8.2 all-reduce.8
  86.5 3.2 multiply_multiply_fusion
  92.5 3.5 slice_negate_fusion
  104.3 3.6 fusion.24
  108.0 6.2 convolution_convert_fusion.2
  121.6 65.5 %all-gather.20.cloned.1.call-done = bf16[4,2048,512]{1,2,0:T(8,128)(2,1)} async-done(((bf16[4,256,512]{1,2,0:T(8,128)(2,1)}), bf16[4,2048,512]{1,2,0:T(8,128)(2,1)}) %all-gather.20.cloned.1.call-update) | async-done | bytes 8388624 | tf_op jit(solution)/shard_map/all_gather | solution.py:116
  187.1 17.9 fusion
  205.0 64.7 %all-gather.14.cloned.1.call-done = bf16[4,2048,512]{2,1,0:T(8,128)(2,1)} async-done(((bf16[4,256,512]{2,1,0:T(8,128)(2,1)}), bf16[4,2048,512]{2,1,0:T(8,128)(2,1)}) %all-gather.14.cloned.1.call-update) | async-done | bytes 8388624 | tf_op jit(solution)/shard_map/all_gather | solution.py:117
  269.7 11.3 copy.81
  281.0 15.8 exponential_reduce_fusion
  297.5 14.1 fusion.25
  312.3 7.5 fusion.28
  322.0 12.2 all-gather
  334.1 158.8 %all-reduce.14.cloned.1.call-done = f32[1024,2048]{1,0:T(8,128)} async-done(((f32[1024,2048]{1,0:T(8,128)}), f32[1024,2048]{1,0:T(8,128)}) %all-reduce.14.cloned.1.call-update) | async-done | bytes 8388624 | tf_op jit(solution)/shard_map/psum | solution.py:128
  493.0 4.1 multiply_reduce_fusion.4
  498.7 4.6 fusion.12
  503.4 71.8 %all-gather.24.cloned.1.call-done = bf16[2048,2048]{1,0:T(8,128)(2,1)} async-done(((bf16[256,2048]{1,0:T(8,128)(2,1)}), bf16[2048,2048]{1,0:T(8,128)(2,1)}) %all-gather.24.cloned.1.call-update) | async-done | bytes 8388624 | tf_op jit(solution)/shard_map/all_gather | solution.py:92
  575.2 14.6 fusion.56
  589.8 67.7 %all-gather.26.cloned.1.call-done = bf16[2048,2048]{1,0:T(8,128)(2,1)} async-done(((bf16[256,2048]{1,0:T(8,128)(2,1)}), bf16[2048,2048]{1,0:T(8,128)(2,1)}) %all-gather.26.cloned.1.call-update) | async-done | bytes 8388624 | tf_op jit(solution)/shard_map/all_gather | solution.py:93
  657.5 17.1 multiply_convert_fusion.2
  674.6 65.2 %all-gather.28.cloned.1.call-done = bf16[2048,2048]{1,0:T(8,128)(2,1)} async-done(((bf16[2048,256]{1,0:T(8,128)(2,1)}), bf16[2048,2048]{1,0:T(8,128)(2,1)}) %all-gather.28.cloned.1.call-update) | async-done | bytes 8388624 | tf_op jit(solution)/shard_map/all_gather | solution.py:94
  739.8 14.6 fusion.57
  755.0 12.1 all-gather.1
  767.2 160.2 %all-reduce.16.cloned.1.call-done = f32[1024,2048]{1,0:T(8,128)} async-done(((f32[1024,2048]{1,0:T(8,128)}), f32[1024,2048]{1,0:T(8,128)}) %all-reduce.16.cloned.1.call-update) | async-done | bytes 8388624 | tf_op jit(solution)/shard_map/psum | solution.py:134
  927.4 4.1 multiply_reduce_fusion.3
  933.2 5.4 fusion.10
  941.0 20.1 multiply_convert_fusion.1
  961.2 12.7 fusion.58
  973.9 13.6 convolution_add_fusion
  987.6 172.9 %all-reduce.18.cloned.1.call-done = f32[1024,2048]{1,0:T(8,128)} async-done(((f32[1024,2048]{1,0:T(8,128)}), f32[1024,2048]{1,0:T(8,128)}) %all-reduce.18.cloned.1.call-update) | async-done | bytes 8388624 | tf_op jit(solution)/shard_map/psum | solution.py:164
  1160.5 10.3 multiply_reduce_fusion.1
  1170.9 13.4 fusion.9
  1184.2 5.2 convolution_convert_fusion.1
  1190.5 18.4 fusion.33
  1208.9 16.4 copy.95
  1225.3 28.9 %multiply_reduce_fusion = (f32[4,4,256]{2,1,0:T(4,128)S(1)}, f32[4,4,256,2048]{3,2,1,0:T(8,128)}) fusion(f32[4,4,256,2048]{3,2,1,0:T(8,128)} %get-tuple-element.110, f32[4,4,256]{2,1,0:T(4,128)S(1)} %copy-done.30, pred[256,2048]{1,0:T(8,128)(4,1)S(1)} %copy-done.3, bf16[4,256,4,128]{1,3,2,0:T(8,128)(2,1)S(1)} %copy.94, bf16[4,2048,4,128]{1,3,2,0:T(8,128)(2,1)} %bitcast.150), kind=kOutput, calls=%fused_computation.1 | convolution fusion | flops 2189422592 | bytes 77103104 | tf_op jit(solution)/shard_map/sqhd,skhd->shqk/dot_general | solution.py:177
  1254.2 28.7 %multiply_convert_fusion = bf16[4,4,256,2048]{3,2,1,0:T(8,128)(2,1)} fusion(f32[4,4,256,2048]{3,2,1,0:T(8,128)} %get-tuple-element.114, f32[4,4,256,2048]{3,2,1,0:T(8,128)} %get-tuple-element.110, f32[4,4,256]{2,1,0:T(4,128)S(1)} %get-tuple-element.113, f32[4,4,256]{2,1,0:T(4,128)S(1)} %copy-done.30, pred[256,2048]{1,0:T(8,128)(4,1)S(1)} %copy-done.3), kind=kLoop, calls=%fused_computation | loop fusion | flops 50331648 | bytes 84443136 | tf_op jit(solution)/shard_map/convert_element_type | solution.py:181
  1282.9 14.8 broadcast_multiply_fusion
  1297.8 95.1 %reduce-scatter.12.cloned.1.call-done = f32[4,256,512]{2,1,0:T(8,128)} async-done(((f32[4,2048,512]{2,1,0:T(8,128)}), f32[4,256,512]{2,1,0:T(8,128)}) %reduce-scatter.12.cloned.1.call-update) | async-done | bytes 2097168 | tf_op jit(solution)/shard_map/reduce_scatter | solution.py:202
  1394.6 6.6 convolution_bitcast_fusion
  1402.1 11.5 bitcast_multiply_fusion.3
  1418.7 143.1 %reduce-scatter.10.cloned.1.call-done = f32[4,256,512]{1,2,0:T(8,128)} async-done(((f32[4,2048,512]{1,2,0:T(8,128)}), f32[4,256,512]{1,2,0:T(8,128)}) %reduce-scatter.10.cloned.1.call-update) | async-done | bytes 2097168 | tf_op jit(solution)/shard_map/reduce_scatter | solution.py:196
  1568.6 2.9 fusion.18
  1571.5 8.1 all-reduce.7
  1583.5 4.4 convolution_bitcast_fusion.1
  1591.9 4.4 convolution_bitcast_fusion.2
  1597.5 4.1 fusion.60
  1604.1 6.0 add_add_fusion.2
  1611.2 6.6 fusion.26
  1618.3 15.4 fusion.63
  1633.8 15.4 fusion.61
  1649.4 15.4 fusion.62
  1666.7 25.5 %all-reduce.6 = (f32[512]{0:T(512)}, f32[512]{0:T(512)}, f32[2048]{0:T(1024)S(1)}, f32[2048]{0:T(1024)S(1)}) all-reduce(f32[512]{0:T(512)S(1)} %get-tuple-element.71, f32[512]{0:T(512)S(1)} %get-tuple-element.69, f32[2048]{0:T(1024)S(1)} %copy-done.45, f32[2048]{0:T(1024)S(1)} %copy-done.46), channel_id=1, replica_groups=mesh['context'=8,'tensor'=4] {'context'}, use_global_device_ids=true, to_apply=%region_31.32 | all-reduce | flops 5120 | bytes 40960 | tf_op jit(solution)/shard_map/psum | solution.py:229
  1697.6 16.4 reduce-scatter.14.cloned.1.call-done
  1716.0 174.2 %all-reduce.20.cloned.1.call-done = f32[1024,2048]{1,0:T(8,128)} async-done(((f32[1024,2048]{1,0:T(8,128)}), f32[1024,2048]{1,0:T(8,128)}) %all-reduce.20.cloned.1.call-update) | async-done | bytes 8388624 | tf_op jit(solution)/shard_map/psum | solution.py:237
  1890.2 13.5 fusion.32
  1903.7 38.5 %reduce-scatter.20.cloned.1.call-done = f32[512,256]{1,0:T(8,128)} async-done(((f32[512,2048]{1,0:T(8,128)}), f32[512,256]{1,0:T(8,128)}) %reduce-scatter.20.cloned.1.call-update) | async-done | bytes 524304 | tf_op jit(solution)/shard_map/reduce_scatter | solution.py:253
  1942.2 169.2 %reduce-scatter.26.cloned.1.call-done = f32[2048,256]{1,0:T(8,128)} async-done(((f32[2048,2048]{1,0:T(8,128)}), f32[2048,256]{1,0:T(8,128)}) %reduce-scatter.26.cloned.1.call-update) | async-done | bytes 2097168 | tf_op jit(solution)/shard_map/reduce_scatter | solution.py:262
  2111.4 169.6 %reduce-scatter.22.cloned.1.call-done = f32[256,2048]{1,0:T(8,128)} async-done(((f32[2048,2048]{1,0:T(8,128)}), f32[256,2048]{1,0:T(8,128)}) %reduce-scatter.22.cloned.1.call-update) | async-done | bytes 2097168 | tf_op jit(solution)/shard_map/reduce_scatter | solution.py:256
  2281.0 169.6 %reduce-scatter.24.cloned.1.call-done = f32[256,2048]{1,0:T(8,128)} async-done(((f32[2048,2048]{1,0:T(8,128)}), f32[256,2048]{1,0:T(8,128)}) %reduce-scatter.24.cloned.1.call-update) | async-done | bytes 2097168 | tf_op jit(solution)/shard_map/reduce_scatter | solution.py:259
  (219 shorter events, 71.9 us)
Async XLA Ops:
  7.2 33.1 %all-gather.16.cloned.1.call-start = ((), (), s32[]{:S(2)}) async-start(), calls=%async_computation.11 | async-start | bytes 2359296 | tf_op jit(solution)/shard_map/all_gather | solution.py:88
  7.9 62.6 %all-gather.18.cloned.1.call-start = ((), (), s32[]{:S(2)}) async-start(), calls=%async_computation.12 | async-start | bytes 2359296 | tf_op jit(solution)/shard_map/all_gather | solution.py:89
  8.7 99.3 %all-gather.12.cloned.1.call-start = ((), (), s32[]{:S(2)}) async-start(), calls=%async_computation.9 | async-start | bytes 2359296 | tf_op jit(solution)/shard_map/all_gather | solution.py:90
  9.4 177.7 %all-gather.20.cloned.1.call-start = ((), (), s32[]{:S(2)}) async-start(), calls=%async_computation.13 | async-start | bytes 9437184 | tf_op jit(solution)/shard_map/all_gather | solution.py:116
  10.1 75.7 %copy-start.41 = (f32[512]{0:T(512)}, f32[512]{0:T(512)S(1)}, u32[]{:S(2)}) copy-start(f32[512]{0:T(512)S(1)} %convert_element_type.93) | copy-start | bytes 6148
  12.0 108.1 %copy-start.22 = (f32[256,128]{0,1:T(8,128)}, f32[256,128]{0,1:T(8,128)S(1)}, u32[]{:S(2)}) copy-start(f32[256,128]{0,1:T(8,128)S(1)} %get-tuple-element.119) | copy-start | bytes 393220
  12.0 108.1 %copy-start.24 = (f32[256,128]{0,1:T(8,128)}, f32[256,128]{0,1:T(8,128)S(1)}, u32[]{:S(2)}) copy-start(f32[256,128]{0,1:T(8,128)S(1)} %get-tuple-element.98) | copy-start | bytes 393220
  45.6 70.0 %copy-start.10 = (f32[1024,512]{0,1:T(8,128)}, f32[1024,512]{0,1:T(8,128)S(1)}, u32[]{:S(2)}) copy-start(f32[1024,512]{0,1:T(8,128)S(1)} %get-tuple-element.106) | copy-start | bytes 6291460
  85.9 29.7 %copy-start.33 = (f32[1024]{0:T(1024)}, f32[1024]{0:T(1024)S(1)}, u32[]{:S(2)}) copy-start(f32[1024]{0:T(1024)S(1)} %get-tuple-element.117) | copy-start | bytes 12292
  107.9 7.1 copy-start.50
  107.9 7.1 copy-start.49
  107.9 161.8 %all-gather.14.cloned.1.call-start = ((), (), s32[]{:S(2)}) async-start(), calls=%async_computation.10 | async-start | bytes 9437184 | tf_op jit(solution)/shard_map/all_gather | solution.py:117
  114.2 198.0 %all-gather.22.cloned.1.call-start = ((), (), s32[]{:S(2)}) async-start(), calls=%async_computation.14 | async-start | bytes 2359296 | tf_op jit(solution)/shard_map/all_gather | solution.py:91
  114.8 378.2 %all-reduce.14.cloned.1.call-start = ((), (), s32[]{:S(2)}) async-start(), calls=%async_computation.15 | async-start | bytes 16777216 | tf_op jit(solution)/shard_map/psum | solution.py:128
  115.5 181.3 %copy-start.2 = (pred[256,2048]{1,0:T(8,128)(4,1)}, pred[256,2048]{1,0:T(8,128)(4,1)S(1)}, u32[]{:S(2)}) copy-start(pred[256,2048]{1,0:T(8,128)(4,1)S(1)} %broadcast_compare_fusion) | copy-start | bytes 1572868
  281.0 16.4 copy-start.9
  312.2 7.6 copy-start.15
  319.8 2.2 copy-start.52
  319.8 255.4 %all-gather.24.cloned.1.call-start = ((), (), s32[]{:S(2)}) async-start(), calls=%async_computation.16 | async-start | bytes 9437184 | tf_op jit(solution)/shard_map/all_gather | solution.py:92
  320.6 336.9 %all-gather.26.cloned.1.call-start = ((), (), s32[]{:S(2)}) async-start(), calls=%async_computation.17 | async-start | bytes 9437184 | tf_op jit(solution)/shard_map/all_gather | solution.py:93
  321.3 418.5 %all-gather.28.cloned.1.call-start = ((), (), s32[]{:S(2)}) async-start(), calls=%async_computation.18 | async-start | bytes 9437184 | tf_op jit(solution)/shard_map/all_gather | solution.py:94
  321.9 605.5 %all-reduce.16.cloned.1.call-start = ((), (), s32[]{:S(2)}) async-start(), calls=%async_computation.19 | async-start | bytes 16777216 | tf_op jit(solution)/shard_map/psum | solution.py:134
  334.1 163.6 %copy-start.31 = (f32[8,1,256]{2,1,0:T(1,128)}, f32[8,1,256]{2,1,0:T(1,128)S(1)}, u32[]{:S(2)}) copy-start(f32[8,1,256]{2,1,0:T(1,128)S(1)} %convert_element_type.116) | copy-start | bytes 24580
  493.0 5.8 copy-start
  754.4 406.1 %all-reduce.18.cloned.1.call-start = ((), (), s32[]{:S(2)}) async-start(), calls=%async_computation.20 | async-start | bytes 16777216 | tf_op jit(solution)/shard_map/psum | solution.py:164
  927.4 5.8 copy-start.1
  933.2 5.5 copy-start.4
  941.0 20.1 copy-start.19
  961.2 12.7 copy-start.55
  987.5 173.0 %copy-start.32 = (f32[8,1,256]{2,1,0:T(1,128)S(1)}, f32[8,1,256]{2,1,0:T(1,128)}, u32[]{:S(2)}) copy-start(f32[8,1,256]{2,1,0:T(1,128)} %copy-done.31) | copy-start | bytes 24580
  987.5 173.0 %copy-start.38 = (f32[1024]{0:T(1024)S(1)}, f32[1024]{0:T(1024)}, u32[]{:S(2)}) copy-start(f32[1024]{0:T(1024)} %copy-done.37) | copy-start | bytes 12292
  987.6 183.3 %copy-start.40 = (f32[1024]{0:T(1024)S(1)}, f32[1024]{0:T(1024)}, u32[]{:S(2)}) copy-start(f32[1024]{0:T(1024)} %copy-done.39) | copy-start | bytes 12292
  987.6 405.3 %reduce-scatter.12.cloned.1.call-start = ((), (), s32[]{:S(2)}) async-start(), calls=%async_computation.22 | async-start | bytes 18874368 | tf_op jit(solution)/shard_map/reduce_scatter | solution.py:202
  1160.5 10.3 copy-start.5
  1160.5 10.3 copy-start.6
  1225.3 336.5 %reduce-scatter.10.cloned.1.call-start = ((), (), s32[]{:S(2)}) async-start(), calls=%async_computation.21 | async-start | bytes 18874368 | tf_op jit(solution)/shard_map/reduce_scatter | solution.py:196
  1254.2 28.7 %copy-start.13 = (bf16[4,256,4,128]{1,3,2,0:T(8,128)(2,1)S(1)}, bf16[4,256,4,128]{1,3,2,0:T(8,128)(2,1)}, u32[]{:S(2)}) copy-start(bf16[4,256,4,128]{1,3,2,0:T(8,128)(2,1)} %fusion.20) | copy-start | bytes 3145732
  1297.7 395.8 %reduce-scatter.18.cloned.1.call-start = ((), (), s32[]{:S(2)}) async-start(), calls=%async_computation.26 | async-start | bytes 4718592 | tf_op jit(solution)/shard_map/reduce_scatter | solution.py:250
  1401.2 294.3 %reduce-scatter.16.cloned.1.call-start = ((), (), s32[]{:S(2)}) async-start(), calls=%async_computation.25 | async-start | bytes 4718592 | tf_op jit(solution)/shard_map/reduce_scatter | solution.py:247
  1414.9 3.2 copy-start.11
  1414.9 3.2 copy-start.34
  1414.9 3.2 copy-start.44
  1416.3 145.6 %copy-start.25 = (f32[256,128]{0,1:T(8,128)S(1)}, f32[256,128]{0,1:T(8,128)}, u32[]{:S(2)}) copy-start(f32[256,128]{0,1:T(8,128)} %copy-done.24) | copy-start | bytes 393220
  1416.8 1.3 copy-start.12
  1561.8 2.2 copy-start.14
  1561.8 2.2 copy-start.23
  1564.1 4.5 copy-start.36
  1564.1 4.5 copy-start.42
  1565.7 13.9 copy-start.48
  1579.5 3.9 copy-start.7
  1587.9 126.0 %reduce-scatter.14.cloned.1.call-start = ((), (), s32[]{:S(2)}) async-start(), calls=%async_computation.24 | async-start | bytes 4718592 | tf_op jit(solution)/shard_map/reduce_scatter | solution.py:244
  1588.0 3.9 copy-start.8
  1596.3 1.2 copy-start.18
  1596.3 5.3 copy-start.27
  1596.3 293.9 %all-reduce.20.cloned.1.call-start = ((), (), s32[]{:S(2)}) async-start(), calls=%async_computation.23 | async-start | bytes 16777216 | tf_op jit(solution)/shard_map/psum | solution.py:237
  1597.5 4.1 copy-start.51
  1601.6 2.4 copy-start.21
  1610.0 1.2 copy-start.16
  1610.0 332.2 %reduce-scatter.20.cloned.1.call-start = ((), (), s32[]{:S(2)}) async-start(), calls=%async_computation.27 | async-start | bytes 4718592 | tf_op jit(solution)/shard_map/reduce_scatter | solution.py:253
  1617.9 493.6 %reduce-scatter.26.cloned.1.call-start = ((), (), s32[]{:S(2)}) async-start(), calls=%async_computation.30 | async-start | bytes 18874368 | tf_op jit(solution)/shard_map/reduce_scatter | solution.py:262
  1633.7 647.3 %reduce-scatter.22.cloned.1.call-start = ((), (), s32[]{:S(2)}) async-start(), calls=%async_computation.28 | async-start | bytes 18874368 | tf_op jit(solution)/shard_map/reduce_scatter | solution.py:256
  1649.2 801.4 %reduce-scatter.24.cloned.1.call-start = ((), (), s32[]{:S(2)}) async-start(), calls=%async_computation.29 | async-start | bytes 18874368 | tf_op jit(solution)/shard_map/reduce_scatter | solution.py:259
  1664.8 1.9 copy-start.45
  1664.8 1.9 copy-start.46
  (14 other events, 10.9 us)
Sparse Core Ops, SparseCore 0:
  9.6 30.6 all-gather.15
  41.9 28.5 all-gather.17
  72.1 28.5 all-gather.11
  108.0 79.0 all-gather.19
  189.1 80.5 all-gather.13
  271.1 33.8 all-gather.21
  319.9 172.9 all-reduce.13
  494.6 80.5 all-gather.23
  576.9 80.5 all-gather.25
  659.0 80.7 all-gather.27
  754.5 172.8 all-reduce.15
  987.7 172.7 all-reduce.17
  1225.4 167.4 reduce-scatter.11
  1395.2 166.5 reduce-scatter.9
  1564.1 48.3 reduce-scatter.17
  1614.7 48.1 reduce-scatter.15
  1665.2 48.7 reduce-scatter.13
  1718.3 171.7 all-reduce.19
  1893.0 49.1 reduce-scatter.19
  1945.0 166.3 reduce-scatter.25
  2114.4 166.6 reduce-scatter.21
  2284.0 166.5 reduce-scatter.23
where the time goes:
time: 2470 us; the launch traced here: 2460 us
  waiting for transfers between devices  1860 us (75%)
  matrix products  310 us (13%)
  other arithmetic  137 us (6%)
  local copies, waits for them, and re-layouts  66.8 us (3%)
  blocking collectives  66 us (3%)
    psum x1, waiting for transfers between devices, local(): lax.psum(by_transpose(query_raw_low, w_query) + by_transpose(key_raw_low,...  174 us
    psum x1, waiting for transfers between devices, local(): lax.psum(by_transpose(gate_low, w_gate) + by_transpose(up_low, w_up), 'te...  173 us
    reduce_scatter x1, waiting for transfers between devices, local(): lax.psum_scatter(transpose_by(hidden_low, gate_low), 'context', scatter_d...  170 us
    reduce_scatter x1, waiting for transfers between devices, local(): lax.psum_scatter(transpose_by(hidden_low, up_low), 'context', scatter_dim...  170 us
    reduce_scatter x1, waiting for transfers between devices, local(): lax.psum_scatter(transpose_by(act_low, fed_low), 'context', scatter_dimen...  169 us
    psum x1, waiting for transfers between devices, local(): lax.psum(jnp.dot(act_low, w_down, preferred_element_type=jnp.float32), 't...  160 us
    psum x1, waiting for transfers between devices, local(): lax.psum(jnp.dot(mixed_low, w_output, preferred_element_type=jnp.float32)...  159 us
    reduce_scatter x1, waiting for transfers between devices, local(): lax.psum_scatter(key_terms.reshape(seqs, full_len, heads * HD), 'context'...  143 us
  transfers between devices with their start and end apart: 22, of which 18 were waited for; matrix products, arithmetic and copies ran while one was open for 14% of the time, Pallas kernels for 0%

commit v1 on v0

v1 whole, which is shorter than its diff:
```python
import functools

import jax
import jax.numpy as jnp
from jax import lax
from jax.experimental import pallas as pl
from jax.experimental.pallas import tpu as pltpu
from jax.sharding import PartitionSpec as P

HD = 128
EPS = 1e-06
THETA = 500000.0
BF = jnp.bfloat16
F32 = jnp.float32
VMEM_LIMIT = 60 * 1024 * 1024
MESH = pl.DeviceIdType.MESH


def dot_nn(left, right):
    return jnp.dot(left, right, preferred_element_type=F32)


def dot_nt(left, right):
    return lax.dot_general(left, right, (((1,), (1,)), ((), ())), preferred_element_type=F32)


def dot_tn(left, right):
    return lax.dot_general(left, right, (((0,), (0,)), ((), ())), preferred_element_type=F32)


def after(values, *others):
    return lax.optimization_barrier((values, *others))[0]


def swap(values, axis, mask):
    size = lax.axis_size(axis)
    return lax.ppermute(values, axis, [(i, i ^ mask) for i in range(size)])


def gather_rows(shard):
    return [shard] + [swap(shard, "tensor", k) for k in range(1, lax.axis_size("tensor"))]


def scatter_rows(parts):
    total = parts[0]
    for k in range(1, len(parts)):
        total = total + swap(parts[k].astype(BF), "tensor", k).astype(F32)
    return total


def sum_over_tensor(values):
    size = lax.axis_size("tensor")
    chunks = values.reshape(values.shape[0], size, -1)
    total = chunks
    for m in range(1, size):
        other = swap(chunks, "tensor", m)
        total = total + jnp.stack([other[:, m ^ k] for k in range(size)], axis=1)
    return total.reshape(values.shape)


def to_sequences(values, s, t):
    seqs, local_len, width = values.shape
    size = lax.axis_size("tensor")
    mine = lax.dynamic_index_in_dim(values.reshape(seqs, size, local_len // size, width), t, 1, keepdims=False)
    pieces = []
    for j in range(seqs):
        piece = lax.dynamic_index_in_dim(mine, s ^ j, 0, keepdims=False)
        pieces.append(piece if j == 0 else swap(piece, "context", 2 * j))
    return jnp.concatenate(pieces, axis=0)


def place_kernel(at_ref, in_ref, out_ref):
    for a in range(out_ref.shape[0]):
        out_ref[a, 0] = in_ref[0, a ^ at_ref[0]].astype(out_ref.dtype)


def to_ranks(shard, seqs):
    pieces = shard.reshape(seqs, -1, shard.shape[1])
    return jnp.stack([pieces[0]] + [swap(pieces[j], "context", 2 * j) for j in range(1, seqs)], axis=0)


def in_place(every, s, t, dtype):
    size, seqs, piece, width = every.shape
    full = pl.pallas_call(
        place_kernel,
        grid_spec=pltpu.PrefetchScalarGridSpec(
            num_scalar_prefetch=1,
            grid=(size,),
            in_specs=[pl.BlockSpec((1, seqs, piece, width), lambda b, at: (b ^ at[1], 0, 0, 0))],
            out_specs=pl.BlockSpec((seqs, 1, piece, width), lambda b, at: (0, b, 0, 0)),
        ),
        out_shape=jax.ShapeDtypeStruct((seqs, size, piece, width), dtype),
        name="place_rows",
    )(jnp.stack([s, t]).astype(jnp.int32), every)
    return full.reshape(seqs, size * piece, width)


def norm_factor(values):
    return lax.rsqrt(jnp.mean(values * values, axis=-1, keepdims=True) + EPS)


def norm_back(values, factor, gain, grad):
    scaled = grad * gain
    inner = jnp.mean(values * scaled, axis=-1, keepdims=True)
    return factor * scaled - values * (factor**3 * inner), grad * values * factor


def flip(index, mask):
    bit = 1
    result = index
    while bit <= mask:
        if mask & bit:
            result = result + bit - 2 * bit * ((index // bit) % 2)
        bit *= 2
    return result


def exchange_kernel(size, width, depth, offset, tile, finish, chips, last, n_in, n_out, a_ref, w_ref, *refs):
    ins, rest = refs[:n_in], refs[n_in:]
    every, outs, rest = rest[0], rest[1 : 1 + n_out], rest[1 + n_out :]
    a_buf, w_buf, sent, got, total, mine, a_sem, w_sem, sent_sem, got_sem, out_sem, in_sem, own_sem = rest[:13]
    t = lax.axis_index("tensor")
    c = lax.axis_index("context")
    rows = total.shape[0]
    half = rows // 2

    def a_copy(k):
        at = pl.ds(k * rows, rows)
        return pltpu.make_async_copy(a_ref.at[at, :], a_buf.at[at, :], a_sem.at[k])

    def w_copy(j):
        at = pl.ds(pl.multiple_of(j * tile, tile), tile)
        return pltpu.make_async_copy(w_ref.at[at, pl.ds(offset, depth)], w_buf.at[at, :], w_sem.at[j])

    order = [3, 1, 2, 0] if size == 4 else [*range(1, size), 0]
    tiles = width // tile
    parts = 2 if last and size == 4 else 1
    across = width // parts
    a_copy(order[0]).start()
    for j in range(tiles):
        w_copy(j).start()
    for k in order[1:]:
        a_copy(k).start()
    barrier = pltpu.get_barrier_semaphore()
    for k in range(1, size):
        pl.semaphore_signal(barrier, inc=1, device_id={"tensor": flip(t, k)}, device_id_type=MESH)

    met = range(1, 2 * chips) if last else range(2, 2 * chips, 2)
    for mask in met:
        pl.semaphore_signal(barrier, inc=1, device_id={"context": flip(c, mask)}, device_id_type=MESH)
    for out in outs:
        if out.shape[0] == 8:
            out[...] = jnp.zeros_like(out)

    def cross(j, source, target, sems, base=0):
        if j == 0:
            return pltpu.make_async_copy(source, target, sems[0].at[base])
        return pltpu.make_async_remote_copy(
            src_ref=source,
            dst_ref=target,
            send_sem=sems[0].at[base + j],
            recv_sem=sems[1].at[base + j],
            device_id={"context": flip(c, 2 * j)},
            device_id_type=MESH,
        )

    def send(slot, source, target, partner, sems):
        return pltpu.make_async_remote_copy(
            src_ref=source,
            dst_ref=target,
            send_sem=sems[0].at[slot],
            recv_sem=sems[1].at[slot],
            device_id={"tensor": flip(t, partner)},
            device_id_type=MESH,
        )

    def product(k, first=False, part=0):
        if part == 0:
            a_copy(k).wait()

        def step(j, carry):
            if first:
                w_copy(j).wait()
            at = pl.ds(pl.multiple_of(j * tile, tile), tile)
            value = dot_nt(a_buf[k * rows : (k + 1) * rows, :], w_buf[at, :])
            if k:
                sent[k - 1, :, at] = value.astype(BF)
            else:
                total[:, at] = value
            return carry

        lax.fori_loop(part * tiles // parts, (part + 1) * tiles // parts, step, 0)

    def add(slot, other, first, columns):
        def step(i, carry):
            at = pl.ds(pl.multiple_of(first + i * 16, 16), 16)
            sent[slot, at, columns] = (sent[slot, at, columns].astype(F32) + got[other, at, columns].astype(F32)).astype(BF)
            return carry

        lax.fori_loop(0, half // 16, step, 0)

    def columns_of_part(part):
        return pl.ds(part * across, across)

    low, high = pl.ds(0, half), pl.ds(half, half)
    sums = (sent_sem, got_sem)
    product(order[0], first=True)
    pl.semaphore_wait(barrier, size - 1 + len(met))
    piece = rows // max(1, chips)
    crossing = []
    small = []
    if last:
        gain_rows, head_rows, gain_got, head_got, own_got, small_sent, small_got = rest[18:]
        attn_rows, feed_rows, two_heads = ins[1:]
        gain_rows[...] = jnp.zeros_like(gain_rows)
        head_rows[...] = jnp.zeros_like(head_rows)
        for i, part in enumerate((attn_rows, feed_rows)):
            gain_rows[i : i + 1, :] = jnp.sum(part[...], axis=0, keepdims=True)
            head_rows[i : i + 1, :] = jnp.sum(two_heads[8 * i : 8 * i + 8, :], axis=0, keepdims=True)
        own_width = outs[0].shape[1]

        def tell(source, target, device):
            copy = pltpu.make_async_remote_copy(
                src_ref=source,
                dst_ref=target,
                send_sem=small_sent.at[len(small)],
                recv_sem=small_got.at[len(small)],
                device_id=device,
                device_id_type=MESH,
            )
            copy.start()
            small.append(copy)

        for k in range(1, size):
            tell(gain_rows, gain_got.at[k - 1], {"tensor": flip(t, k)})
        for mask in met:
            tell(head_rows, head_got.at[mask - 1], {"context": flip(c, mask)})
    if chips and not last:
        source, target = ins[0], outs[0]
        for j in range(chips):
            crossing.append(
                cross(
                    j,
                    source.at[flip(c // 2, j), pl.ds(pl.multiple_of(t * piece, piece), piece), :],
                    target.at[pl.ds(j * piece, piece), :],
                    rest[13:15],
                )
            )
            crossing[-1].start()

    def home(part):
        at = columns_of_part(part)
        return [
            cross(j, mine.at[pl.ds(j * piece, piece), at], rest[17].at[pl.ds(j * piece, piece), at], rest[15:17], part * chips)
            for j in range(chips)
        ]

    def finish_last(part, group):
        at = columns_of_part(part)
        for copy in group[2:] if size == 4 else group:
            copy.wait_recv()

        def step(i, carry):
            row = pl.ds(pl.multiple_of(i * 16, 16), 16)
            summed = ins[0][row, at] + total[row, at]
            for other in range(2 if size == 4 else size - 1):
                summed = summed + got[other, row, at].astype(F32)
            mine[row, at] = summed.astype(BF)
            return carry

        lax.fori_loop(0, rows // 16, step, 0)
        for copy in home(part):
            copy.start()

    def sums_of(part):
        at = columns_of_part(part)
        return [
            send(6 * part + 0, sent.at[2, low, at], got.at[2, low, at], 1, sums),
            send(6 * part + 1, sent.at[2, high, at], got.at[2, high, at], 2, sums),
            send(6 * part + 2, sent.at[0, low, at], got.at[0, low, at], 1, sums),
            send(6 * part + 3, sent.at[1, high, at], got.at[1, high, at], 2, sums),
            send(6 * part + 4, sent.at[1, low, at], got.at[1, low, at], 2, sums),
            send(6 * part + 5, sent.at[0, high, at], got.at[0, high, at], 1, sums),
        ]

    if size == 4:
        groups = [sums_of(part) for part in range(parts)]
        copies = sum(groups, [])
        copies[0].start()
        copies[1].start()
        product(1)
        copies[2].start()
        product(2)
        copies[3].start()
        for part in range(1, parts):
            product(3, first=True, part=part)
            product(1, part=part)
            product(2, part=part)
        for part, group in enumerate(groups):
            at = columns_of_part(part)
            group[0].wait_recv()
            add(1, 2, 0, at)
            group[4].start()
            group[1].wait_recv()
            add(0, 2, half, at)
            group[5].start()
            for copy in groups[part + 1][:4] if part + 1 < parts else []:
                copy.start()
            product(0, part=part)
            if part + 1 < parts:
                finish_last(part, group)
        if not last:
            for copy in copies[2:]:
                copy.wait_recv()
        used = 2
    else:
        copies = [send(k - 1, sent.at[k - 1], got.at[k - 1], k, sums) for k in range(1, size)]
        copies[0].start()
        for k in range(2, size):
            product(k)
            copies[k - 1].start()
        product(0)
        groups = [copies]
        if not last:
            for copy in copies:
                copy.wait_recv()
        used = size - 1
    if last:
        finish_last(parts - 1, groups[-1])
    if chips and not last:
        crossing[0].wait()
        for copy in crossing[1:]:
            copy.wait_recv()

    def finish_rows(first, count, part=0):
        def step(i, carry):
            at = pl.ds(pl.multiple_of(first + i * 16, 16), 16)
            summed = total[at, :]
            for other in range(used):
                summed = summed + got[other, at, :].astype(F32)
            mine[at, :] = finish(at, summed, ins, outs).astype(BF)
            return carry

        lax.fori_loop(0, count // 16, step, 0)

    gather = (out_sem, in_sem)
    shared = rest[17] if last else mine
    own = pltpu.make_async_copy(shared, every.at[pl.ds(0, rows), :], own_sem)
    if last:
        going_home = [home(part) for part in range(parts)]
    else:
        going_home = [[cross(j, outs[1].at[pl.ds(j * piece, piece), :], outs[2].at[j], rest[15:17]) for j in range(chips)]]
    if last:
        for copy in small:
            copy.wait()
        for k in range(1, size):
            gain_rows[...] += gain_got[k - 1]
        outs[1][...] = head_rows[...]
        for mask in met:
            outs[1][...] += head_got[mask - 1]
        for mask in met:
            at = pl.ds(pl.multiple_of(flip(c, mask) * own_width, own_width), own_width)
            tell(gain_rows.at[:, at], own_got.at[mask - 1], {"context": flip(c, mask)})

    def came_home(first, count, part=0):
        for j in range(first // piece, (first + count) // piece):
            if j == 0:
                going_home[part][j].wait()
            else:
                going_home[part][j].wait_recv()

    make_ready = came_home if last else finish_rows
    then = [own] if last else [own, *going_home[0]]
    if size == 4:

        def chunk(k, side, part):
            return every.at[pl.ds(k * rows + side * half, half), columns_of_part(part)]

        def share(k, side, part):
            source = shared.at[pl.ds(side * half, half), columns_of_part(part)]
            return send(6 * part + 2 * k + side, source, chunk(k + 1, side, part), k + 1, gather)

        groups = []
        for part in range(parts):
            shares = [share(k, side, part) for k in (0, 1) for side in (0, 1)]
            passed = [
                send(6 * part + 4, chunk(1, 0, part), chunk(3, 0, part), 2, gather),
                send(6 * part + 5, chunk(2, 1, part), chunk(3, 1, part), 1, gather),
            ]
            groups.append(shares + passed)
        for part, group in enumerate(groups):
            make_ready(0, half, part)
            group[0].start()
            group[2].start()
            make_ready(half, half, part)
            group[3].start()
            group[1].start()
            if part == parts - 1:
                for copy in then:
                    copy.start()
            group[0].wait_recv()
            group[4].start()
            group[3].wait_recv()
            group[5].start()
        for group in groups:
            for at in (1, 2, 4, 5):
                group[at].wait_recv()
        shares = sum(groups, [])
    else:
        make_ready(0, rows)
        shares = [send(k - 1, shared, every.at[pl.ds(k * rows, rows), :], k, gather) for k in range(1, size)]
        for copy in [*shares, *then]:
            copy.start()
        for copy in shares:
            copy.wait_recv()
    own.wait()
    if chips and not last:
        came_home(0, rows)
    if last:
        for copy in small[size - 1 + len(met) :]:
            copy.wait()
        outs[0][...] = gain_rows[:, pl.ds(pl.multiple_of(c * own_width, own_width), own_width)]
        for mask in met:
            outs[0][...] += own_got[mask - 1]
    for copy in copies + shares + crossing[1:] + sum([group[1:] for group in going_home], []):
        copy.wait_send()


def exchange(name, number, a, w, finish, ins, outs, offset=0, chips=0, last=False):
    size = lax.axis_size("tensor")
    rows, width, depth = a.shape[0] // size, w.shape[0], a.shape[1]
    tile = min(512, width)
    parts = 2 if last and size == 4 else 1
    links = 6 * parts if size == 4 else size - 1
    whole = pl.BlockSpec(memory_space=pltpu.VMEM)
    anywhere = pl.BlockSpec(memory_space=pl.ANY)
    dma = pltpu.SemaphoreType.DMA
    gain_scratch = []
    if last:
        own, head_width = outs[0][0][1], outs[1][0][1]
        ranks = 2 * chips
        gain_scratch = [
            pltpu.VMEM((rows, width), BF),
            pltpu.VMEM((8, width), F32),
            pltpu.VMEM((8, head_width), F32),
            pltpu.VMEM((size - 1, 8, width), F32),
            pltpu.VMEM((ranks - 1, 8, head_width), F32),
            pltpu.VMEM((ranks - 1, 8, own), F32),
            dma((size - 1 + 2 * (ranks - 1),)),
            dma((size - 1 + 2 * (ranks - 1),)),
        ]
    return pl.pallas_call(
        functools.partial(exchange_kernel, size, width, depth, offset, tile, finish, chips, last, len(ins), len(outs)),
        in_specs=[anywhere, anywhere] + [anywhere if chips and not last and i == 0 else whole for i in range(len(ins))],
        out_specs=[anywhere] + [whole] * len(outs),
        out_shape=[jax.ShapeDtypeStruct((size * rows, width), BF)] + [jax.ShapeDtypeStruct(*out) for out in outs],
        scratch_shapes=[
            pltpu.VMEM((size * rows, depth), BF),
            pltpu.VMEM((width, depth), BF),
            pltpu.VMEM((size - 1, rows, width), BF),
            pltpu.VMEM((size - 1, rows, width), BF),
            pltpu.VMEM((rows, width), F32),
            pltpu.VMEM((rows, width), BF),
            dma((size,)),
            dma((width // tile,)),
            dma((links,)),
            dma((links,)),
            dma((links,)),
            dma((links,)),
            dma,
        ]
        + [dma((chips * parts,))] * (4 if chips else 0)
        + gain_scratch,
        compiler_params=pltpu.CompilerParams(vmem_limit_bytes=VMEM_LIMIT, collective_id=number, has_side_effects=True),
        cost_estimate=pl.CostEstimate(flops=2 * size * rows * width * depth, bytes_accessed=240_000_000, transcendentals=0),
        name=name,
    )(a, w, *ins)


def add_rows(ref, values):
    ref[...] += values[:8] + values[8:]


def finish_attended(at, attended, ins, outs):
    tokens, gain = ins
    outs[0][at, :] = attended
    hidden = tokens[at, :].astype(F32) + attended * norm_factor(attended) * gain[...]
    outs[1][at, :] = hidden
    return hidden


def finish_fed(at, fed, ins, outs):
    hidden, gain = ins[1:]
    factor = norm_factor(fed)
    outs[1][at, :] = (hidden[at, :] + fed * factor * gain[...]).astype(BF)
    grad, gain_rows = norm_back(fed, factor, gain[...], outs[0][at, :].astype(F32))
    add_rows(outs[3], gain_rows)
    return grad


def finish_hidden_grad(at, summed, ins, outs):
    attended, cotangent, gain = ins
    hidden_grad = cotangent[at, :].astype(F32) + summed
    outs[0][at, :] = hidden_grad
    values = attended[at, :]
    grad, gain_rows = norm_back(values, norm_factor(values), gain[...], hidden_grad)
    add_rows(outs[1], gain_rows)
    return grad


def turn(values, cosine, sine):
    heads = [values[:, i : i + HD] for i in range(0, values.shape[1], HD)]
    return jnp.concatenate([head * cosine + pltpu.roll(head, HD // 2, 1) * sine for head in heads], axis=1)


def turn_kernel(core_ref, raw_ref, column_ref, gain_ref, cosine_ref, sine_ref, keep_ref, send_ref):
    width = gain_ref.shape[1]
    half = width // 2
    cosine, sine = cosine_ref[...], sine_ref[...]
    first = core_ref[0] == 0
    for i in range(3):
        values = raw_ref[:, i * width : (i + 1) * width]
        if i < 2:
            values = turn(values * column_ref[:, i : i + 1] * gain_ref[i : i + 1, :], cosine, sine)
        low, high = values[:, :half].astype(BF), values[:, half:].astype(BF)
        keep_ref[i] = jnp.where(first, low, high)
        send_ref[i] = jnp.where(first, high, low)


def head_grads(core_ref, own_ref, other_ref, i):
    first = core_ref[0] == 0
    own, other = own_ref[i], other_ref[i]
    return jnp.concatenate([jnp.where(first, own, other), jnp.where(first, other, own)], axis=1).astype(F32)


def inner_kernel(core_ref, own_ref, other_ref, raw_ref, column_ref, gain_ref, cosine_ref, sine_ref, inner_ref, gains_ref):
    width = gain_ref.shape[1]
    cosine, sine = cosine_ref[...], -sine_ref[...]

    @pl.when(pl.program_id(0) == 0)
    def _():
        gains_ref[...] = jnp.zeros_like(gains_ref)

    for i in range(2):
        flat = turn(head_grads(core_ref, own_ref, other_ref, i), cosine, sine) * raw_ref[:, i * width : (i + 1) * width]
        inner_ref[i] = lax.dot_general(
            jnp.ones((8, width), F32),
            flat * gain_ref[i : i + 1, :],
            (((1,), (1,)), ((), ())),
            precision=lax.Precision.HIGHEST,
            preferred_element_type=F32,
        )
        flat = flat * column_ref[:, i : i + 1]
        gains_ref[i] += jnp.sum(flat.reshape(-1, 8, width), axis=0)


def raw_grad_kernel(core_ref, own_ref, other_ref, raw_ref, column_ref, gain_ref, cosine_ref, sine_ref, out_ref):
    width = gain_ref.shape[1]
    cosine, sine = cosine_ref[...], -sine_ref[...]
    for i in range(3):
        values = head_grads(core_ref, own_ref, other_ref, i)
        if i < 2:
            values = turn(values, cosine, sine) * column_ref[:, i : i + 1] * gain_ref[i : i + 1, :]
            values = values - raw_ref[:, i * width : (i + 1) * width] * column_ref[:, i + 2 : i + 3]
        out_ref[:, i * width : (i + 1) * width] = values.astype(BF)


def by_rows(kernel, name, core, ins, outs, rows=128):
    def spec(shape, dim):
        block = tuple(rows if i == dim else extent for i, extent in enumerate(shape))
        return pl.BlockSpec(block, lambda i, core: tuple(i if at == dim else 0 for at in range(len(shape))))

    count = next(out[0][dim] for *out, dim in outs if dim is not None)
    return pl.pallas_call(
        kernel,
        grid_spec=pltpu.PrefetchScalarGridSpec(
            num_scalar_prefetch=1,
            grid=(count // rows,),
            in_specs=[spec((array.shape[0], count, array.shape[2]) if dim == 1 else array.shape, dim) for array, dim in ins],
            out_specs=[spec(shape, dim) for shape, _, dim in outs],
        ),
        out_shape=[jax.ShapeDtypeStruct(shape, dtype) for shape, dtype, _ in outs],
        compiler_params=pltpu.CompilerParams(vmem_limit_bytes=VMEM_LIMIT),
        name=name,
    )(core[None].astype(jnp.int32), *[array for array, _ in ins])


def act_back_kernel(tile, grad_ref, w_ref, gate_up_ref, out_ref):
    hidden = w_ref.shape[1]

    def step(j, carry):
        at = pl.ds(pl.multiple_of(j * tile, tile), tile)
        up_at = pl.ds(pl.multiple_of(hidden + j * tile, tile), tile)
        act_grad = dot_nn(grad_ref[...], w_ref[:, at])
        gate, up = gate_up_ref[:, at], gate_up_ref[:, up_at]
        logistic = jax.nn.sigmoid(gate)
        silu = gate * logistic
        out_ref[:, at] = (act_grad * up * (logistic + silu * (1.0 - logistic))).astype(BF)
        out_ref[:, up_at] = (act_grad * silu).astype(BF)
        return carry

    lax.fori_loop(0, hidden // tile, step, 0)


def act_back(fed_low, w_down, gate_up):
    count, width = fed_low.shape
    hidden = w_down.shape[1]
    rows = 256
    return pl.pallas_call(
        functools.partial(act_back_kernel, 256),
        grid=(count // rows,),
        in_specs=[
            pl.BlockSpec((rows, width), lambda i: (i, 0)),
            pl.BlockSpec((width, hidden), lambda i: (0, 0)),
            pl.BlockSpec((rows, 2 * hidden), lambda i: (i, 0)),
        ],
        out_specs=pl.BlockSpec((rows, 2 * hidden), lambda i: (i, 0)),
        out_shape=jax.ShapeDtypeStruct((count, 2 * hidden), BF),
        compiler_params=pltpu.CompilerParams(vmem_limit_bytes=VMEM_LIMIT),
        cost_estimate=pl.CostEstimate(flops=2 * count * width * hidden, bytes_accessed=40_000_000, transcendentals=count * hidden),
        name="act_back",
    )(fed_low, w_down, gate_up)


def rank_products_kernel(tile, count, core_ref, *refs):
    out_ref = refs[-1]
    base = 0
    for left_ref, right_ref in zip(refs[:count], refs[count : 2 * count]):
        left = left_ref[...].astype(F32).T.astype(BF)
        for at in range(0, right_ref.shape[1], tile):
            part = dot_nn(left, right_ref[:, at : at + tile])
            if len(refs) > 2 * count + 1:
                part = part + refs[2 * count][:, base + at : base + at + tile].astype(F32)
            out_ref[:, base + at : base + at + tile] = part.astype(BF)
        base += right_ref.shape[1]


def rank_products(core, pairs, own, added=None):
    lefts, rights = [left for left, _ in pairs], [right for _, right in pairs]
    count, width = lefts[0].shape
    chips = width // (2 * own)
    across = sum(right.shape[1] for right in rights)
    block = pl.BlockSpec((own, across), lambda j, core: (j, 0))
    return pl.pallas_call(
        functools.partial(rank_products_kernel, min(512, *[right.shape[1] for right in rights]), len(pairs)),
        grid_spec=pltpu.PrefetchScalarGridSpec(
            num_scalar_prefetch=1,
            grid=(chips,),
            in_specs=[pl.BlockSpec((count, own), lambda j, core: (0, 2 * j + core[0]))] * len(pairs)
            + [pl.BlockSpec(right.shape, lambda j, core: (0, 0)) for right in rights]
            + [block] * (added is not None),
            out_specs=block,
        ),
        out_shape=jax.ShapeDtypeStruct((chips * own, across), BF),
        compiler_params=pltpu.CompilerParams(vmem_limit_bytes=VMEM_LIMIT),
        cost_estimate=pl.CostEstimate(flops=count * width * across, bytes_accessed=30_000_000, transcendentals=0),
        name="rank_products",
    )(core[None].astype(jnp.int32), *lefts, *rights, *([] if added is None else [added]))


def columns_of(*values):
    stacked = jnp.stack(values, axis=1)
    return jnp.pad(stacked, ((0, 0), (0, 8 - len(values))))


def in_order(at_ref, source, target, piece):
    def step(p, carry):
        start = pl.multiple_of(at_ref[p], piece)
        target[pl.ds(pl.multiple_of(p * piece, piece), piece), :] = source[pl.ds(start, piece), :]
        return carry

    lax.fori_loop(0, target.shape[0] // piece, step, 0)


def out_of_order(at_ref, source, target, piece):
    def step(p, carry):
        start = pl.multiple_of(at_ref[p], piece)
        target[pl.ds(start, piece), :] = source[pl.ds(pl.multiple_of(p * piece, piece), piece), :].astype(target.dtype)
        return carry

    lax.fori_loop(0, source.shape[0] // piece, step, 0)


def causal(tile):
    key_at = lax.broadcasted_iota(jnp.int32, (tile, tile), 0)
    query_at = lax.broadcasted_iota(jnp.int32, (tile, tile), 1)
    return query_at >= key_at


def attend_kernel(piece, tile, at_ref, qkv_ref, out_ref, log_ref, query, key, value, value_t, mixed):
    for slot, held in enumerate((query, key, value)):
        in_order(at_ref, qkv_ref.at[slot], held, piece)
    value_t[...] = value[...].astype(F32).T.astype(BF)
    allowed = causal(tile)
    for i in range(query.shape[0] // tile):
        low, high = i * tile, (i + 1) * tile
        rows = query[low:high, :]
        near = jnp.where(allowed, dot_nt(key[low:high, :], rows) * HD ** (-0.5), -1e30)
        top = jnp.max(near, axis=0, keepdims=True)
        if i:
            far = dot_nt(key[0:low, :], rows) * HD ** (-0.5)
            top = jnp.maximum(top, jnp.max(far, axis=0, keepdims=True))
        near = jnp.exp(near - top)
        total = jnp.sum(near, axis=0, keepdims=True)
        summed = dot_nn(value_t[:, low:high], near.astype(BF))
        if i:
            far = jnp.exp(far - top)
            total = total + jnp.sum(far, axis=0, keepdims=True)
            summed = summed + dot_nn(value_t[:, 0:low], far.astype(BF))
        mixed[low:high, :] = (summed / total).T
        log_ref[0, :, low:high] = top + jnp.log(total)
    out_of_order(at_ref, mixed, out_ref, piece)


def attend(qkv, at, piece):
    rows, width = qkv.shape[1:]
    heads = width // HD
    return pl.pallas_call(
        functools.partial(attend_kernel, piece, 256),
        grid_spec=pltpu.PrefetchScalarGridSpec(
            num_scalar_prefetch=1,
            grid=(heads,),
            in_specs=[pl.BlockSpec((3, rows, HD), lambda h, at: (0, 0, h))],
            out_specs=[
                pl.BlockSpec((rows, HD), lambda h, at: (0, h)),
                pl.BlockSpec((1, 1, rows), lambda h, at: (h, 0, 0)),
            ],
            scratch_shapes=[pltpu.VMEM((rows, HD), BF)] * 3 + [pltpu.VMEM((HD, rows), BF), pltpu.VMEM((rows, HD), F32)],
        ),
        out_shape=[jax.ShapeDtypeStruct((rows, width), BF), jax.ShapeDtypeStruct((heads, 1, rows), F32)],
        compiler_params=pltpu.CompilerParams(vmem_limit_bytes=VMEM_LIMIT),
        cost_estimate=pl.CostEstimate(
            flops=2 * 2 * heads * rows * rows * HD, bytes_accessed=8 * rows * width, transcendentals=heads * rows * rows // 2
        ),
        name="attend",
    )(at, qkv)


def attend_back_kernel(
    piece, tile, at_ref, qkv_ref, out_ref, grad_ref, log_ref, dqkv_ref, query, key, value, key_t, grad, mixed, dquery, dkey, dvalue
):
    for slot, held in enumerate((query, key, value)):
        in_order(at_ref, qkv_ref.at[slot], held, piece)
    in_order(at_ref, grad_ref, grad, piece)
    in_order(at_ref, out_ref, mixed, piece)
    key_t[...] = key[...].astype(F32).T.astype(BF)
    allowed = causal(tile)
    dkey[...] = jnp.zeros_like(dkey)
    dvalue[...] = jnp.zeros_like(dvalue)
    scale = HD ** (-0.5)
    for i in range(query.shape[0] // tile):
        low, high = i * tile, (i + 1) * tile
        rows = query[low:high, :]
        rows_grad = grad[low:high, :]
        log = log_ref[0, :, low:high]
        spread = jnp.sum((rows_grad.astype(F32) * mixed[low:high, :].astype(F32)).T, axis=0, keepdims=True)
        dquery_t = None
        for start, stop, masked in ((0, low, False), (low, high, True)):
            if start == stop:
                continue
            scores = dot_nt(key[start:stop, :], rows) * scale
            if masked:
                scores = jnp.where(allowed, scores, -1e30)
            probs = jnp.exp(scores - log)
            probs_grad = dot_nt(value[start:stop, :], rows_grad)
            scores_grad = (probs * (probs_grad - spread)).astype(BF)
            dvalue[start:stop, :] += dot_nn(probs.astype(BF), rows_grad)
            dkey[start:stop, :] += dot_nn(scores_grad, rows)
            term = dot_nn(key_t[:, start:stop], scores_grad)
            dquery_t = term if dquery_t is None else dquery_t + term
        dquery[low:high, :] = dquery_t.T * scale
    dkey[...] = dkey[...] * scale
    for slot, held in enumerate((dquery, dkey, dvalue)):
        out_of_order(at_ref, held, dqkv_ref.at[slot], piece)


def attend_back(qkv, out, grad, log, at, piece):
    rows, width = qkv.shape[1:]
    heads = width // HD
    return pl.pallas_call(
        functools.partial(attend_back_kernel, piece, 256),
        grid_spec=pltpu.PrefetchScalarGridSpec(
            num_scalar_prefetch=1,
            grid=(heads,),
            in_specs=[
                pl.BlockSpec((3, rows, HD), lambda h, at: (0, 0, h)),
                pl.BlockSpec((rows, HD), lambda h, at: (0, h)),
                pl.BlockSpec((rows, HD), lambda h, at: (0, h)),
                pl.BlockSpec((1, 1, rows), lambda h, at: (h, 0, 0)),
            ],
            out_specs=pl.BlockSpec((3, rows, HD), lambda h, at: (0, 0, h)),
            scratch_shapes=[pltpu.VMEM((rows, HD), BF)] * 3
            + [pltpu.VMEM((HD, rows), BF)]
            + [pltpu.VMEM((rows, HD), BF)] * 2
            + [pltpu.VMEM((rows, HD), F32)] * 3,
        ),
        out_shape=jax.ShapeDtypeStruct((3, rows, width), BF),
        compiler_params=pltpu.CompilerParams(vmem_limit_bytes=VMEM_LIMIT),
        cost_estimate=pl.CostEstimate(
            flops=5 * heads * rows * rows * HD * 2, bytes_accessed=16 * rows * width, transcendentals=heads * rows * rows // 2
        ),
        name="attend_back",
    )(at, qkv, out, grad, log)


def local(
    tokens,
    block_order,
    query_weight,
    key_weight,
    value_weight,
    output_weight,
    gate_weight,
    up_weight,
    down_weight,
    query_gain,
    key_gain,
    attention_gain,
    forward_gain,
    cotangent,
):
    seqs, local_len, width = tokens.shape
    ranks = lax.axis_size("context")
    columns = lax.axis_size("tensor")
    full_len = local_len * ranks
    piece_len = full_len // block_order.shape[0]
    piece = local_len // columns
    shard_rows = seqs * piece
    count = shard_rows * columns
    context = lax.axis_index("context")
    t = lax.axis_index("tensor")
    s, core = context // 2, context % 2
    head_width = query_weight.shape[1]
    half_width = head_width // 2
    hidden_width = gate_weight.shape[1]

    def gather(values, axis):
        return lax.all_gather(values, "context", axis=axis, tiled=True)

    gain_columns = jnp.stack([attention_gain, forward_gain], axis=1)
    gain_columns = jnp.pad(gain_columns, ((0, 0), (0, HD - 2)))
    w_first = gather(jnp.concatenate([query_weight, key_weight, value_weight, output_weight.T, gain_columns], axis=1), 0)
    qkv_width = 3 * head_width
    gains = w_first[:, 4 * head_width :]
    gain_attn, gain_feed = gains[:, 0].astype(F32)[None], gains[:, 1].astype(F32)[None]
    w_gate_up = gather(jnp.concatenate([gate_weight, up_weight], axis=1), 0)
    w_down = gather(down_weight.T, 0)
    query_scaling = query_gain.astype(F32)
    key_scaling = key_gain.astype(F32)

    chips = s ^ jnp.arange(seqs, dtype=jnp.int32)
    shards = t ^ jnp.arange(columns, dtype=jnp.int32)
    starts = (2 * chips[None, :] + core) * local_len + shards[:, None] * piece
    stored = (starts[:, :, None] + jnp.arange(piece, dtype=jnp.int32)).reshape(count)
    block = stored // piece_len
    slots = jnp.arange(block_order.shape[0], dtype=jnp.int32)
    place = jnp.sum(jnp.where(block[:, None] == slots[None, :], block_order[None, :], 0), axis=1) * piece_len
    place = place + stored % piece_len
    freq = THETA ** (-jnp.arange(0, HD, 2, dtype=F32) / HD)
    angle = place.astype(F32)[:, None] * freq[None, :]
    cosine = jnp.concatenate([jnp.cos(angle), jnp.cos(angle)], axis=-1)
    sine = jnp.concatenate([-jnp.sin(angle), jnp.sin(angle)], axis=-1)
    per_block = piece_len // piece
    pieces = jnp.arange(full_len // piece, dtype=jnp.int32)
    hits = block_order[None, :] == (pieces // per_block)[:, None]
    block_at = jnp.sum(jnp.where(hits, slots[None, :], 0), axis=1)
    piece_at = block_at * per_block + pieces % per_block
    rank_of, shard_of = piece_at // columns, piece_at % columns
    at = (((rank_of % 2) ^ core) * columns + (shard_of ^ t)) * seqs + ((rank_of // 2) ^ s)
    at = (at * piece).astype(jnp.int32)

    row_shard = to_sequences(tokens, s, t)
    rows = jnp.concatenate(gather_rows(row_shard), axis=0)
    qkv_raw = dot_nn(rows, w_first[:, :qkv_width])
    query_raw = qkv_raw[:, :head_width]
    key_raw = qkv_raw[:, head_width : 2 * head_width]
    totals = sum_over_tensor(jnp.stack([jnp.sum(query_raw * query_raw, axis=1), jnp.sum(key_raw * key_raw, axis=1)]))
    factors = lax.rsqrt(totals / width + EPS)
    scaling = jnp.stack([query_gain, key_gain]).astype(F32)
    keep, send = by_rows(
        turn_kernel,
        "turn",
        core,
        [(qkv_raw, 0), (columns_of(*factors), 0), (scaling, None), (cosine, 0), (sine, 0)],
        [((3, count, half_width), BF, 1)] * 2,
    )
    qkv = jnp.concatenate([keep, swap(send, "context", 1)], axis=1)
    mixed_heads, log = attend(qkv, at, piece)

    def to_heads(values):
        keep = lax.dynamic_slice_in_dim(values, core * half_width, half_width, axis=1)
        send = lax.dynamic_slice_in_dim(values, (1 - core) * half_width, half_width, axis=1)
        return jnp.concatenate([keep, swap(send, "context", 1)], axis=0)

    def to_rows(values):
        own, other = values[:count], swap(values[count:], "context", 1)
        return jnp.concatenate([jnp.where(core == 0, own, other), jnp.where(core == 0, other, own)], axis=1)

    mixed_low = to_rows(mixed_heads)

    def chunk(values, k):
        return values[k * shard_rows : (k + 1) * shard_rows]

    order = list(range(columns))
    shard = (shard_rows, width)
    hidden_low, attended, hidden = exchange(
        "attended", 1, mixed_low, w_first, finish_attended, [row_shard, gain_attn], [(shard, F32), (shard, F32)], offset=qkv_width
    )
    gate_up = dot_nn(hidden_low, w_gate_up)
    gate, up = gate_up[:, :hidden_width], gate_up[:, hidden_width:]
    act_low = (gate * jax.nn.sigmoid(gate) * up).astype(BF)

    fed_low, upstream, _, output_pieces, feed_gain_rows = exchange(
        "fed",
        2,
        act_low,
        w_down,
        finish_fed,
        [cotangent, hidden, gain_feed],
        [(shard, BF), (shard, BF), ((seqs, piece, width), BF), ((8, width), F32)],
        chips=seqs,
    )

    own = width // ranks
    cores = [list(range(0, ranks, 2)), list(range(1, ranks, 2))]

    def product_sum(*pairs):
        other = swap(rank_products(1 - core, pairs, own), "context", 1)
        return rank_products(core, pairs, own, other)

    def scatter(values):
        return lax.psum_scatter(values, "context", scatter_dimension=0, axis_index_groups=cores, tiled=True)

    down_part = dot_tn(fed_low, act_low).astype(BF)
    down_summed = lax.psum_scatter(down_part, "context", scatter_dimension=0, tiled=True)
    output_rows = gather_rows(output_pieces)
    gate_up_low = act_back(after(fed_low, down_part), w_down, gate_up)
    gate_up_other = rank_products(1 - core, [(after(hidden_low, gate_up_low, *output_rows[:3]), gate_up_low)], own)
    gate_up_other = swap(gate_up_other, "context", 1)
    layer_output = in_place(jnp.stack(output_rows), s, t, BF)
    gate_up_part = rank_products(core, [(after(hidden_low, layer_output), gate_up_low)], own, gate_up_other)
    gate_up_summed = scatter(gate_up_part)
    gate_up_low = after(gate_up_low, gate_up_part)
    attended_low, hidden_grad, attn_gain_rows = exchange(
        "hidden_grad",
        3,
        gate_up_low,
        w_gate_up,
        finish_hidden_grad,
        [attended, upstream, gain_attn],
        [(shard, F32), ((8, width), F32)],
    )
    mixed_grad = dot_nn(attended_low, w_first[:, qkv_width : 4 * head_width]).astype(BF)
    dqkv = attend_back(qkv, mixed_heads, to_heads(mixed_grad), log, at, piece)
    dqkv_other = swap(dqkv[:, count:], "context", 1)
    inner, head_gain_rows = by_rows(
        inner_kernel,
        "inner",
        core,
        [(dqkv, 1), (dqkv_other, 1), (qkv_raw, 0), (columns_of(*factors), 0), (scaling, None), (cosine, 0), (sine, 0)],
        [((2, 8, count), F32, 2), ((2, 8, head_width), F32, None)],
    )
    inner = sum_over_tensor(inner[:, 0])
    (qkv_low,) = by_rows(
        raw_grad_kernel,
        "raw_grad",
        core,
        [
            (dqkv, 1),
            (dqkv_other, 1),
            (qkv_raw, 0),
            (columns_of(*factors, *(inner * factors**3 / width)), 0),
            (scaling, None),
            (cosine, 0),
            (sine, 0),
        ],
        [((count, 3 * head_width), BF, 0)],
    )
    qkv_part = product_sum((rows, qkv_low), (attended_low, mixed_low))
    qkv_out_summed = scatter(after(qkv_part, gate_up_summed, down_summed))
    every, width_gains, head_gains = exchange(
        "tokens_grad",
        4,
        after(qkv_low, qkv_part),
        w_first,
        None,
        [hidden_grad, attn_gain_rows, feed_gain_rows, head_gain_rows.reshape(16, head_width)],
        [((8, own), F32), ((8, head_width), F32)],
        chips=seqs,
        last=True,
    )
    tokens_grad = in_place(every.reshape(columns, seqs, piece, width), s, t, F32)

    down_summed, gate_up_summed, qkv_out_summed = (
        values.astype(F32) for values in (down_summed, gate_up_summed, qkv_out_summed)
    )
    return (
        layer_output,
        tokens_grad,
        qkv_out_summed[:, :head_width],
        qkv_out_summed[:, head_width : 2 * head_width],
        qkv_out_summed[:, 2 * head_width : 3 * head_width],
        qkv_out_summed[:, 3 * head_width :].T,
        gate_up_summed[:, :hidden_width],
        gate_up_summed[:, hidden_width:],
        down_summed.T,
        head_gains[0],
        head_gains[1],
        width_gains[0],
        width_gains[1],
    )


def solution(mesh):
    return jax.shard_map(
        local,
        mesh=mesh,
        in_specs=(
            P(None, "context", None),
            P(),
            P("context", "tensor"),
            P("context", "tensor"),
            P("context", "tensor"),
            P("tensor", "context"),
            P("context", "tensor"),
            P("context", "tensor"),
            P("tensor", "context"),
            P("tensor"),
            P("tensor"),
            P("context"),
            P("context"),
            P(None, "context", None),
        ),
        out_specs=(
            P(None, "context", None),
            P(None, "context", None),
            P("context", "tensor"),
            P("context", "tensor"),
            P("context", "tensor"),
            P("tensor", "context"),
            P("context", "tensor"),
            P("context", "tensor"),
            P("tensor", "context"),
            P("tensor"),
            P("tensor"),
            P("context"),
            P("context"),
        ),
        check_vma=False,
    )
```

time: 2470 us -> 844 us (0.34)
  waiting for transfers between devices: 1860 us -> 191 us
  Pallas kernels: 0 us -> 481 us
  matrix products: 310 us -> 51.4 us
  other arithmetic: 137 us -> 24.3 us
  blocking collectives: 66 us -> 0 us
    reduce_scatter x9 -> x3, waiting for transfers between devices: 801 us -> 0.01 us  [the longest x2 0.01 us: scatter(): lax.psum_scatter(values, 'context', scatter_dimension=0, axis_index_group...]
    psum x4 -> x0, waiting for transfers between devices: 666 us -> none  [the longest x1 174 us: local(): lax.psum(by_transpose(query_raw_low, w_query) + by_transpose(key_raw_low,...]
    pallas_call x0 -> x16, Pallas kernels: none -> 481 us  [the longest x4 335 us: exchange(): pl.pallas_call(functools.partial(exchange_kernel, size, width, depth, off...]
    all_gather x9 -> x3, waiting for transfers between devices: 388 us -> 86.1 us  [gather(): return lax.all_gather(values, 'context', axis=axis, tiled=True)]
    dot_general x27 -> x4, matrix products: 310 us -> 51.4 us  [the longest x3 37.4 us: dot_nn(): return jnp.dot(left, right, preferred_element_type=F32)]
    ppermute x0 -> x21, waiting for transfers between devices: none -> 105 us  [swap(): return lax.ppermute(values, axis, [(i, i ^ mask) for i in range(size)])]
    convert_element_type x14 -> x5, other arithmetic: 61.8 us -> 8.43 us  [the longest x1 3.88 us: local(): act_low = (gate * jax.nn.sigmoid(gate) * up).astype(BF)]
    reduce_sum x9 -> x3, other arithmetic: 44.2 us -> 0.52 us  [the longest x1 0.35 us: local(): jnp.sum(key_raw * key_raw, axis=1)]
  transfers between devices with their start and end apart: 22 -> 27, of which waited for: 18 -> 19; matrix products, arithmetic and copies ran while one was open for 14% -> 10% of each run, Pallas kernels for 0% -> 48%
where the time goes in v1:
time: 844 us; the launch traced here: 835 us
  Pallas kernels  481 us (57%)
  waiting for transfers between devices  191 us (23%)
  matrix products  51.4 us (6%)
  local copies, waits for them, and re-layouts  47.4 us (6%)
  starting transfers between devices  25.1 us (3%)
  other arithmetic  24.3 us (3%)
  between operations  15 us (2%)
    pallas_call x4, Pallas kernels, exchange(): pl.pallas_call(functools.partial(exchange_kernel, size, width, depth, off...  335 us
    ppermute x21, waiting for transfers between devices, swap(): return lax.ppermute(values, axis, [(i, i ^ mask) for i in range(size)])  105 us
    all_gather x3, waiting for transfers between devices, gather(): return lax.all_gather(values, 'context', axis=axis, tiled=True)  86.1 us
    pallas_call x4, Pallas kernels, rank_products(): pl.pallas_call(functools.partial(rank_products_kernel, min(512, *[right.s...  49.1 us
    dot_general x3, matrix products, dot_nn(): return jnp.dot(left, right, preferred_element_type=F32)  37.4 us
    unnamed x64, local copies, waits for them, and re-layouts  31.1 us
    pallas_call x3, Pallas kernels, by_rows(): pl.pallas_call(kernel, grid_spec=pltpu.PrefetchScalarGridSpec(num_scalar_...  26.5 us
    ppermute x21, starting transfers between devices, swap(): return lax.ppermute(values, axis, [(i, i ^ mask) for i in range(size)])  24.8 us
  transfers between devices with their start and end apart: 27, of which 19 were waited for; matrix products, arithmetic and copies ran while one was open for 10% of the time, Pallas kernels for 48%

profile of v1, /device:TPU:9, one launch (start us, length us, event | category | flops | bytes accessed | tf_op | source)
XLA Modules:
  0.0 835.0 jit_solution(5102117216609640706)
XLA Ops:
  14.0 2.8 pad_maximum_fusion.1
  18.1 2.5 collective-permute-start.1
  20.8 1.4 copy.53
  22.3 1.7 constant_dynamic-update-slice_fusion.6
  24.4 6.2 collective-permute-done
  30.6 5.7 collective-permute-done.1
  36.3 24.1 %collective-permute-done.2 = bf16[64,2048]{1,0:T(8,128)(2,1)S(1)} collective-permute-done((bf16[64,2048]{1,0:T(8,128)(2,1)S(1)}, bf16[64,2048]{1,0:T(8,128)(2,1)S(1)}, u32[]{:S(2)}, u32[]{:S(2)}) %collective-permute-start.2) | collective-permute-done | bytes 262176 | tf_op jit(solution)/shard_map/ppermute | solution.py:37
  60.5 1.2 collective-permute-start.3
  61.8 1.9 fusion.10
  64.7 1.3 collective-permute-start.4
  69.4 5.6 collective-permute-done.3
  76.1 8.7 %collective-permute-done.4 = bf16[256,2048]{1,0:T(8,128)(2,1)S(1)} collective-permute-done((bf16[256,2048]{1,0:T(8,128)(2,1)S(1)}, bf16[256,2048]{1,0:T(8,128)(2,1)S(1)}, u32[]{:S(2)}, u32[]{:S(2)}) %collective-permute-start.4) | collective-permute-done | bytes 1048608 | tf_op jit(solution)/shard_map/ppermute | solution.py:37
  85.9 12.4 %collective-permute-done.5 = bf16[256,2048]{1,0:T(8,128)(2,1)S(1)} collective-permute-done((bf16[256,2048]{1,0:T(8,128)(2,1)S(1)}, bf16[256,2048]{1,0:T(8,128)(2,1)S(1)}, u32[]{:S(2)}, u32[]{:S(2)}) %collective-permute-start.5) | collective-permute-done | bytes 1048608 | tf_op jit(solution)/shard_map/ppermute | solution.py:37
  99.4 16.1 %all-gather.4.cloned.1.call-done.w_ref = bf16[2048,2176]{1,0:T(8,128)(2,1)} async-done(((bf16[256,2176]{1,0:T(8,128)(2,1)}), bf16[2048,2176]{1,0:T(8,128)(2,1)}) %all-gather.4.cloned.1.call-update) | async-done | bytes 8912912 | tf_op jit(solution)/shard_map/all_gather | solution.py:838
  115.5 10.5 %fusion.1.raw_ref = f32[1024,1536]{1,0:T(8,128)S(1)} fusion(bf16[1024,2048]{1,0:T(8,128)(2,1)} %constant_dynamic-update-slice_fusion.refs_0_, bf16[2048,2176]{1,0:T(8,128)(2,1)} %all-gather.4.cloned.1.call-done.w_ref), kind=kOutput, calls=%fused_computation.3 | convolution fusion | flops 6442450944 | bytes 16777216 | tf_op jit(solution)/shard_map/dot_general | solution.py:20
  126.0 2.6 copy-done
  129.0 1.3 collective-permute-start.7
  131.0 1.2 collective-permute-start.6
  133.5 2.5 collective-permute-done.8
  137.8 8.2 turn.1
  146.0 1.7 collective-permute-start.9
  148.4 1.5 constant_dynamic-update-slice_fusion.13
  151.1 1.8 copy-done.11
  152.8 14.8 %attend.1 = (bf16[2048,256]{1,0:T(8,128)(2,1)}, f32[2,1,2048]{2,1,0:T(1,128)}) custom-call(s32[32]{0:T(128)} %add_multiply_fusion.1.at_ref, bf16[3,2048,256]{2,1,0:T(8,128)(2,1)} %copy-done.11), custom_call_target="tpu_custom_call" | custom-call | flops 4294967296 | bytes 4194304 | tf_op jit(solution)/shard_map/attend/pallas_call | solution.py:718
  169.1 2.4 convert_reduce_fusion
  173.7 77.3 %attended.1 = (bf16[1024,2048]{1,0:T(8,128)(2,1)}, f32[256,2048]{1,0:T(8,128)}, f32[256,2048]{1,0:T(8,128)}) custom-call(bf16[1024,512]{1,0:T(8,128)(2,1)} %pad_maximum_fusion.3.a_ref.refs_3_, bf16[2048,2176]{1,0:T(8,128)(2,1)} %all-gather.4.cloned.1.call-done.w_ref, bf16[256,2048]{1,0:T(8,128)(2,1)} %copy-done.5, f32[1,2048]{1,0:T(1,128)} %bitcast.89), custom_call_target="tpu_custom_call" | custom-call | flops 2147483648 | bytes 240000000 | tf_op jit(solution)/shard_map/attended/pallas_call | solution.py:452
  251.0 18.5 %all-gather.6.cloned.1.call-done.w_ref = bf16[2048,4096]{1,0:T(8,128)(2,1)} async-done(((bf16[256,4096]{1,0:T(8,128)(2,1)}), bf16[2048,4096]{1,0:T(8,128)(2,1)}) %all-gather.6.cloned.1.call-update) | async-done | bytes 16777232 | tf_op jit(solution)/shard_map/all_gather | solution.py:838
  269.5 21.6 %fusion.38.gate_up_ref = f32[1024,4096]{1,0:T(8,128)S(1)} fusion(bf16[1024,2048]{1,0:T(8,128)(2,1)} %get-tuple-element.47.refs_0_, bf16[2048,4096]{1,0:T(8,128)(2,1)} %all-gather.6.cloned.1.call-done.w_ref), kind=kOutput, calls=%fused_computation.127 | convolution fusion | flops 17179869184 | bytes 37748736 | tf_op jit(solution)/shard_map/dot_general | solution.py:20
  291.2 5.8 copy-done.1
  296.9 3.9 fusion.a_ref
  300.8 51.5 %all-gather.8.cloned.1.call-done.w_ref = bf16[2048,2048]{1,0:T(8,128)(2,1)} async-done(((bf16[256,2048]{1,0:T(8,128)(2,1)}), bf16[2048,2048]{1,0:T(8,128)(2,1)}) %all-gather.8.cloned.1.call-update) | async-done | bytes 8388624 | tf_op jit(solution)/shard_map/all_gather | solution.py:838
  352.3 81.5 %fed.1 = (bf16[1024,2048]{1,0:T(8,128)(2,1)}, bf16[256,2048]{1,0:T(8,128)(2,1)}, bf16[256,2048]{1,0:T(8,128)(2,1)}, bf16[4,64,2048]{2,1,0:T(8,128)(2,1)}, f32[8,2048]{1,0:T(8,128)}) custom-call(bf16[1024,2048]{1,0:T(8,128)(2,1)} %fusion.a_ref, bf16[2048,2048]{1,0:T(8,128)(2,1)} %all-gather.8.cloned.1.call-done.w_ref, bf16[4,256,2048]{2,1,0:T(8,128)(2,1)} %refs_0_.1, ...), custom_call_target="tpu_custom_call" | custom-call | flops 8589934592 | bytes 240000000 | tf_op jit(solution)/shard_map/fed/pallas_call | solution.py:452
  433.8 14.0 %convolution_convert_fusion = bf16[2048,2048]{1,0:T(8,128)(2,1)} fusion(bf16[1024,2048]{1,0:T(8,128)(2,1)} %get-tuple-element.45.grad_ref, bf16[1024,2048]{1,0:T(8,128)(2,1)} %fusion.a_ref), kind=kOutput, calls=%fused_computation.2 | convolution fusion | flops 8594128896 | bytes 16777216 | tf_op jit(solution)/shard_map/dot_general | solution.py:28
  450.6 22.5 %act_back.1.refs_1_.a_ref = bf16[1024,4096]{1,0:T(8,128)(2,1)} custom-call(bf16[1024,2048]{1,0:T(8,128)(2,1)} %get-tuple-element.45.grad_ref, bf16[2048,2048]{1,0:T(8,128)(2,1)} %all-gather.8.cloned.1.call-done.w_ref, f32[1024,4096]{1,0:T(8,128)} %copy-done.1), custom_call_target="tpu_custom_call" | custom-call | flops 8589934592 | bytes 40000000 | tf_op jit(solution)/shard_map/act_back/pallas_call | solution.py:609
  473.1 14.6 %rank_products.4 = bf16[1024,4096]{1,0:T(8,128)(2,1)} custom-call(s32[1]{0:T(128)} %bitcast.19.core_ref, bf16[1024,2048]{1,0:T(8,128)(2,1)} %get-tuple-element.47.refs_0_, bf16[1024,4096]{1,0:T(8,128)(2,1)} %act_back.1.refs_1_.a_ref), custom_call_target="tpu_custom_call" | custom-call | flops 8589934592 | bytes 30000000 | tf_op jit(solution)/shard_map/rank_products/pallas_call | solution.py:644
  487.8 3.6 collective-permute-start.14
  493.1 24.0 %collective-permute-done.13 = bf16[4,64,2048]{2,1,0:T(8,128)(2,1)S(1)} collective-permute-done((bf16[4,64,2048]{2,1,0:T(8,128)(2,1)S(1)}, bf16[4,64,2048]{2,1,0:T(8,128)(2,1)S(1)}, u32[]{:S(2)}, u32[]{:S(2)}) %collective-permute-start.13) | collective-permute-done | bytes 1048608 | tf_op jit(solution)/shard_map/ppermute | solution.py:37
  517.1 2.3 pad_maximum_fusion.in_ref
  519.4 5.4 place_rows.2
  524.8 15.3 %rank_products.5 = bf16[1024,4096]{1,0:T(8,128)(2,1)} custom-call(s32[1]{0:T(128)} %bitcast.2.core_ref, bf16[1024,2048]{1,0:T(8,128)(2,1)} %get-tuple-element.47.refs_0_, bf16[1024,4096]{1,0:T(8,128)(2,1)} %act_back.1.refs_1_.a_ref, bf16[1024,4096]{1,0:T(8,128)(2,1)} %collective-permute-done.14.refs_2_), custom_call_target="tpu_custom_call" | custom-call | flops 8589934592 | bytes 30000000 | tf_op jit(solution)/shard_map/rank_products/pallas_call | solution.py:644
  540.2 83.6 %hidden_grad.1 = (bf16[1024,2048]{1,0:T(8,128)(2,1)}, f32[256,2048]{1,0:T(8,128)}, f32[8,2048]{1,0:T(8,128)}) custom-call(bf16[1024,4096]{1,0:T(8,128)(2,1)} %act_back.1.refs_1_.a_ref, bf16[2048,4096]{1,0:T(8,128)(2,1)} %all-gather.6.cloned.1.call-done.w_ref, f32[256,2048]{1,0:T(8,128)} %get-tuple-element.49.refs_0_, ...), custom_call_target="tpu_custom_call" | custom-call | flops 17179869184 | bytes 240000000 | tf_op jit(solution)/shard_map/hidden_grad/pallas_call | solution.py:452
  623.8 5.2 fusion.7
  629.1 3.2 collective-permute-start.15
  632.3 1.5 collective-permute-done.15
  634.9 20.3 %attend_back.1.own_ref = bf16[3,2048,256]{2,1,0:T(8,128)(2,1)} custom-call(s32[32]{0:T(128)} %add_multiply_fusion.1.at_ref, bf16[3,2048,256]{2,1,0:T(8,128)(2,1)} %copy-done.11, bf16[2048,256]{1,0:T(8,128)(2,1)} %get-tuple-element.40.out_ref, bf16[2048,256]{1,0:T(8,128)(2,1)} %pad_maximum_fusion.4.grad_ref, f32[2,1,2048]{2,1,0:T(1,128)} %get-tuple-element.52.log_ref), custom_call_target="tpu_custom_call" | custom-call | flops 10737418240 | bytes 8388608 | tf_op jit(solution)/shard_map/attend_back/pallas_call | solution.py:780
  655.2 1.5 slice.197
  657.2 3.0 collective-permute-done.16.other_ref
  661.4 9.7 %inner.1 = (f32[2,8,1024]{2,1,0:T(8,128)}, f32[2,8,512]{2,1,0:T(8,128)}) custom-call(s32[1]{0:T(128)} %bitcast.2.core_ref, bf16[3,2048,256]{2,1,0:T(8,128)(2,1)} %attend_back.1.own_ref, bf16[3,1024,256]{2,1,0:T(8,128)(2,1)} %copy-done.4, f32[1024,1536]{1,0:T(8,128)} %copy-done, f32[1024,8]{1,0:T(8,128)} %pad.14.column_ref, ...), custom_call_target="tpu_custom_call" | custom-call | tf_op jit(solution)/shard_map/inner/pallas_call | solution.py:574
  672.3 1.2 collective-permute-start.17
  673.5 1.2 collective-permute-start.19
  675.2 1.7 collective-permute-done.19
  678.2 8.5 %raw_grad.1.refs_2_.a_ref = bf16[1024,1536]{1,0:T(8,128)(2,1)} custom-call(s32[1]{0:T(128)} %bitcast.2.core_ref, bf16[3,2048,256]{2,1,0:T(8,128)(2,1)} %attend_back.1.own_ref, bf16[3,1024,256]{2,1,0:T(8,128)(2,1)} %copy-done.4, f32[1024,1536]{1,0:T(8,128)} %copy-done, f32[1024,8]{1,0:T(8,128)} %pad.15.column_ref, f32[2,512]{1,0:T(2,128)} %maximum_convert_fusion.gain_ref, ...), custom_call_target="tpu_custom_call" | custom-call | tf_op jit(solution)/shard_map/raw_grad/pallas_call | solution.py:574
  686.7 9.1 %rank_products.6 = bf16[1024,2048]{1,0:T(8,128)(2,1)} custom-call(s32[1]{0:T(128)} %bitcast.19.core_ref, bf16[1024,2048]{1,0:T(8,128)(2,1)} %constant_dynamic-update-slice_fusion.refs_0_, bf16[1024,2048]{1,0:T(8,128)(2,1)} %get-tuple-element.51.refs_1_, bf16[1024,1536]{1,0:T(8,128)(2,1)} %raw_grad.1.refs_2_.a_ref, ...), custom_call_target="tpu_custom_call" | custom-call | flops 4294967296 | bytes 30000000 | tf_op jit(solution)/shard_map/rank_products/pallas_call | solution.py:644
  695.9 2.0 collective-permute-start.20
  697.8 7.1 collective-permute-done.20.refs_4_
  704.9 10.0 %rank_products.7 = bf16[1024,2048]{1,0:T(8,128)(2,1)} custom-call(s32[1]{0:T(128)} %bitcast.2.core_ref, bf16[1024,2048]{1,0:T(8,128)(2,1)} %constant_dynamic-update-slice_fusion.refs_0_, bf16[1024,2048]{1,0:T(8,128)(2,1)} %get-tuple-element.51.refs_1_, bf16[1024,1536]{1,0:T(8,128)(2,1)} %raw_grad.1.refs_2_.a_ref, ...), custom_call_target="tpu_custom_call" | custom-call | flops 4294967296 | bytes 30000000 | tf_op jit(solution)/shard_map/rank_products/pallas_call | solution.py:644
  715.0 92.7 %tokens_grad.1 = (bf16[1024,2048]{1,0:T(8,128)(2,1)}, f32[8,256]{1,0:T(8,128)}, f32[8,512]{1,0:T(8,128)}) custom-call(bf16[1024,1536]{1,0:T(8,128)(2,1)} %raw_grad.1.refs_2_.a_ref, bf16[2048,2176]{1,0:T(8,128)(2,1)} %all-gather.4.cloned.1.call-done.w_ref, f32[256,2048]{1,0:T(8,128)} %get-tuple-element.55.refs_0_, f32[8,2048]{1,0:T(8,128)} %get-tuple-element.56.refs_1_, ...), custom_call_target="tpu_custom_call" | custom-call | flops 6442450944 | bytes 240000000 | tf_op jit(solution)/shard_map/tokens_grad/pallas_call | solution.py:452
  807.7 6.8 place_rows.3
  814.4 1.4 fusion.31
  815.9 1.4 fusion.30
  817.2 1.6 convert_bitcast_fusion
  818.8 2.9 copy.56
  821.7 2.5 fusion.27
  824.2 1.5 convert_element_type.68
  (152 shorter events, 38.0 us)
Async XLA Ops:
  7.2 6.8 copy-start.9
  7.2 108.3 %all-gather.4.cloned.1.call-start = ((), (), s32[]{:S(2)}) async-start(), calls=%async_computation.3 | async-start | bytes 10027008 | tf_op jit(solution)/shard_map/all_gather | solution.py:838
  12.9 1.0 copy-start.6
  13.9 6.9 copy-start.8
  13.9 255.6 %all-gather.6.cloned.1.call-start = ((), (), s32[]{:S(2)}) async-start(), calls=%async_computation.4 | async-start | bytes 18874368 | tf_op jit(solution)/shard_map/all_gather | solution.py:838
  16.8 7.5 copy-start.20
  16.8 335.5 %all-gather.8.cloned.1.call-start = ((), (), s32[]{:S(2)}) async-start(), calls=%async_computation.5 | async-start | bytes 9437184 | tf_op jit(solution)/shard_map/all_gather | solution.py:838
  18.0 45.6 %copy-start.18 = (bf16[512]{0:T(512)(128)(2,1)S(1)}, bf16[512]{0:T(512)(128)(2,1)}, u32[]{:S(2)}) copy-start(bf16[512]{0:T(512)(128)(2,1)} %param.23) | copy-start | bytes 3076
  18.1 45.6 %copy-start.19 = (bf16[512]{0:T(512)(128)(2,1)S(1)}, bf16[512]{0:T(512)(128)(2,1)}, u32[]{:S(2)}) copy-start(bf16[512]{0:T(512)(128)(2,1)} %param.24) | copy-start | bytes 3076
  18.1 12.5 %collective-permute-start = (bf16[64,2048]{1,0:T(8,128)(2,1)S(1)}, bf16[64,2048]{1,0:T(8,128)(2,1)S(1)}, u32[]{:S(2)}, u32[]{:S(2)}) collective-permute-start(bf16[64,2048]{1,0:T(8,128)(2,1)S(1)} %get-tuple-element.123), channel_id=1, source_target_pairs={{0,8},{4,12},{8,0},{12,4},{16,24},{20,28},{24,16},{28,20},{1,9},{5... | collective-permute-start | bytes 786440 | tf_op jit(solution)/shard_map/ppermute | solution.py:37
  18.1 18.1 %collective-permute-start.1 = (bf16[64,2048]{1,0:T(8,128)(2,1)S(1)}, bf16[64,2048]{1,0:T(8,128)(2,1)S(1)}, u32[]{:S(2)}, u32[]{:S(2)}) collective-permute-start(bf16[64,2048]{1,0:T(8,128)(2,1)S(1)} %get-tuple-element.122), channel_id=1, source_target_pairs={{0,16},{4,20},{8,24},{12,28},{16,0},{20,4},{24,8},{28,12},{1,17},{... | collective-permute-start | bytes 786440 | tf_op jit(solution)/shard_map/ppermute | solution.py:37
  20.6 39.8 %collective-permute-start.2 = (bf16[64,2048]{1,0:T(8,128)(2,1)S(1)}, bf16[64,2048]{1,0:T(8,128)(2,1)S(1)}, u32[]{:S(2)}, u32[]{:S(2)}) collective-permute-start(bf16[64,2048]{1,0:T(8,128)(2,1)S(1)} %get-tuple-element.121), channel_id=1, source_target_pairs={{0,24},{4,28},{8,16},{12,20},{16,8},{20,12},{24,0},{28,4},{1,25},{... | collective-permute-start | bytes 786440 | tf_op jit(solution)/shard_map/ppermute | solution.py:37
  22.2 692.7 %reduce-scatter.6.cloned.1.call-start = ((), (), s32[]{:S(2)}) async-start(), calls=%async_computation.7 | async-start | bytes 9437184 | tf_op jit(solution)/shard_map/reduce_scatter | solution.py:935
  60.5 25.4 %copy-start.5 = (bf16[256,2048]{1,0:T(8,128)(2,1)}, bf16[256,2048]{1,0:T(8,128)(2,1)S(1)}, u32[]{:S(2)}) copy-start(bf16[256,2048]{1,0:T(8,128)(2,1)S(1)} %pad_maximum_fusion.2.refs_0_) | copy-start | bytes 3145732
  60.5 14.5 %collective-permute-start.3 = (bf16[256,2048]{1,0:T(8,128)(2,1)S(1)}, bf16[256,2048]{1,0:T(8,128)(2,1)S(1)}, u32[]{:S(2)}, u32[]{:S(2)}) collective-permute-start(bf16[256,2048]{1,0:T(8,128)(2,1)S(1)} %pad_maximum_fusion.2.refs_0_), channel_id=1, source_target_pairs={{0,1},{1,0},{2,3},{3,2},{4,5},{5,4},{6,7},{7,6},{8,9},{9,8},{10,11... | collective-permute-start | bytes 3145736 | tf_op jit(solution)/shard_map/ppermute | solution.py:37
  64.7 20.1 %collective-permute-start.4 = (bf16[256,2048]{1,0:T(8,128)(2,1)S(1)}, bf16[256,2048]{1,0:T(8,128)(2,1)S(1)}, u32[]{:S(2)}, u32[]{:S(2)}) collective-permute-start(bf16[256,2048]{1,0:T(8,128)(2,1)S(1)} %pad_maximum_fusion.2.refs_0_), channel_id=1, source_target_pairs={{0,2},{1,3},{2,0},{3,1},{4,6},{5,7},{6,4},{7,5},{8,10},{9,11},{10,... | collective-permute-start | bytes 3145736 | tf_op jit(solution)/shard_map/ppermute | solution.py:37
  67.0 31.3 %collective-permute-start.5 = (bf16[256,2048]{1,0:T(8,128)(2,1)S(1)}, bf16[256,2048]{1,0:T(8,128)(2,1)S(1)}, u32[]{:S(2)}, u32[]{:S(2)}) collective-permute-start(bf16[256,2048]{1,0:T(8,128)(2,1)S(1)} %pad_maximum_fusion.2.refs_0_), channel_id=1, source_target_pairs={{0,3},{1,2},{2,1},{3,0},{4,7},{5,6},{6,5},{7,4},{8,11},{9,10},{10,... | collective-permute-start | bytes 3145736 | tf_op jit(solution)/shard_map/ppermute | solution.py:37
  126.0 2.6 copy-start
  129.0 3.3 collective-permute-start.7
  131.0 2.5 collective-permute-start.6
  132.2 3.8 collective-permute-start.8
  136.0 0.6 copy-start.12
  136.1 0.6 copy-start.14
  136.1 0.6 copy-start.16
  146.0 5.0 collective-permute-start.9
  151.1 1.8 copy-start.11
  168.7 2.8 collective-permute-start.10
  291.1 5.8 copy-start.1
  447.9 1.2 copy-start.10
  447.9 267.0 %reduce-scatter.4.cloned.1.call-start = ((), (), s32[]{:S(2)}) async-start(), calls=%async_computation.6 | async-start | bytes 10485760 | tf_op jit(solution)/shard_map/reduce_scatter | solution.py:932
  449.1 24.0 %collective-permute-start.11 = (bf16[4,64,2048]{2,1,0:T(8,128)(2,1)S(1)}, bf16[4,64,2048]{2,1,0:T(8,128)(2,1)S(1)}, u32[]{:S(2)}, u32[]{:S(2)}) collective-permute-start(bf16[4,64,2048]{2,1,0:T(8,128)(2,1)S(1)} %copy-done.10), channel_id=1, source_target_pairs={{0,1},{1,0},{2,3},{3,2},{4,5},{5,4},{6,7},{7,6},{8,9},{9,8},{10,11... | collective-permute-start | bytes 3145736 | tf_op jit(solution)/shard_map/ppermute | solution.py:37
  449.6 23.5 %collective-permute-start.12 = (bf16[4,64,2048]{2,1,0:T(8,128)(2,1)S(1)}, bf16[4,64,2048]{2,1,0:T(8,128)(2,1)S(1)}, u32[]{:S(2)}, u32[]{:S(2)}) collective-permute-start(bf16[4,64,2048]{2,1,0:T(8,128)(2,1)S(1)} %copy-done.10), channel_id=1, source_target_pairs={{0,2},{1,3},{2,0},{3,1},{4,6},{5,7},{6,4},{7,5},{8,10},{9,11},{10,... | collective-permute-start | bytes 3145736 | tf_op jit(solution)/shard_map/ppermute | solution.py:37
  487.8 37.0 %collective-permute-start.14 = (bf16[1024,4096]{1,0:T(8,128)(2,1)}, bf16[1024,4096]{1,0:T(8,128)(2,1)}, u32[]{:S(2)}, u32[]{:S(2)}) collective-permute-start(bf16[1024,4096]{1,0:T(8,128)(2,1)} %rank_products.4), channel_id=1, source_target_pairs={{0,4},{4,0},{8,12},{12,8},{16,20},{20,16},{24,28},{28,24},{1,5},{5... | collective-permute-start | bytes 25165832 | tf_op jit(solution)/shard_map/ppermute | solution.py:37
  491.4 25.7 %collective-permute-start.13 = (bf16[4,64,2048]{2,1,0:T(8,128)(2,1)S(1)}, bf16[4,64,2048]{2,1,0:T(8,128)(2,1)S(1)}, u32[]{:S(2)}, u32[]{:S(2)}) collective-permute-start(bf16[4,64,2048]{2,1,0:T(8,128)(2,1)S(1)} %copy-done.10), channel_id=1, source_target_pairs={{0,3},{1,2},{2,1},{3,0},{4,7},{5,6},{6,5},{7,4},{8,11},{9,10},{10,... | collective-permute-start | bytes 3145736 | tf_op jit(solution)/shard_map/ppermute | solution.py:37
  540.1 284.1 %reduce-scatter.8.cloned.1.call-start = ((), (), s32[]{:S(2)}) async-start(), calls=%async_computation.8 | async-start | bytes 5242880 | tf_op jit(solution)/shard_map/reduce_scatter | solution.py:932
  629.1 4.8 collective-permute-start.15
  656.7 20.3 %copy-start.13 = (f32[2,1024]{1,0:T(2,128)S(1)}, f32[2,1024]{1,0:T(2,128)}, u32[]{:S(2)}) copy-start(f32[2,1024]{1,0:T(2,128)} %copy-done.12) | copy-start | bytes 24580
  656.7 20.3 %copy-start.15 = (f32[1024,1]{0,1:T(1,128)S(1)}, f32[1024,1]{0,1:T(1,128)}, u32[]{:S(2)}) copy-start(f32[1024,1]{0,1:T(1,128)} %copy-done.14) | copy-start | bytes 12292
  656.8 20.3 %copy-start.17 = (f32[1024,1]{0,1:T(1,128)S(1)}, f32[1024,1]{0,1:T(1,128)}, u32[]{:S(2)}) copy-start(f32[1024,1]{0,1:T(1,128)} %copy-done.16) | copy-start | bytes 12292
  656.8 3.5 collective-permute-start.16
  660.2 1.1 copy-start.4
  672.0 3.0 collective-permute-start.18
  672.3 2.9 collective-permute-start.17
  673.5 3.5 collective-permute-start.19
  695.9 9.1 %collective-permute-start.20 = (bf16[1024,2048]{1,0:T(8,128)(2,1)}, bf16[1024,2048]{1,0:T(8,128)(2,1)}, u32[]{:S(2)}, u32[]{:S(2)}) collective-permute-start(bf16[1024,2048]{1,0:T(8,128)(2,1)} %rank_products.6), channel_id=1, source_target_pairs={{0,4},{4,0},{8,12},{12,8},{16,20},{20,16},{24,28},{28,24},{1,5},{5... | collective-permute-start | bytes 12582920 | tf_op jit(solution)/shard_map/ppermute | solution.py:37
  807.6 9.6 %copy-start.7 = (bf16[256,2048]{1,0:T(8,128)(2,1)S(1)}, bf16[256,2048]{1,0:T(8,128)(2,1)}, u32[]{:S(2)}) copy-start(bf16[256,2048]{1,0:T(8,128)(2,1)} %reduce-scatter.6.cloned.1.call-done) | copy-start | bytes 3145732
  814.4 7.3 copy-start.2
  824.2 2.6 copy-start.3
Sparse Core Ops, SparseCore 0:
  14.0 101.4 all-gather.3
  117.7 151.7 all-gather.5
  271.7 80.5 all-gather.7
  448.0 89.7 reduce-scatter.5
  540.3 144.4 reduce-scatter.3
  715.1 103.3 reduce-scatter.7

commit v2 on v1

--- a/solution.py
+++ b/solution.py
@@ -508,6 +508,397 @@
     return grad
 
 
+def remote(source, target, sems, slot, device):
+    return pltpu.make_async_remote_copy(
+        src_ref=source,
+        dst_ref=target,
+        send_sem=sems[0].at[slot],
+        recv_sem=sems[1].at[slot],
+        device_id=device,
+        device_id_type=MESH,
+    )
+
+
+def meet(t, c, size, masks):
+    barrier = pltpu.get_barrier_semaphore()
+    for k in range(1, size):
+        pl.semaphore_signal(barrier, inc=1, device_id={"tensor": flip(t, k)}, device_id_type=MESH)
+    for mask in masks:
+        pl.semaphore_signal(barrier, inc=1, device_id={"context": flip(c, mask)}, device_id_type=MESH)
+    return lambda: pl.semaphore_wait(barrier, size - 1 + len(masks))
+
+
+class Line:
+    def __init__(self, chips, own, buf, up_sems, down_sems, core_sems):
+        self.chips, self.own, self.buf = chips, own, buf
+        self.sems, self.core_sems = {1: up_sems, -1: down_sems}, core_sems
+        self.c = lax.axis_index("context")
+        self.s, self.core = self.c // 2, self.c % 2
+
+    def rows(self, chip):
+        return pl.ds(pl.multiple_of((2 * chip + self.core) * self.own, self.own), self.own)
+
+    def hop(self, k, way, chip):
+        part = self.buf.at[self.rows(chip), :]
+        return remote(part, part, self.sems[way], k, {"context": self.c + 2 * way})
+
+    def cross(self, k, way, chip):
+        part = self.buf.at[self.rows(chip), :]
+        return remote(part, part, self.core_sems, 0 if k < 0 else 1 + 2 * k + (way < 0), {"context": flip(self.c, 1)})
+
+    def sends(self, k, way):
+        if way > 0:
+            return (self.s >= k) & (self.s < self.chips - 1)
+        return (self.s + k < self.chips) & (self.s > 0)
+
+    def gets(self, k, way):
+        return self.s >= k + 1 if way > 0 else self.s + k + 1 < self.chips
+
+    def each(self, test, k, act):
+        for way in (1, -1):
+            pl.when(test(k, way))(functools.partial(act, k, way))
+
+    def start(self, k):
+        self.each(self.sends, k, lambda k, way: self.hop(k, way, self.s - way * k).start())
+
+    def begin(self):
+        self.start(0)
+        self.cross(-1, 1, self.s).start()
+
+    def advance(self, k):
+        def got(k, way):
+            chip = self.s - way * (k + 1)
+            self.hop(k, way, chip).wait_recv()
+            self.cross(k, way, chip).start()
+
+        self.each(self.gets, k, got)
+        if k + 1 < self.chips - 1:
+            self.start(k + 1)
+
+    def other_core(self, k):
+        if k < 0:
+            self.cross(-1, 1, self.s).wait_recv()
+        else:
+            self.each(self.gets, k, lambda k, way: self.cross(k, way, self.s - way * (k + 1)).wait_recv())
+
+    def end(self):
+        self.cross(-1, 1, self.s).wait_send()
+        for k in range(self.chips - 1):
+            self.each(self.sends, k, lambda k, way: self.hop(k, way, self.s - way * k).wait_send())
+            self.each(self.gets, k, lambda k, way: self.cross(k, way, self.s - way * (k + 1)).wait_send())
+
+
+def line_sems(chips):
+    dma = pltpu.SemaphoreType.DMA
+    return [dma((chips - 1,))] * 4 + [dma((2 * chips - 1,))] * 2
+
+
+class Sums:
+    def __init__(self, size, t, sent, got, columns, sems, base):
+        rows = sent.shape[1]
+        low, high = pl.ds(0, rows // 2), pl.ds(rows // 2, rows // 2)
+        self.size, self.sent, self.got, self.columns, self.half = size, sent, got, columns, rows // 2
+
+        def send(slot, of, to, at, partner):
+            return remote(sent.at[of, at, columns], got.at[to, at, columns], sems, base + slot, {"tensor": flip(t, partner)})
+
+        if size == 4:
+            self.copies = [
+                send(0, 2, 2, low, 1),
+                send(1, 2, 2, high, 2),
+                send(2, 0, 0, low, 1),
+                send(3, 1, 1, high, 2),
+                send(4, 1, 1, low, 2),
+                send(5, 0, 0, high, 1),
+            ]
+            self.after_product = {3: self.copies[:2], 1: self.copies[2:3], 2: self.copies[3:4]}
+        else:
+            self.copies = [send(k - 1, k - 1, k - 1, pl.ds(0, rows), k) for k in range(1, size)]
+            self.after_product = {k: self.copies[k - 1 : k] for k in range(1, size)}
+
+    def pass_on(self):
+        if self.size != 4:
+            return
+        for copy, slot, first, then in ((0, 1, 0, 4), (1, 0, self.half, 5)):
+            self.copies[copy].wait_recv()
+
+            def step(i, carry):
+                at = pl.ds(pl.multiple_of(first + i * 16, 16), 16)
+                summed = self.sent[slot, at, self.columns].astype(F32) + self.got[2, at, self.columns].astype(F32)
+                self.sent[slot, at, self.columns] = summed.astype(BF)
+                return carry
+
+            lax.fori_loop(0, self.half // 16, step, 0)
+            self.copies[then].start()
+
+    def wait(self):
+        for copy in self.copies[2:] if self.size == 4 else self.copies:
+            copy.wait_recv()
+
+
+class Gather:
+    def __init__(self, size, t, shared, every, sems, own_sem):
+        rows = shared.shape[0]
+        half = rows // 2
+        self.size = size
+        self.own = pltpu.make_async_copy(shared, every.at[pl.ds(0, rows), :], own_sem)
+
+        def chunk(k, side):
+            return every.at[pl.ds(k * rows + side * half, half), :]
+
+        def send(slot, source, target, partner):
+            return remote(source, target, sems, slot, {"tensor": flip(t, partner)})
+
+        if size == 4:
+            self.copies = [send(2 * k + side, shared.at[pl.ds(side * half, half), :], chunk(k + 1, side), k + 1) for k in (0, 1) for side in (0, 1)]
+            self.copies += [send(4, chunk(1, 0), chunk(3, 0), 2), send(5, chunk(2, 1), chunk(3, 1), 1)]
+            self.ready = (self.copies[0:3:2], self.copies[3:0:-2])
+        else:
+            self.copies = [send(k - 1, shared, every.at[pl.ds(k * rows, rows), :], k) for k in range(1, size)]
+            self.ready = ((), self.copies)
+
+    def start(self, side):
+        for copy in self.ready[side]:
+            copy.start()
+        if side:
+            self.own.start()
+
+    def pass_on(self):
+        if self.size == 4:
+            self.copies[0].wait_recv()
+            self.copies[4].start()
+            self.copies[3].wait_recv()
+            self.copies[5].start()
+
+    def wait(self):
+        for at, copy in enumerate(self.copies):
+            if self.size != 4 or at not in (0, 3):
+                copy.wait_recv()
+        self.own.wait()
+
+    def end(self):
+        for copy in self.copies:
+            copy.wait_send()
+
+
+def links_of(size):
+    return 6 if size == 4 else size - 1
+
+
+def feed_kernel(size, chips, tile, *refs):
+    h_ref, gate_up_w_ref, down_ref, cotangent_ref, residual_ref, gain_ref = refs[:6]
+    every, slopes_ref, act_ref, down_all_ref, upstream, output, pieces, gain_rows = refs[6:14]
+    h_buf, w_buf, act, down, sent, got, total, mine, stage = refs[14:23]
+    h_sem, w_sem, stage_sem, keep_sem, own_sem = refs[23:28]
+    line_refs, sums, gather, coming, going = refs[28:34], refs[34:36], refs[36:38], refs[38:40], refs[40:42]
+    t, c = lax.axis_index("tensor"), lax.axis_index("context")
+    s = c // 2
+    rows, width = total.shape
+    hidden = act.shape[1]
+    own = down_ref.shape[0]
+    piece = rows // chips
+    tiles = hidden // tile
+    order = [3, 1, 2, 0] if size == 4 else [*range(1, size), 0]
+    line = Line(chips, own, down, line_refs[0:2], line_refs[2:4], line_refs[4:6])
+
+    def h_copy(k):
+        at = pl.ds(k * rows, rows)
+        return pltpu.make_async_copy(h_ref.at[at, :], h_buf.at[at, :], h_sem.at[k])
+
+    def w_copy(j, i):
+        at = pl.ds(pl.multiple_of(i * hidden + j * tile, tile), tile)
+        return pltpu.make_async_copy(gate_up_w_ref.at[:, at], w_buf.at[:, at], w_sem.at[j, i])
+
+    own_rows = line.rows(s)
+    own_down = pltpu.make_async_copy(down_ref, down.at[own_rows, :], keep_sem.at[0])
+    own_down.start()
+    wait_others = meet(t, c, size, [1, *range(2, 2 * chips, 2)])
+    h_copy(order[0]).start()
+    for j in range(tiles):
+        for i in range(2):
+            w_copy(j, i).start()
+    for k in order[1:]:
+        h_copy(k).start()
+    gain_rows[...] = jnp.zeros_like(gain_rows)
+    own_down.wait()
+    wait_others()
+    line.begin()
+
+    def stage_copy(slot, i, k, j):
+        at = pl.ds(pl.multiple_of(i * hidden + j * tile, tile), tile)
+        return pltpu.make_async_copy(stage.at[slot, i], slopes_ref.at[pl.ds(k * rows, rows), at], stage_sem.at[slot, i])
+
+    for n, k in enumerate(order):
+        h_copy(k).wait()
+        chunk = pl.ds(k * rows, rows)
+
+        def step(j, carry):
+            slot = (n * tiles + j) % 2
+            if n == 0:
+                for i in range(2):
+                    w_copy(j, i).wait()
+
+            @pl.when(n * tiles + j >= 2)
+            def _():
+                for i in range(2):
+                    stage_copy(slot, i, k, j).wait()
+
+            gate, up = [
+                dot_nn(h_buf[chunk, :], w_buf[:, pl.ds(pl.multiple_of(i * hidden + j * tile, tile), tile)]) for i in range(2)
+            ]
+            logistic = jax.nn.sigmoid(gate)
+            silu = gate * logistic
+            act[chunk, pl.ds(pl.multiple_of(j * tile, tile), tile)] = (silu * up).astype(BF)
+            stage[slot, 0] = (up * (logistic + silu * (1.0 - logistic))).astype(BF)
+            stage[slot, 1] = silu.astype(BF)
+            for i in range(2):
+                stage_copy(slot, i, k, j).start()
+            return carry
+
+        lax.fori_loop(0, tiles, step, 0)
+    for slot in range(2):
+        for i in range(2):
+            stage_copy(slot, i, 0, 0).wait()
+    act_out = pltpu.make_async_copy(act, act_ref, keep_sem.at[1])
+    act_out.start()
+
+    rounds = []
+
+    def fed_round(i):
+        at = pl.ds(pl.multiple_of(flip(s, i) * 2 * own, 2 * own), 2 * own)
+        group = Sums(size, t, sent, got, at, sums, links_of(size) * i)
+        for k in order:
+            value = dot_nt(act[k * rows : (k + 1) * rows, :], down[at, :])
+            if k:
+                sent[k - 1, :, at] = value.astype(BF)
+                for copy in group.after_product[k]:
+                    copy.start()
+            else:
+                total[:, at] = value
+        rounds.append(group)
+
+    line.advance(0)
+    line.other_core(-1)
+    fed_round(0)
+    line.other_core(0)
+    fed_round(1)
+    rounds[0].pass_on()
+    rounds[1].pass_on()
+    for k in range(1, chips - 1):
+        line.advance(k)
+        line.other_core(k)
+        fed_round(k + 1)
+        if k + 1 == chips - 1:
+            arrivals = [
+                (cotangent_ref.at[flip(s, j), pl.ds(pl.multiple_of(t * piece, piece), piece), :], upstream.at[pl.ds(j * piece, piece), :])
+                for j in range(chips)
+            ]
+            first = pltpu.make_async_copy(*arrivals[0], coming[0].at[0])
+            others = [remote(*arrivals[j], coming, j, {"context": flip(c, 2 * j)}) for j in range(1, chips)]
+            for copy in [first, *others]:
+                copy.start()
+        rounds[k + 1].pass_on()
+    down_out = pltpu.make_async_copy(down, down_all_ref, keep_sem.at[2])
+    down_out.start()
+    for group in rounds:
+        group.wait()
+    first.wait()
+    for copy in others:
+        copy.wait_recv()
+
+    used = 2 if size == 4 else size - 1
+
+    def finish_rows(side):
+        def step(i, carry):
+            at = pl.ds(pl.multiple_of(side * (rows // 2) + i * 16, 16), 16)
+            fed = total[at, :]
+            for other in range(used):
+                fed = fed + got[other, at, :].astype(F32)
+            factor = norm_factor(fed)
+            output[at, :] = (residual_ref[at, :] + fed * factor * gain_ref[...]).astype(BF)
+            grad, gains = norm_back(fed, factor, gain_ref[...], upstream[at, :].astype(F32))
+            gain_rows[...] += gains[:8] + gains[8:]
+            mine[at, :] = grad.astype(BF)
+            return carry
+
+        lax.fori_loop(0, rows // 32, step, 0)
+
+    share = Gather(size, t, mine, every, gather, own_sem)
+    finish_rows(0)
+    share.start(0)
+    finish_rows(1)
+    share.start(1)
+    kept = pltpu.make_async_copy(output.at[pl.ds(0, piece), :], pieces.at[0], going[0].at[0])
+    gone = [
+        remote(output.at[pl.ds(j * piece, piece), :], pieces.at[j], going, j, {"context": flip(c, 2 * j)})
+        for j in range(1, chips)
+    ]
+    for copy in [kept, *gone]:
+        copy.start()
+    share.pass_on()
+    share.wait()
+    kept.wait()
+    for copy in gone:
+        copy.wait_recv()
+    act_out.wait()
+    down_out.wait()
+    line.end()
+    share.end()
+    for copy in [*sum([group.copies for group in rounds], []), *others, *gone]:
+        copy.wait_send()
+
+
+def feed(hidden_low, gate_up_weight, down_shard, cotangent, residual, gain, chips):
+    size = lax.axis_size("tensor")
+    count, width = hidden_low.shape
+    rows = count // size
+    own, hidden = down_shard.shape
+    ranks = 2 * chips
+    tile = min(512, hidden)
+    links = links_of(size)
+    dma = pltpu.SemaphoreType.DMA
+    anywhere, whole = pl.BlockSpec(memory_space=pl.ANY), pl.BlockSpec(memory_space=pltpu.VMEM)
+    shape = jax.ShapeDtypeStruct
+    return pl.pallas_call(
+        functools.partial(feed_kernel, size, chips, tile),
+        in_specs=[anywhere] * 4 + [whole] * 2,
+        out_specs=[anywhere] * 4 + [whole] * 4,
+        out_shape=[
+            shape((count, width), BF),
+            shape((count, 2 * hidden), BF),
+            shape((count, hidden), BF),
+            shape((ranks * own, hidden), BF),
+            shape((rows, width), BF),
+            shape((rows, width), BF),
+            shape((chips, rows // chips, width), BF),
+            shape((8, width), F32),
+        ],
+        scratch_shapes=[
+            pltpu.VMEM((count, width), BF),
+            pltpu.VMEM((width, 2 * hidden), BF),
+            pltpu.VMEM((count, hidden), BF),
+            pltpu.VMEM((ranks * own, hidden), BF),
+            pltpu.VMEM((size - 1, rows, width), BF),
+            pltpu.VMEM((size - 1, rows, width), BF),
+            pltpu.VMEM((rows, width), F32),
+            pltpu.VMEM((rows, width), BF),
+            pltpu.VMEM((2, 2, rows, tile), BF),
+            dma((size,)),
+            dma((hidden // tile, 2)),
+            dma((2, 2)),
+            dma((3,)),
+            dma,
+        ]
+        + line_sems(chips)
+        + [dma((links * chips,))] * 2
+        + [dma((links,))] * 2
+        + [dma((chips,))] * 4,
+        compiler_params=pltpu.CompilerParams(vmem_limit_bytes=VMEM_LIMIT, collective_id=2, has_side_effects=True),
+        cost_estimate=pl.CostEstimate(flops=6 * count * width * hidden, bytes_accessed=400_000_000, transcendentals=count * hidden),
+        name="feed",
+    )(hidden_low, gate_up_weight, down_shard, cotangent, residual, gain)
+
+
 def turn(values, cosine, sine):
     heads = [values[:, i : i + HD] for i in range(0, values.shape[1], HD)]
     return jnp.concatenate([head * cosine + pltpu.roll(head, HD // 2, 1) * sine for head in heads], axis=1)
@@ -565,7 +956,7 @@
         out_ref[:, i * width : (i + 1) * width] = values.astype(BF)
 
 
-def by_rows(kernel, name, core, ins, outs, rows=128):
+def by_rows(kernel, name, core, ins, outs, rows=256):
     def spec(shape, dim):
         block = tuple(rows if i == dim else extent for i, extent in enumerate(shape))
         return pl.BlockSpec(block, lambda i, core: tuple(i if at == dim else 0 for at in range(len(shape))))
@@ -585,29 +976,20 @@
     )(core[None].astype(jnp.int32), *[array for array, _ in ins])
 
 
-def act_back_kernel(tile, grad_ref, w_ref, gate_up_ref, out_ref):
+def act_back_kernel(tile, grad_ref, w_ref, slopes_ref, out_ref):
     hidden = w_ref.shape[1]
-
-    def step(j, carry):
-        at = pl.ds(pl.multiple_of(j * tile, tile), tile)
-        up_at = pl.ds(pl.multiple_of(hidden + j * tile, tile), tile)
-        act_grad = dot_nn(grad_ref[...], w_ref[:, at])
-        gate, up = gate_up_ref[:, at], gate_up_ref[:, up_at]
-        logistic = jax.nn.sigmoid(gate)
-        silu = gate * logistic
-        out_ref[:, at] = (act_grad * up * (logistic + silu * (1.0 - logistic))).astype(BF)
-        out_ref[:, up_at] = (act_grad * silu).astype(BF)
-        return carry
-
-    lax.fori_loop(0, hidden // tile, step, 0)
-
-
-def act_back(fed_low, w_down, gate_up):
+    for j in range(0, hidden, tile):
+        act_grad = dot_nn(grad_ref[...], w_ref[:, j : j + tile])
+        for at in (j, hidden + j):
+            out_ref[:, at : at + tile] = (act_grad * slopes_ref[:, at : at + tile].astype(F32)).astype(BF)
+
+
+def act_back(fed_low, w_down, slopes):
     count, width = fed_low.shape
     hidden = w_down.shape[1]
     rows = 256
     return pl.pallas_call(
-        functools.partial(act_back_kernel, 256),
+        functools.partial(act_back_kernel, 512),
         grid=(count // rows,),
         in_specs=[
             pl.BlockSpec((rows, width), lambda i: (i, 0)),
@@ -619,43 +1001,90 @@
         compiler_params=pltpu.CompilerParams(vmem_limit_bytes=VMEM_LIMIT),
         cost_estimate=pl.CostEstimate(flops=2 * count * width * hidden, bytes_accessed=40_000_000, transcendentals=count * hidden),
         name="act_back",
-    )(fed_low, w_down, gate_up)
-
-
-def rank_products_kernel(tile, count, core_ref, *refs):
-    out_ref = refs[-1]
-    base = 0
-    for left_ref, right_ref in zip(refs[:count], refs[count : 2 * count]):
-        left = left_ref[...].astype(F32).T.astype(BF)
-        for at in range(0, right_ref.shape[1], tile):
-            part = dot_nn(left, right_ref[:, at : at + tile])
-            if len(refs) > 2 * count + 1:
-                part = part + refs[2 * count][:, base + at : base + at + tile].astype(F32)
-            out_ref[:, base + at : base + at + tile] = part.astype(BF)
-        base += right_ref.shape[1]
-
-
-def rank_products(core, pairs, own, added=None):
+    )(fed_low, w_down, slopes)
+
+
+def rank_sums_kernel(chips, tile, count, *refs):
+    lefts, rights, out_ref = refs[:count], refs[count : 2 * count], refs[2 * count]
+    refs = refs[2 * count + 1 :]
+    left_bufs, right_bufs = refs[:count], refs[count : 2 * count]
+    passed, got, out, left_sem, right_sem, out_sem, sent_sem, got_sem = refs[2 * count :]
+    c = lax.axis_index("context")
+    core = c % 2
+    own = out.shape[1]
+    blocks = [(j, core_at) for core_at in (1, 0) for j in range(chips)]
+
+    def left_copy(i, j, core_at):
+        rank = 2 * j + (core if core_at == 0 else 1 - core)
+        at = pl.ds(pl.multiple_of(rank * own, own), own)
+        block = left_bufs[i].at[core_at * chips + j]
+        return pltpu.make_async_copy(lefts[i].at[:, at], block, left_sem.at[i, core_at * chips + j])
+
+    tiles = [right.shape[1] // tile for right in rights]
+
+    def right_copy(i, n):
+        at = pl.ds(pl.multiple_of(n * tile, tile), tile)
+        return pltpu.make_async_copy(rights[i].at[:, at], right_bufs[i].at[:, at], right_sem.at[i, n])
+
+    barrier = pltpu.get_barrier_semaphore()
+    pl.semaphore_signal(barrier, inc=1, device_id={"context": flip(c, 1)}, device_id_type=MESH)
+    for i in range(count):
+        left_copy(i, *blocks[0]).start()
+        for n in range(tiles[i]):
+            right_copy(i, n).start()
+        for block in blocks[1:]:
+            left_copy(i, *block).start()
+    pl.semaphore_wait(barrier, 1)
+    sends = [remote(passed.at[j], got.at[j], (sent_sem, got_sem), j, {"context": flip(c, 1)}) for j in range(chips)]
+    writes = [pltpu.make_async_copy(out.at[j], out_ref.at[pl.ds(j * own, own), :], out_sem.at[j]) for j in range(chips)]
+    for at, (j, core_at) in enumerate(blocks):
+        base = 0
+        if core_at == 0:
+            sends[j].wait_recv()
+        for i in range(count):
+            left_copy(i, j, core_at).wait()
+            left = left_bufs[i][core_at * chips + j].astype(F32).T.astype(BF)
+
+            def step(n, carry):
+                if at == 0:
+                    right_copy(i, n).wait()
+                part = dot_nn(left, right_bufs[i][:, pl.ds(pl.multiple_of(n * tile, tile), tile)])
+                to = pl.ds(pl.multiple_of(base + n * tile, tile), tile)
+                if core_at:
+                    passed[j, :, to] = part.astype(BF)
+                else:
+                    out[j, :, to] = (part + got[j, :, to].astype(F32)).astype(BF)
+                return carry
+
+            lax.fori_loop(0, tiles[i], step, 0)
+            base += tiles[i] * tile
+        (sends if core_at else writes)[j].start()
+    for j in range(chips):
+        sends[j].wait_send()
+        writes[j].wait()
+
+
+def rank_sums(number, pairs, own):
     lefts, rights = [left for left, _ in pairs], [right for _, right in pairs]
     count, width = lefts[0].shape
     chips = width // (2 * own)
     across = sum(right.shape[1] for right in rights)
-    block = pl.BlockSpec((own, across), lambda j, core: (j, 0))
+    tile = min(512, *[right.shape[1] for right in rights])
+    most = max(right.shape[1] for right in rights) // tile
+    dma = pltpu.SemaphoreType.DMA
     return pl.pallas_call(
-        functools.partial(rank_products_kernel, min(512, *[right.shape[1] for right in rights]), len(pairs)),
-        grid_spec=pltpu.PrefetchScalarGridSpec(
-            num_scalar_prefetch=1,
-            grid=(chips,),
-            in_specs=[pl.BlockSpec((count, own), lambda j, core: (0, 2 * j + core[0]))] * len(pairs)
-            + [pl.BlockSpec(right.shape, lambda j, core: (0, 0)) for right in rights]
-            + [block] * (added is not None),
-            out_specs=block,
-        ),
+        functools.partial(rank_sums_kernel, chips, tile, len(pairs)),
+        in_specs=[pl.BlockSpec(memory_space=pl.ANY)] * (2 * len(pairs)),
+        out_specs=pl.BlockSpec(memory_space=pl.ANY),
         out_shape=jax.ShapeDtypeStruct((chips * own, across), BF),
-        compiler_params=pltpu.CompilerParams(vmem_limit_bytes=VMEM_LIMIT),
-        cost_estimate=pl.CostEstimate(flops=count * width * across, bytes_accessed=30_000_000, transcendentals=0),
-        name="rank_products",
-    )(core[None].astype(jnp.int32), *lefts, *rights, *([] if added is None else [added]))
+        scratch_shapes=[pltpu.VMEM((2 * chips, count, own), BF)] * len(pairs)
+        + [pltpu.VMEM(right.shape, BF) for right in rights]
+        + [pltpu.VMEM((chips, own, across), BF)] * 3
+        + [dma((len(pairs), 2 * chips)), dma((len(pairs), most)), dma((chips,)), dma((chips,)), dma((chips,))],
+        compiler_params=pltpu.CompilerParams(vmem_limit_bytes=VMEM_LIMIT, collective_id=number, has_side_effects=True),
+        cost_estimate=pl.CostEstimate(flops=2 * count * width * across, bytes_accessed=60_000_000, transcendentals=0),
+        name="rank_sums",
+    )(*lefts, *rights)
 
 
 def columns_of(*values):
@@ -663,10 +1092,16 @@
     return jnp.pad(stacked, ((0, 0), (0, 8 - len(values))))
 
 
-def in_order(at_ref, source, target, piece):
+def in_order(at_ref, source, target, piece, other=None):
+    rows = source.shape[0]
+
     def step(p, carry):
-        start = pl.multiple_of(at_ref[p], piece)
-        target[pl.ds(pl.multiple_of(p * piece, piece), piece), :] = source[pl.ds(start, piece), :]
+        start = at_ref[p]
+        at = pl.ds(pl.multiple_of(start % rows, piece), piece)
+        values = source[at, :]
+        if other is not None:
+            values = jnp.where(start < rows, values, other[at, :])
+        target[pl.ds(pl.multiple_of(p * piece, piece), piece), :] = values
         return carry
 
     lax.fori_loop(0, target.shape[0] // piece, step, 0)
@@ -687,9 +1122,9 @@
     return query_at >= key_at
 
 
-def attend_kernel(piece, tile, at_ref, qkv_ref, out_ref, log_ref, query, key, value, value_t, mixed):
+def attend_kernel(piece, tile, at_ref, own_ref, other_ref, out_ref, log_ref, query, key, value, value_t, mixed):
     for slot, held in enumerate((query, key, value)):
-        in_order(at_ref, qkv_ref.at[slot], held, piece)
+        in_order(at_ref, own_ref.at[slot], held, piece, other_ref.at[slot])
     value_t[...] = value[...].astype(F32).T.astype(BF)
     allowed = causal(tile)
     for i in range(query.shape[0] // tile):
@@ -712,15 +1147,16 @@
     out_of_order(at_ref, mixed, out_ref, piece)
 
 
-def attend(qkv, at, piece):
-    rows, width = qkv.shape[1:]
+def attend(own, other, at, piece):
+    half, width = own.shape[1:]
+    rows = 2 * half
     heads = width // HD
     return pl.pallas_call(
         functools.partial(attend_kernel, piece, 256),
         grid_spec=pltpu.PrefetchScalarGridSpec(
             num_scalar_prefetch=1,
             grid=(heads,),
-            in_specs=[pl.BlockSpec((3, rows, HD), lambda h, at: (0, 0, h))],
+            in_specs=[pl.BlockSpec((3, half, HD), lambda h, at: (0, 0, h))] * 2,
             out_specs=[
                 pl.BlockSpec((rows, HD), lambda h, at: (0, h)),
                 pl.BlockSpec((1, 1, rows), lambda h, at: (h, 0, 0)),
@@ -733,14 +1169,14 @@
             flops=2 * 2 * heads * rows * rows * HD, bytes_accessed=8 * rows * width, transcendentals=heads * rows * rows // 2
         ),
         name="attend",
-    )(at, qkv)
+    )(at, own, other)
 
 
 def attend_back_kernel(
-    piece, tile, at_ref, qkv_ref, out_ref, grad_ref, log_ref, dqkv_ref, query, key, value, key_t, grad, mixed, dquery, dkey, dvalue
+    piece, tile, at_ref, own_ref, other_ref, out_ref, grad_ref, log_ref, dqkv_ref, query, key, value, key_t, grad, mixed, dquery, dkey, dvalue
 ):
     for slot, held in enumerate((query, key, value)):
-        in_order(at_ref, qkv_ref.at[slot], held, piece)
+        in_order(at_ref, own_ref.at[slot], held, piece, other_ref.at[slot])
     in_order(at_ref, grad_ref, grad, piece)
     in_order(at_ref, out_ref, mixed, piece)
     key_t[...] = key[...].astype(F32).T.astype(BF)
@@ -774,8 +1210,9 @@
         out_of_order(at_ref, held, dqkv_ref.at[slot], piece)
 
 
-def attend_back(qkv, out, grad, log, at, piece):
-    rows, width = qkv.shape[1:]
+def attend_back(own, other, out, grad, log, at, piece):
+    half, width = own.shape[1:]
+    rows = 2 * half
     heads = width // HD
     return pl.pallas_call(
         functools.partial(attend_back_kernel, piece, 256),
@@ -783,7 +1220,8 @@
             num_scalar_prefetch=1,
             grid=(heads,),
             in_specs=[
-                pl.BlockSpec((3, rows, HD), lambda h, at: (0, 0, h)),
+                pl.BlockSpec((3, half, HD), lambda h, at: (0, 0, h)),
+                pl.BlockSpec((3, half, HD), lambda h, at: (0, 0, h)),
                 pl.BlockSpec((rows, HD), lambda h, at: (0, h)),
                 pl.BlockSpec((rows, HD), lambda h, at: (0, h)),
                 pl.BlockSpec((1, 1, rows), lambda h, at: (h, 0, 0)),
@@ -800,7 +1238,7 @@
             flops=5 * heads * rows * rows * HD * 2, bytes_accessed=16 * rows * width, transcendentals=heads * rows * rows // 2
         ),
         name="attend_back",
-    )(at, qkv, out, grad, log)
+    )(at, own, other, out, grad, log)
 
 
 def local(
@@ -844,7 +1282,6 @@
     gains = w_first[:, 4 * head_width :]
     gain_attn, gain_feed = gains[:, 0].astype(F32)[None], gains[:, 1].astype(F32)[None]
     w_gate_up = gather(jnp.concatenate([gate_weight, up_weight], axis=1), 0)
-    w_down = gather(down_weight.T, 0)
     query_scaling = query_gain.astype(F32)
     key_scaling = key_gain.astype(F32)
 
@@ -884,8 +1321,8 @@
         [(qkv_raw, 0), (columns_of(*factors), 0), (scaling, None), (cosine, 0), (sine, 0)],
         [((3, count, half_width), BF, 1)] * 2,
     )
-    qkv = jnp.concatenate([keep, swap(send, "context", 1)], axis=1)
-    mixed_heads, log = attend(qkv, at, piece)
+    received = swap(send, "context", 1)
+    mixed_heads, log = attend(keep, received, at, piece)
 
     def to_heads(values):
         keep = lax.dynamic_slice_in_dim(values, core * half_width, half_width, axis=1)
@@ -906,41 +1343,28 @@
     hidden_low, attended, hidden = exchange(
         "attended", 1, mixed_low, w_first, finish_attended, [row_shard, gain_attn], [(shard, F32), (shard, F32)], offset=qkv_width
     )
-    gate_up = dot_nn(hidden_low, w_gate_up)
-    gate, up = gate_up[:, :hidden_width], gate_up[:, hidden_width:]
-    act_low = (gate * jax.nn.sigmoid(gate) * up).astype(BF)
-
-    fed_low, upstream, _, output_pieces, feed_gain_rows = exchange(
-        "fed",
-        2,
-        act_low,
-        w_down,
-        finish_fed,
-        [cotangent, hidden, gain_feed],
-        [(shard, BF), (shard, BF), ((seqs, piece, width), BF), ((8, width), F32)],
-        chips=seqs,
+
+    fed_low, slopes, act_low, w_down, upstream, _, output_pieces, feed_gain_rows = feed(
+        hidden_low, w_gate_up, down_weight.T, cotangent, hidden, gain_feed, seqs
     )
 
     own = width // ranks
     cores = [list(range(0, ranks, 2)), list(range(1, ranks, 2))]
 
-    def product_sum(*pairs):
-        other = swap(rank_products(1 - core, pairs, own), "context", 1)
-        return rank_products(core, pairs, own, other)
-
     def scatter(values):
         return lax.psum_scatter(values, "context", scatter_dimension=0, axis_index_groups=cores, tiled=True)
 
-    down_part = dot_tn(fed_low, act_low).astype(BF)
-    down_summed = lax.psum_scatter(down_part, "context", scatter_dimension=0, tiled=True)
-    output_rows = gather_rows(output_pieces)
-    gate_up_low = act_back(after(fed_low, down_part), w_down, gate_up)
-    gate_up_other = rank_products(1 - core, [(after(hidden_low, gate_up_low, *output_rows[:3]), gate_up_low)], own)
-    gate_up_other = swap(gate_up_other, "context", 1)
+    down_part = rank_sums(5, [(fed_low, act_low)], own)
+    down_summed = scatter(down_part)
+    gate_up_low = act_back(after(fed_low, down_part), w_down, slopes)
+    output_rows = [output_pieces] + [swap(output_pieces, "tensor", k) for k in (order[1:3] if columns == 4 else order[1:])]
+    gate_up_part = rank_sums(6, [(after(hidden_low, *output_rows), gate_up_low)], own)
+    gate_up_summed = scatter(gate_up_part)
+    if columns == 4:
+        passed = [swap(output_rows[1][: seqs // 2], "tensor", 2), swap(output_rows[2][seqs // 2 :], "tensor", 1)]
+        output_rows.append(jnp.concatenate(passed, axis=0))
     layer_output = in_place(jnp.stack(output_rows), s, t, BF)
-    gate_up_part = rank_products(core, [(after(hidden_low, layer_output), gate_up_low)], own, gate_up_other)
-    gate_up_summed = scatter(gate_up_part)
-    gate_up_low = after(gate_up_low, gate_up_part)
+    gate_up_low = after(gate_up_low, gate_up_part, layer_output)
     attended_low, hidden_grad, attn_gain_rows = exchange(
         "hidden_grad",
         3,
@@ -951,7 +1375,7 @@
         [(shard, F32), ((8, width), F32)],
     )
     mixed_grad = dot_nn(attended_low, w_first[:, qkv_width : 4 * head_width]).astype(BF)
-    dqkv = attend_back(qkv, mixed_heads, to_heads(mixed_grad), log, at, piece)
+    dqkv = attend_back(keep, received, mixed_heads, to_heads(mixed_grad), log, at, piece)
     dqkv_other = swap(dqkv[:, count:], "context", 1)
     inner, head_gain_rows = by_rows(
         inner_kernel,
@@ -976,8 +1400,9 @@
         ],
         [((count, 3 * head_width), BF, 0)],
     )
-    qkv_part = product_sum((rows, qkv_low), (attended_low, mixed_low))
+    qkv_part = rank_sums(7, [(rows, qkv_low), (attended_low, mixed_low)], own)
     qkv_out_summed = scatter(after(qkv_part, gate_up_summed, down_summed))
+    down_grad = down_summed.astype(F32).T
     every, width_gains, head_gains = exchange(
         "tokens_grad",
         4,
@@ -991,9 +1416,7 @@
     )
     tokens_grad = in_place(every.reshape(columns, seqs, piece, width), s, t, F32)
 
-    down_summed, gate_up_summed, qkv_out_summed = (
-        values.astype(F32) for values in (down_summed, gate_up_summed, qkv_out_summed)
-    )
+    gate_up_summed, qkv_out_summed = gate_up_summed.astype(F32), qkv_out_summed.astype(F32)
     return (
         layer_output,
         tokens_grad,
@@ -1003,7 +1426,7 @@
         qkv_out_summed[:, 3 * head_width :].T,
         gate_up_summed[:, :hidden_width],
         gate_up_summed[:, hidden_width:],
-        down_summed.T,
+        down_grad,
         head_gains[0],
         head_gains[1],
         width_gains[0],

time: 844 us -> 815 us (0.966)
  Pallas kernels: 481 us -> 564 us
  waiting for transfers between devices: 191 us -> 129 us
  matrix products: 51.4 us -> 15.5 us
    pallas_call x5, Pallas kernels: 71.6 us -> 230 us  [the longest x1 141 us: feed(): pl.pallas_call(functools.partial(feed_kernel, size, chips, tile), in_spec...]
    pallas_call x4 -> x3, Pallas kernels: 335 us -> 262 us  [exchange(): pl.pallas_call(functools.partial(exchange_kernel, size, width, depth, off...]
    all_gather x3 -> x2, waiting for transfers between devices: 86.1 us -> 30 us  [gather(): return lax.all_gather(values, 'context', axis=axis, tiled=True)]
    dot_general x3 -> x2, matrix products: 37.4 us -> 15.5 us  [dot_nn(): return jnp.dot(left, right, preferred_element_type=F32)]
    dot_general x1 -> x0, matrix products: 14 us -> none  [dot_tn(): lax.dot_general(left, right, (((0,), (0,)), ((), ())), preferred_element_...]
    unnamed x64 -> x51, local copies, waits for them, and re-layouts: 31.1 us -> 22.5 us
    ppermute x21 -> x20, waiting for transfers between devices: 105 us -> 99.1 us  [swap(): return lax.ppermute(values, axis, [(i, i ^ mask) for i in range(size)])]
    ppermute x21 -> x20, starting transfers between devices: 24.8 us -> 21 us  [swap(): return lax.ppermute(values, axis, [(i, i ^ mask) for i in range(size)])]
  transfers between devices with their start and end apart: 27 -> 25, of which waited for: 19 -> 19; matrix products, arithmetic and copies ran while one was open for 10% -> 7% of each run, Pallas kernels for 48% -> 50%
where the time goes in v2:
time: 815 us; the launch traced here: 806 us
  Pallas kernels  564 us (69%)
  waiting for transfers between devices  129 us (16%)
  local copies, waits for them, and re-layouts  40.5 us (5%)
  starting transfers between devices  21.2 us (3%)
  other arithmetic  20.8 us (3%)
  matrix products  15.5 us (2%)
  between operations  14.9 us (2%)
    pallas_call x3, Pallas kernels, exchange(): pl.pallas_call(functools.partial(exchange_kernel, size, width, depth, off...  262 us
    pallas_call x1, Pallas kernels, feed(): pl.pallas_call(functools.partial(feed_kernel, size, chips, tile), in_spec...  141 us
    ppermute x20, waiting for transfers between devices, swap(): return lax.ppermute(values, axis, [(i, i ^ mask) for i in range(size)])  99.1 us
    pallas_call x3, Pallas kernels, rank_sums(): pl.pallas_call(functools.partial(rank_sums_kernel, chips, tile, len(pairs...  72.9 us
    all_gather x2, waiting for transfers between devices, gather(): return lax.all_gather(values, 'context', axis=axis, tiled=True)  30 us
    unnamed x51, local copies, waits for them, and re-layouts  22.5 us
    pallas_call x1, Pallas kernels, attend_back(): pl.pallas_call(functools.partial(attend_back_kernel, piece, 256), grid_sp...  22.3 us
    ppermute x20, starting transfers between devices, swap(): return lax.ppermute(values, axis, [(i, i ^ mask) for i in range(size)])  21 us
  transfers between devices with their start and end apart: 25, of which 19 were waited for; matrix products, arithmetic and copies ran while one was open for 7% of the time, Pallas kernels for 50%

profile of v2, /device:TPU:9, one launch (start us, length us, event | category | flops | bytes accessed | tf_op | source)
XLA Modules:
  0.0 806.0 jit_solution(9703067563314716312)
XLA Ops:
  14.0 2.7 pad_maximum_fusion.1
  16.8 1.2 dynamic-slice_bitcast_fusion
  18.0 1.4 collective-permute-start.2
  19.3 1.1 collective-permute-start.1
  20.4 1.1 collective-permute-start
  21.9 1.7 constant_dynamic-update-slice_fusion.6
  23.6 22.7 %collective-permute-done.2 = bf16[64,2048]{1,0:T(8,128)(2,1)S(1)} collective-permute-done((bf16[64,2048]{1,0:T(8,128)(2,1)S(1)}, bf16[64,2048]{1,0:T(8,128)(2,1)S(1)}, u32[]{:S(2)}, u32[]{:S(2)}) %collective-permute-start.2) | collective-permute-done | bytes 262176 | tf_op jit(solution)/shard_map/ppermute | solution.py:37
  46.4 14.7 %collective-permute-done.1 = bf16[64,2048]{1,0:T(8,128)(2,1)S(1)} collective-permute-done((bf16[64,2048]{1,0:T(8,128)(2,1)S(1)}, bf16[64,2048]{1,0:T(8,128)(2,1)S(1)}, u32[]{:S(2)}, u32[]{:S(2)}) %collective-permute-start.1) | collective-permute-done | bytes 262176 | tf_op jit(solution)/shard_map/ppermute | solution.py:37
  61.2 1.3 collective-permute-start.3
  62.5 1.9 fusion.9
  65.4 1.2 collective-permute-start.4
  70.0 9.1 %collective-permute-done.3 = bf16[256,2048]{1,0:T(8,128)(2,1)S(1)} collective-permute-done((bf16[256,2048]{1,0:T(8,128)(2,1)S(1)}, bf16[256,2048]{1,0:T(8,128)(2,1)S(1)}, u32[]{:S(2)}, u32[]{:S(2)}) %collective-permute-start.3) | collective-permute-done | bytes 1048608 | tf_op jit(solution)/shard_map/ppermute | solution.py:37
  80.2 5.7 collective-permute-done.4
  87.0 15.5 %collective-permute-done.5 = bf16[256,2048]{1,0:T(8,128)(2,1)S(1)} collective-permute-done((bf16[256,2048]{1,0:T(8,128)(2,1)S(1)}, bf16[256,2048]{1,0:T(8,128)(2,1)S(1)}, u32[]{:S(2)}, u32[]{:S(2)}) %collective-permute-start.5) | collective-permute-done | bytes 1048608 | tf_op jit(solution)/shard_map/ppermute | solution.py:37
  103.6 10.8 %all-gather.3.cloned.1.call-done.w_ref = bf16[2048,2176]{1,0:T(8,128)(2,1)} async-done(((bf16[256,2176]{1,0:T(8,128)(2,1)}), bf16[2048,2176]{1,0:T(8,128)(2,1)}) %all-gather.3.cloned.1.call-update) | async-done | bytes 8912912 | tf_op jit(solution)/shard_map/all_gather | solution.py:1276
  114.3 10.3 %fusion.raw_ref = f32[1024,1536]{1,0:T(8,128)S(1)} fusion(bf16[1024,2048]{1,0:T(8,128)(2,1)} %constant_dynamic-update-slice_fusion.refs_0_, bf16[2048,2176]{1,0:T(8,128)(2,1)} %all-gather.3.cloned.1.call-done.w_ref), kind=kOutput, calls=%fused_computation | convolution fusion | flops 6442450944 | bytes 16777216 | tf_op jit(solution)/shard_map/dot_general | solution.py:20
  124.6 2.6 copy-done
  127.6 1.3 collective-permute-start.7
  129.6 1.2 collective-permute-start.8
  131.0 2.0 collective-permute-done.8
  134.4 6.1 turn.1
  140.5 2.8 collective-permute-start.9
  143.9 2.8 collective-permute-done.9.other_ref
  146.7 1.1 copy-done.14
  147.8 16.5 %attend.1 = (bf16[2048,256]{1,0:T(8,128)(2,1)}, f32[2,1,2048]{2,1,0:T(1,128)}) custom-call(s32[32]{0:T(128)} %add_multiply_fusion.1.at_ref, bf16[3,1024,256]{2,1,0:T(8,128)(2,1)} %get-tuple-element.40.own_ref, bf16[3,1024,256]{2,1,0:T(8,128)(2,1)} %copy-done.14), custom_call_target="tpu_custom_call" | custom-call | flops 4294967296 | bytes 4194304 | tf_op jit(solution)/shard_map/attend/pallas_call | solution.py:1154
  164.4 1.2 slice.151
  165.8 1.4 copy.53
  167.2 2.4 convert_reduce_fusion
  170.8 78.3 %attended.1 = (bf16[1024,2048]{1,0:T(8,128)(2,1)}, f32[256,2048]{1,0:T(8,128)}, f32[256,2048]{1,0:T(8,128)}) custom-call(bf16[1024,512]{1,0:T(8,128)(2,1)} %pad_maximum_fusion.3.a_ref.refs_3_, bf16[2048,2176]{1,0:T(8,128)(2,1)} %all-gather.3.cloned.1.call-done.w_ref, bf16[256,2048]{1,0:T(8,128)(2,1)} %copy-done.4, f32[1,2048]{1,0:T(1,128)} %bitcast.84), custom_call_target="tpu_custom_call" | custom-call | flops 2147483648 | bytes 240000000 | tf_op jit(solution)/shard_map/attended/pallas_call | solution.py:452
  249.1 19.2 %all-gather.5.cloned.1.call-done.refs_1_.w_ref = bf16[2048,4096]{1,0:T(8,128)(2,1)} async-done(((bf16[256,4096]{1,0:T(8,128)(2,1)}), bf16[2048,4096]{1,0:T(8,128)(2,1)}) %all-gather.5.cloned.1.call-update) | async-done | bytes 16777232 | tf_op jit(solution)/shard_map/all_gather | solution.py:1276
  268.3 141.1 %feed.1 = (bf16[1024,2048]{1,0:T(8,128)(2,1)}, bf16[1024,4096]{1,0:T(8,128)(2,1)}, bf16[1024,2048]{1,0:T(8,128)(2,1)}, bf16[2048,2048]{1,0:T(8,128)(2,1)}, bf16[...) custom-call(bf16[1024,2048]{1,0:T(8,128)(2,1)} %get-tuple-element.51.refs_0_, ...), custom_call_target="tpu_custom_call" | custom-call | flops 25769803776 | bytes 400000000 | tf_op jit(solution)/shard_map/feed/pallas_call | solution.py:862
  409.4 18.9 %rank_sums.3 = bf16[1024,2048]{1,0:T(8,128)(2,1)} custom-call(bf16[1024,2048]{1,0:T(8,128)(2,1)} %get-tuple-element.48.refs_0_.grad_ref, bf16[1024,2048]{1,0:T(8,128)(2,1)} %get-tuple-element.47.refs_1_), custom_call_target="tpu_custom_call" | custom-call | flops 8589934592 | bytes 60000000 | tf_op jit(solution)/shard_map/rank_sums/pallas_call | solution.py:1075
  428.4 1.1 copy-done.10
  430.7 16.4 %act_back.1.refs_1_.a_ref = bf16[1024,4096]{1,0:T(8,128)(2,1)} custom-call(bf16[1024,2048]{1,0:T(8,128)(2,1)} %get-tuple-element.48.refs_0_.grad_ref, bf16[2048,2048]{1,0:T(8,128)(2,1)} %get-tuple-element.49.w_ref, bf16[1024,4096]{1,0:T(8,128)(2,1)} %get-tuple-element.50.slopes_ref), custom_call_target="tpu_custom_call" | custom-call | flops 8589934592 | bytes 40000000 | tf_op jit(solution)/shard_map/act_back/pallas_call | solution.py:991
  447.1 7.0 collective-permute-done.12
  455.1 32.9 %rank_sums.4 = bf16[1024,4096]{1,0:T(8,128)(2,1)} custom-call(bf16[1024,2048]{1,0:T(8,128)(2,1)} %get-tuple-element.51.refs_0_, bf16[1024,4096]{1,0:T(8,128)(2,1)} %act_back.1.refs_1_.a_ref), custom_call_target="tpu_custom_call" | custom-call | flops 17179869184 | bytes 60000000 | tf_op jit(solution)/shard_map/rank_sums/pallas_call | solution.py:1075
  490.2 1.2 collective-permute-start.13
  492.0 10.9 %collective-permute-done.14 = bf16[2,64,2048]{2,1,0:T(8,128)(2,1)} collective-permute-done((bf16[2,64,2048]{2,1,0:T(8,128)(2,1)}, bf16[2,64,2048]{2,1,0:T(8,128)(2,1)}, u32[]{:S(2)}, u32[]{:S(2)}) %collective-permute-start.14) | collective-permute-done | bytes 524320 | tf_op jit(solution)/shard_map/ppermute | solution.py:37
  502.9 1.1 collective-permute-done.13
  504.0 1.3 maximum_bitcast_fusion
  505.3 2.6 pad_maximum_fusion.in_ref
  507.9 5.4 place_rows.2
  513.3 83.4 %hidden_grad.1 = (bf16[1024,2048]{1,0:T(8,128)(2,1)}, f32[256,2048]{1,0:T(8,128)}, f32[8,2048]{1,0:T(8,128)}) custom-call(bf16[1024,4096]{1,0:T(8,128)(2,1)} %act_back.1.refs_1_.a_ref, bf16[2048,4096]{1,0:T(8,128)(2,1)} %all-gather.5.cloned.1.call-done.refs_1_.w_ref, f32[256,2048]{1,0:T(8,128)} %get-tuple-element.53.refs_0_, ...), custom_call_target="tpu_custom_call" | custom-call | flops 17179869184 | bytes 240000000 | tf_op jit(solution)/shard_map/hidden_grad/pallas_call | solution.py:452
  596.7 5.2 fusion.6
  602.0 3.1 collective-permute-start.15
  605.1 1.5 collective-permute-done.15
  607.7 22.3 %attend_back.1.own_ref = bf16[3,2048,256]{2,1,0:T(8,128)(2,1)} custom-call(s32[32]{0:T(128)} %add_multiply_fusion.1.at_ref, bf16[3,1024,256]{2,1,0:T(8,128)(2,1)} %get-tuple-element.40.own_ref, bf16[3,1024,256]{2,1,0:T(8,128)(2,1)} %copy-done.14, bf16[2048,256]{1,0:T(8,128)(2,1)} %get-tuple-element.42.out_ref, bf16[2048,256]{1,0:T(8,128)(2,1)} %pad_maximum_fusion.4.grad_ref, ...), custom_call_target="tpu_custom_call" | custom-call | flops 10737418240 | bytes 8388608 | tf_op jit(solution)/shard_map/attend_back/pallas_call | solution.py:1217
  629.9 1.6 slice.197
  631.9 3.0 collective-permute-done.16.other_ref
  635.0 1.1 copy-done.3
  636.1 8.1 inner.1
  646.7 1.1 collective-permute-start.17
  648.0 1.3 collective-permute-done.19
  650.8 6.7 raw_grad.1.refs_2_.a_ref
  657.5 21.1 %rank_sums.5 = bf16[1024,2048]{1,0:T(8,128)(2,1)} custom-call(bf16[1024,2048]{1,0:T(8,128)(2,1)} %constant_dynamic-update-slice_fusion.refs_0_, bf16[1024,2048]{1,0:T(8,128)(2,1)} %get-tuple-element.55.refs_1_, bf16[1024,1536]{1,0:T(8,128)(2,1)} %raw_grad.1.refs_2_.a_ref, bf16[1024,512]{1,0:T(8,128)(2,1)} %pad_maximum_fusion.3.a_ref.refs_3_), custom_call_target="tpu_custom_call" | custom-call | flops 8589934592 | bytes 60000000 | tf_op jit(solution)/shard_map/rank_sums/pallas_call | solution.py:1075
  678.6 100.0 %tokens_grad.1 = (bf16[1024,2048]{1,0:T(8,128)(2,1)}, f32[8,256]{1,0:T(8,128)}, f32[8,512]{1,0:T(8,128)}) custom-call(bf16[1024,1536]{1,0:T(8,128)(2,1)} %raw_grad.1.refs_2_.a_ref, bf16[2048,2176]{1,0:T(8,128)(2,1)} %all-gather.3.cloned.1.call-done.w_ref, f32[256,2048]{1,0:T(8,128)} %get-tuple-element.59.refs_0_, f32[8,2048]{1,0:T(8,128)} %get-tuple-element.60.refs_1_, ...), custom_call_target="tpu_custom_call" | custom-call | flops 6442450944 | bytes 240000000 | tf_op jit(solution)/shard_map/tokens_grad/pallas_call | solution.py:452
  778.6 6.8 place_rows.3
  785.4 1.4 fusion.30
  786.8 1.4 fusion.29
  788.2 1.6 convert_bitcast_fusion
  789.8 2.9 copy.56
  792.6 2.5 fusion.26
  795.2 1.5 convert_element_type.60
  797.8 1.2 fusion.27
  (132 shorter events, 31.1 us)
Async XLA Ops:
  7.2 6.8 copy-start.9
  7.2 107.1 %all-gather.3.cloned.1.call-start = ((), (), s32[]{:S(2)}) async-start(), calls=%async_computation.3 | async-start | bytes 10027008 | tf_op jit(solution)/shard_map/all_gather | solution.py:1276
  12.9 1.0 copy-start.5
  13.9 7.9 copy-start.13
  13.9 254.4 %all-gather.5.cloned.1.call-start = ((), (), s32[]{:S(2)}) async-start(), calls=%async_computation.4 | async-start | bytes 18874368 | tf_op jit(solution)/shard_map/all_gather | solution.py:1276
  16.7 47.7 %copy-start.11 = (bf16[512]{0:T(512)(128)(2,1)S(1)}, bf16[512]{0:T(512)(128)(2,1)}, u32[]{:S(2)}) copy-start(bf16[512]{0:T(512)(128)(2,1)} %param.23) | copy-start | bytes 3076
  16.7 47.7 %copy-start.12 = (bf16[512]{0:T(512)(128)(2,1)S(1)}, bf16[512]{0:T(512)(128)(2,1)}, u32[]{:S(2)}) copy-start(bf16[512]{0:T(512)(128)(2,1)} %param.24) | copy-start | bytes 3076
  16.7 661.8 %reduce-scatter.6.cloned.1.call-start = ((), (), s32[]{:S(2)}) async-start(), calls=%async_computation.6 | async-start | bytes 5242880 | tf_op jit(solution)/shard_map/reduce_scatter | solution.py:1355
  18.0 28.4 %collective-permute-start.2 = (bf16[64,2048]{1,0:T(8,128)(2,1)S(1)}, bf16[64,2048]{1,0:T(8,128)(2,1)S(1)}, u32[]{:S(2)}, u32[]{:S(2)}) collective-permute-start(bf16[64,2048]{1,0:T(8,128)(2,1)S(1)} %get-tuple-element.125), channel_id=1, source_target_pairs={{0,24},{4,28},{8,16},{12,20},{16,8},{20,12},{24,0},{28,4},{1,25},{... | collective-permute-start | bytes 786440 | tf_op jit(solution)/shard_map/ppermute | solution.py:37
  19.3 41.7 %collective-permute-start.1 = (bf16[64,2048]{1,0:T(8,128)(2,1)S(1)}, bf16[64,2048]{1,0:T(8,128)(2,1)S(1)}, u32[]{:S(2)}, u32[]{:S(2)}) collective-permute-start(bf16[64,2048]{1,0:T(8,128)(2,1)S(1)} %get-tuple-element.126), channel_id=1, source_target_pairs={{0,16},{4,20},{8,24},{12,28},{16,0},{20,4},{24,8},{28,12},{1,17},{... | collective-permute-start | bytes 786440 | tf_op jit(solution)/shard_map/ppermute | solution.py:37
  20.4 40.6 %collective-permute-start = (bf16[64,2048]{1,0:T(8,128)(2,1)S(1)}, bf16[64,2048]{1,0:T(8,128)(2,1)S(1)}, u32[]{:S(2)}, u32[]{:S(2)}) collective-permute-start(bf16[64,2048]{1,0:T(8,128)(2,1)S(1)} %get-tuple-element.127), channel_id=1, source_target_pairs={{0,8},{4,12},{8,0},{12,4},{16,24},{20,28},{24,16},{28,20},{1,9},{5... | collective-permute-start | bytes 786440 | tf_op jit(solution)/shard_map/ppermute | solution.py:37
  61.2 25.8 %copy-start.4 = (bf16[256,2048]{1,0:T(8,128)(2,1)}, bf16[256,2048]{1,0:T(8,128)(2,1)S(1)}, u32[]{:S(2)}) copy-start(bf16[256,2048]{1,0:T(8,128)(2,1)S(1)} %pad_maximum_fusion.2.refs_0_) | copy-start | bytes 3145732
  61.2 18.0 %collective-permute-start.3 = (bf16[256,2048]{1,0:T(8,128)(2,1)S(1)}, bf16[256,2048]{1,0:T(8,128)(2,1)S(1)}, u32[]{:S(2)}, u32[]{:S(2)}) collective-permute-start(bf16[256,2048]{1,0:T(8,128)(2,1)S(1)} %pad_maximum_fusion.2.refs_0_), channel_id=1, source_target_pairs={{0,1},{1,0},{2,3},{3,2},{4,5},{5,4},{6,7},{7,6},{8,9},{9,8},{10,11... | collective-permute-start | bytes 3145736 | tf_op jit(solution)/shard_map/ppermute | solution.py:37
  65.4 20.5 %collective-permute-start.4 = (bf16[256,2048]{1,0:T(8,128)(2,1)S(1)}, bf16[256,2048]{1,0:T(8,128)(2,1)S(1)}, u32[]{:S(2)}, u32[]{:S(2)}) collective-permute-start(bf16[256,2048]{1,0:T(8,128)(2,1)S(1)} %pad_maximum_fusion.2.refs_0_), channel_id=1, source_target_pairs={{0,2},{1,3},{2,0},{3,1},{4,6},{5,7},{6,4},{7,5},{8,10},{9,11},{10,... | collective-permute-start | bytes 3145736 | tf_op jit(solution)/shard_map/ppermute | solution.py:37
  67.6 34.9 %collective-permute-start.5 = (bf16[256,2048]{1,0:T(8,128)(2,1)S(1)}, bf16[256,2048]{1,0:T(8,128)(2,1)S(1)}, u32[]{:S(2)}, u32[]{:S(2)}) collective-permute-start(bf16[256,2048]{1,0:T(8,128)(2,1)S(1)} %pad_maximum_fusion.2.refs_0_), channel_id=1, source_target_pairs={{0,3},{1,2},{2,1},{3,0},{4,7},{5,6},{6,5},{7,4},{8,11},{9,10},{10,... | collective-permute-start | bytes 3145736 | tf_op jit(solution)/shard_map/ppermute | solution.py:37
  124.6 2.6 copy-start
  127.6 3.3 collective-permute-start.7
  129.6 3.4 collective-permute-start.8
  130.7 2.5 collective-permute-start.6
  140.5 6.2 collective-permute-start.9
  146.7 1.1 copy-start.14
  147.8 18.0 %copy-start.8 = (bf16[2048,256]{1,0:T(8,128)(2,1)S(1)}, bf16[2048,256]{1,0:T(8,128)(2,1)}, u32[]{:S(2)}) copy-start(bf16[2048,256]{1,0:T(8,128)(2,1)} %param.22) | copy-start | bytes 3145732
  164.4 5.3 copy-start.7
  165.5 4.1 collective-permute-start.10
  428.4 1.2 copy-start.10
  428.4 250.2 %reduce-scatter.4.cloned.1.call-start = ((), (), s32[]{:S(2)}) async-start(), calls=%async_computation.5 | async-start | bytes 10485760 | tf_op jit(solution)/shard_map/reduce_scatter | solution.py:1355
  429.6 24.5 %collective-permute-start.12 = (bf16[4,64,2048]{2,1,0:T(8,128)(2,1)S(1)}, bf16[4,64,2048]{2,1,0:T(8,128)(2,1)S(1)}, u32[]{:S(2)}, u32[]{:S(2)}) collective-permute-start(bf16[4,64,2048]{2,1,0:T(8,128)(2,1)S(1)} %copy-done.10), channel_id=1, source_target_pairs={{0,2},{1,3},{2,0},{3,1},{4,6},{5,7},{6,4},{7,5},{8,10},{9,11},{10,... | collective-permute-start | bytes 3145736 | tf_op jit(solution)/shard_map/ppermute | solution.py:37
  430.4 24.7 %collective-permute-start.11 = (bf16[4,64,2048]{2,1,0:T(8,128)(2,1)S(1)}, bf16[4,64,2048]{2,1,0:T(8,128)(2,1)S(1)}, u32[]{:S(2)}, u32[]{:S(2)}) collective-permute-start(bf16[4,64,2048]{2,1,0:T(8,128)(2,1)S(1)} %copy-done.10), channel_id=1, source_target_pairs={{0,1},{1,0},{2,3},{3,2},{4,5},{5,4},{6,7},{7,6},{8,9},{9,8},{10,11... | collective-permute-start | bytes 3145736 | tf_op jit(solution)/shard_map/ppermute | solution.py:37
  488.1 307.1 %reduce-scatter.8.cloned.1.call-start = ((), (), s32[]{:S(2)}) async-start(), calls=%async_computation.7 | async-start | bytes 5242880 | tf_op jit(solution)/shard_map/reduce_scatter | solution.py:1355
  489.0 13.9 %collective-permute-start.14 = (bf16[2,64,2048]{2,1,0:T(8,128)(2,1)}, bf16[2,64,2048]{2,1,0:T(8,128)(2,1)}, u32[]{:S(2)}, u32[]{:S(2)}) collective-permute-start(bf16[2,64,2048]{2,1,0:T(8,128)(2,1)} %slice.195), channel_id=1, source_target_pairs={{0,1},{1,0},{2,3},{3,2},{4,5},{5,4},{6,7},{7,6},{8,9},{9,8},{10,11... | collective-permute-start | bytes 1572872 | tf_op jit(solution)/shard_map/ppermute | solution.py:37
  490.2 13.8 %collective-permute-start.13 = (bf16[2,64,2048]{2,1,0:T(8,128)(2,1)}, bf16[2,64,2048]{2,1,0:T(8,128)(2,1)}, u32[]{:S(2)}, u32[]{:S(2)}) collective-permute-start(bf16[2,64,2048]{2,1,0:T(8,128)(2,1)} %slice.194), channel_id=1, source_target_pairs={{0,2},{1,3},{2,0},{3,1},{4,6},{5,7},{6,4},{7,5},{8,10},{9,11},{10,... | collective-permute-start | bytes 1572872 | tf_op jit(solution)/shard_map/ppermute | solution.py:37
  602.0 4.6 collective-permute-start.15
  631.5 3.5 collective-permute-start.16
  635.0 1.1 copy-start.3
  645.1 3.0 collective-permute-start.18
  646.0 3.4 collective-permute-start.19
  646.7 2.9 collective-permute-start.17
  778.6 9.6 %copy-start.6 = (bf16[256,2048]{1,0:T(8,128)(2,1)S(1)}, bf16[256,2048]{1,0:T(8,128)(2,1)}, u32[]{:S(2)}) copy-start(bf16[256,2048]{1,0:T(8,128)(2,1)} %reduce-scatter.6.cloned.1.call-done) | copy-start | bytes 3145732
  785.4 7.3 copy-start.1
  795.2 2.6 copy-start.2
Sparse Core Ops, SparseCore 0:
  14.0 100.2 all-gather.2
  116.5 151.7 all-gather.4
  428.5 82.4 reduce-scatter.5
  513.4 144.6 reduce-scatter.3
  678.7 110.1 reduce-scatter.7

commit v3 on v2

--- a/solution.py
+++ b/solution.py
@@ -24,10 +24,6 @@
     return lax.dot_general(left, right, (((1,), (1,)), ((), ())), preferred_element_type=F32)
 
 
-def dot_tn(left, right):
-    return lax.dot_general(left, right, (((0,), (0,)), ((), ())), preferred_element_type=F32)
-
-
 def after(values, *others):
     return lax.optimization_barrier((values, *others))[0]
 
@@ -35,17 +31,6 @@
 def swap(values, axis, mask):
     size = lax.axis_size(axis)
     return lax.ppermute(values, axis, [(i, i ^ mask) for i in range(size)])
-
-
-def gather_rows(shard):
-    return [shard] + [swap(shard, "tensor", k) for k in range(1, lax.axis_size("tensor"))]
-
-
-def scatter_rows(parts):
-    total = parts[0]
-    for k in range(1, len(parts)):
-        total = total + swap(parts[k].astype(BF), "tensor", k).astype(F32)
-    return total
 
 
 def sum_over_tensor(values):
@@ -58,40 +43,32 @@
     return total.reshape(values.shape)
 
 
-def to_sequences(values, s, t):
-    seqs, local_len, width = values.shape
-    size = lax.axis_size("tensor")
-    mine = lax.dynamic_index_in_dim(values.reshape(seqs, size, local_len // size, width), t, 1, keepdims=False)
-    pieces = []
-    for j in range(seqs):
-        piece = lax.dynamic_index_in_dim(mine, s ^ j, 0, keepdims=False)
-        pieces.append(piece if j == 0 else swap(piece, "context", 2 * j))
-    return jnp.concatenate(pieces, axis=0)
-
-
-def place_kernel(at_ref, in_ref, out_ref):
+def place_kernel(at_ref, *refs):
+    out_ref = refs[-1]
     for a in range(out_ref.shape[0]):
-        out_ref[a, 0] = in_ref[0, a ^ at_ref[0]].astype(out_ref.dtype)
-
-
-def to_ranks(shard, seqs):
-    pieces = shard.reshape(seqs, -1, shard.shape[1])
-    return jnp.stack([pieces[0]] + [swap(pieces[j], "context", 2 * j) for j in range(1, seqs)], axis=0)
-
-
-def in_place(every, s, t, dtype):
-    size, seqs, piece, width = every.shape
+        at, base, values = a ^ at_ref[0], 0, None
+        for ref in refs[:-1]:
+            count = ref.shape[1]
+            part = ref[0, jnp.clip(at - base, 0, count - 1)]
+            values = part if values is None else jnp.where(at >= base, part, values)
+            base += count
+        out_ref[a, 0] = values.astype(out_ref.dtype)
+
+
+def in_place(parts, s, t, dtype):
+    size, _, piece, width = parts[0].shape
+    seqs = sum(part.shape[1] for part in parts)
     full = pl.pallas_call(
         place_kernel,
         grid_spec=pltpu.PrefetchScalarGridSpec(
             num_scalar_prefetch=1,
             grid=(size,),
-            in_specs=[pl.BlockSpec((1, seqs, piece, width), lambda b, at: (b ^ at[1], 0, 0, 0))],
+            in_specs=[pl.BlockSpec((1, *part.shape[1:]), lambda b, at: (b ^ at[1], 0, 0, 0)) for part in parts],
             out_specs=pl.BlockSpec((seqs, 1, piece, width), lambda b, at: (0, b, 0, 0)),
         ),
         out_shape=jax.ShapeDtypeStruct((seqs, size, piece, width), dtype),
         name="place_rows",
-    )(jnp.stack([s, t]).astype(jnp.int32), every)
+    )(jnp.stack([s, t]).astype(jnp.int32), *parts)
     return full.reshape(seqs, size * piece, width)
 
 
@@ -134,7 +111,7 @@
 
     order = [3, 1, 2, 0] if size == 4 else [*range(1, size), 0]
     tiles = width // tile
-    parts = 2 if last and size == 4 else 1
+    parts = tiles if size == 4 else 1
     across = width // parts
     a_copy(order[0]).start()
     for j in range(tiles):
@@ -286,16 +263,12 @@
     if size == 4:
         groups = [sums_of(part) for part in range(parts)]
         copies = sum(groups, [])
-        copies[0].start()
-        copies[1].start()
-        product(1)
-        copies[2].start()
-        product(2)
-        copies[3].start()
-        for part in range(1, parts):
-            product(3, first=True, part=part)
-            product(1, part=part)
-            product(2, part=part)
+        for part, group in enumerate(groups):
+            for k, ready in ((3, group[:2]), (1, group[2:3]), (2, group[3:4])):
+                if k != 3 or part:
+                    product(k, first=k == 3, part=part)
+                for copy in [] if last and part else ready:
+                    copy.start()
         for part, group in enumerate(groups):
             at = columns_of_part(part)
             group[0].wait_recv()
@@ -304,13 +277,13 @@
             group[1].wait_recv()
             add(0, 2, half, at)
             group[5].start()
-            for copy in groups[part + 1][:4] if part + 1 < parts else []:
+            for copy in groups[part + 1][:4] if last and part + 1 < parts else []:
                 copy.start()
             product(0, part=part)
-            if part + 1 < parts:
+            if last and part + 1 < parts:
                 finish_last(part, group)
-        if not last:
-            for copy in copies[2:]:
+        for group in [] if last else groups:
+            for copy in group[2:]:
                 copy.wait_recv()
         used = 2
     else:
@@ -369,19 +342,23 @@
             else:
                 going_home[part][j].wait_recv()
 
+    out_parts = parts if last else 1
     make_ready = came_home if last else finish_rows
     then = [own] if last else [own, *going_home[0]]
     if size == 4:
 
+        def out_columns(part):
+            return pl.ds(part * (width // out_parts), width // out_parts)
+
         def chunk(k, side, part):
-            return every.at[pl.ds(k * rows + side * half, half), columns_of_part(part)]
+            return every.at[pl.ds(k * rows + side * half, half), out_columns(part)]
 
         def share(k, side, part):
-            source = shared.at[pl.ds(side * half, half), columns_of_part(part)]
+            source = shared.at[pl.ds(side * half, half), out_columns(part)]
             return send(6 * part + 2 * k + side, source, chunk(k + 1, side, part), k + 1, gather)
 
         groups = []
-        for part in range(parts):
+        for part in range(out_parts):
             shares = [share(k, side, part) for k in (0, 1) for side in (0, 1)]
             passed = [
                 send(6 * part + 4, chunk(1, 0, part), chunk(3, 0, part), 2, gather),
@@ -395,7 +372,7 @@
             make_ready(half, half, part)
             group[3].start()
             group[1].start()
-            if part == parts - 1:
+            if part == out_parts - 1:
                 for copy in then:
                     copy.start()
             group[0].wait_recv()
@@ -430,7 +407,7 @@
     size = lax.axis_size("tensor")
     rows, width, depth = a.shape[0] // size, w.shape[0], a.shape[1]
     tile = min(512, width)
-    parts = 2 if last and size == 4 else 1
+    parts = width // tile if size == 4 else 1
     links = 6 * parts if size == 4 else size - 1
     whole = pl.BlockSpec(memory_space=pltpu.VMEM)
     anywhere = pl.BlockSpec(memory_space=pl.ANY)
@@ -489,15 +466,6 @@
     return hidden
 
 
-def finish_fed(at, fed, ins, outs):
-    hidden, gain = ins[1:]
-    factor = norm_factor(fed)
-    outs[1][at, :] = (hidden[at, :] + fed * factor * gain[...]).astype(BF)
-    grad, gain_rows = norm_back(fed, factor, gain[...], outs[0][at, :].astype(F32))
-    add_rows(outs[3], gain_rows)
-    return grad
-
-
 def finish_hidden_grad(at, summed, ins, outs):
     attended, cotangent, gain = ins
     hidden_grad = cotangent[at, :].astype(F32) + summed
@@ -638,7 +606,7 @@
 
 class Gather:
     def __init__(self, size, t, shared, every, sems, own_sem):
-        rows = shared.shape[0]
+        rows = every.shape[0] // size
         half = rows // 2
         self.size = size
         self.own = pltpu.make_async_copy(shared, every.at[pl.ds(0, rows), :], own_sem)
@@ -683,6 +651,90 @@
 
 def links_of(size):
     return 6 if size == 4 else size - 1
+
+
+def start_kernel(size, chips, offsets, n_pair, *refs):
+    tokens_ref, firsts, pair, refs = refs[0], refs[1 : 1 + len(offsets)], refs[1 + len(offsets) :][:n_pair], refs[1 + len(offsets) + n_pair :]
+    every, whole, both, shard = refs[:4]
+    line_refs, gather, coming, own_sem, keep_sem = refs[4:10], refs[10:12], refs[12:14], refs[14], refs[15]
+    t, c = lax.axis_index("tensor"), lax.axis_index("context")
+    s = c // 2
+    rows = shard.shape[0]
+    piece = rows // chips
+    own = firsts[0].shape[0]
+    line = Line(chips, own, whole, line_refs[0:2], line_refs[2:4], line_refs[4:6])
+    wait_others = meet(t, c, size, [1, *range(2, 2 * chips, 2)])
+    kept = [
+        pltpu.make_async_copy(first, whole.at[line.rows(s), pl.ds(offset, first.shape[1])], keep_sem.at[i])
+        for i, (first, offset) in enumerate(zip(firsts, offsets))
+    ]
+    across = pair[0].shape[1]
+    kept += [
+        pltpu.make_async_copy(part, both.at[:, pl.ds(i * across, across)], keep_sem.at[len(offsets) + i]) for i, part in enumerate(pair)
+    ]
+    for copy in kept:
+        copy.start()
+    arrivals = [
+        (tokens_ref.at[flip(s, j), pl.ds(pl.multiple_of(t * piece, piece), piece), :], shard.at[pl.ds(j * piece, piece), :])
+        for j in range(chips)
+    ]
+    first = pltpu.make_async_copy(*arrivals[0], coming[0].at[0])
+    others = [remote(*arrivals[j], coming, j, {"context": flip(c, 2 * j)}) for j in range(1, chips)]
+    wait_others()
+    for copy in [first, *others]:
+        copy.start()
+    for copy in kept:
+        copy.wait()
+    line.begin()
+    first.wait()
+    for copy in others:
+        copy.wait_recv()
+    share = Gather(size, t, shard, every, gather, own_sem)
+    share.start(0)
+    share.start(1)
+    line.advance(0)
+    share.pass_on()
+    for k in range(1, chips - 1):
+        line.advance(k)
+    share.wait()
+    for k in range(-1, chips - 1):
+        line.other_core(k)
+    line.end()
+    share.end()
+    for copy in others:
+        copy.wait_send()
+
+
+def start(tokens, firsts, pair, chips):
+    size = lax.axis_size("tensor")
+    seqs, local_len, width = tokens.shape
+    rows = seqs * local_len // size
+    own = firsts[0].shape[0]
+    offsets, across = [], 0
+    for first in firsts:
+        offsets.append(across)
+        across += first.shape[1]
+    dma = pltpu.SemaphoreType.DMA
+    anywhere = pl.BlockSpec(memory_space=pl.ANY)
+    shape = jax.ShapeDtypeStruct
+    return pl.pallas_call(
+        functools.partial(start_kernel, size, chips, offsets, len(pair)),
+        in_specs=[anywhere] * (1 + len(firsts) + len(pair)),
+        out_specs=[anywhere] + [pl.BlockSpec(memory_space=pltpu.VMEM)] * 3,
+        out_shape=[
+            shape((size * rows, width), BF),
+            shape((2 * chips * own, across), BF),
+            shape((own, sum(part.shape[1] for part in pair)), BF),
+            shape((rows, width), BF),
+        ],
+        scratch_shapes=line_sems(chips)
+        + [dma((links_of(size),))] * 2
+        + [dma((chips,))] * 2
+        + [dma, dma((len(firsts) + len(pair),))],
+        compiler_params=pltpu.CompilerParams(vmem_limit_bytes=VMEM_LIMIT, collective_id=8, has_side_effects=True),
+        cost_estimate=pl.CostEstimate(flops=0, bytes_accessed=300_000_000, transcendentals=0),
+        name="start",
+    )(tokens, *firsts, *pair)
 
 
 def feed_kernel(size, chips, tile, *refs):
@@ -1004,12 +1056,15 @@
     )(fed_low, w_down, slopes)
 
 
-def rank_sums_kernel(chips, tile, count, *refs):
-    lefts, rights, out_ref = refs[:count], refs[count : 2 * count], refs[2 * count]
-    refs = refs[2 * count + 1 :]
+def rank_sums_kernel(chips, size, tile, count, carries, *refs):
+    lefts, rights, refs = refs[:count], refs[count : 2 * count], refs[2 * count :]
+    if carries:
+        carried_ref, out_ref, every_ref, *refs = refs
+    else:
+        out_ref, *refs = refs
     left_bufs, right_bufs = refs[:count], refs[count : 2 * count]
-    passed, got, out, left_sem, right_sem, out_sem, sent_sem, got_sem = refs[2 * count :]
-    c = lax.axis_index("context")
+    passed, got, out, left_sem, right_sem, out_sem, sent_sem, got_sem = refs[2 * count : 2 * count + 8]
+    t, c = lax.axis_index("tensor"), lax.axis_index("context")
     core = c % 2
     own = out.shape[1]
     blocks = [(j, core_at) for core_at in (1, 0) for j in range(chips)]
@@ -1026,15 +1081,20 @@
         at = pl.ds(pl.multiple_of(n * tile, tile), tile)
         return pltpu.make_async_copy(rights[i].at[:, at], right_bufs[i].at[:, at], right_sem.at[i, n])
 
-    barrier = pltpu.get_barrier_semaphore()
-    pl.semaphore_signal(barrier, inc=1, device_id={"context": flip(c, 1)}, device_id_type=MESH)
+    wait_others = meet(t, c, size if carries else 1, [1])
     for i in range(count):
         left_copy(i, *blocks[0]).start()
         for n in range(tiles[i]):
             right_copy(i, n).start()
         for block in blocks[1:]:
             left_copy(i, *block).start()
-    pl.semaphore_wait(barrier, 1)
+    wait_others()
+    if carries:
+        sent_out, got_out, own_sem = refs[2 * count + 8 :]
+        part = carried_ref.at[pl.ds(carries[0], carries[1]), :]
+        share = Gather(size, t, part, every_ref, (sent_out, got_out), own_sem)
+        share.start(0)
+        share.start(1)
     sends = [remote(passed.at[j], got.at[j], (sent_sem, got_sem), j, {"context": flip(c, 1)}) for j in range(chips)]
     writes = [pltpu.make_async_copy(out.at[j], out_ref.at[pl.ds(j * own, own), :], out_sem.at[j]) for j in range(chips)]
     for at, (j, core_at) in enumerate(blocks):
@@ -1059,32 +1119,41 @@
             lax.fori_loop(0, tiles[i], step, 0)
             base += tiles[i] * tile
         (sends if core_at else writes)[j].start()
+        if carries and at == len(blocks) - 3:
+            share.pass_on()
     for j in range(chips):
         sends[j].wait_send()
         writes[j].wait()
-
-
-def rank_sums(number, pairs, own):
+    if carries:
+        share.wait()
+        share.end()
+
+
+def rank_sums(number, pairs, own, carried=None):
+    size = lax.axis_size("tensor")
     lefts, rights = [left for left, _ in pairs], [right for _, right in pairs]
     count, width = lefts[0].shape
     chips = width // (2 * own)
     across = sum(right.shape[1] for right in rights)
     tile = min(512, *[right.shape[1] for right in rights])
     most = max(right.shape[1] for right in rights) // tile
+    more = [] if carried is None else [carried[0]]
     dma = pltpu.SemaphoreType.DMA
     return pl.pallas_call(
-        functools.partial(rank_sums_kernel, chips, tile, len(pairs)),
-        in_specs=[pl.BlockSpec(memory_space=pl.ANY)] * (2 * len(pairs)),
-        out_specs=pl.BlockSpec(memory_space=pl.ANY),
-        out_shape=jax.ShapeDtypeStruct((chips * own, across), BF),
+        functools.partial(rank_sums_kernel, chips, size, tile, len(pairs), carried and carried[1:]),
+        in_specs=[pl.BlockSpec(memory_space=pl.ANY)] * (2 * len(pairs) + len(more)),
+        out_specs=[pl.BlockSpec(memory_space=pl.ANY)] * (1 + len(more)),
+        out_shape=[jax.ShapeDtypeStruct((chips * own, across), BF)]
+        + [jax.ShapeDtypeStruct((size * carried[2], rows.shape[1]), BF) for rows in more],
         scratch_shapes=[pltpu.VMEM((2 * chips, count, own), BF)] * len(pairs)
         + [pltpu.VMEM(right.shape, BF) for right in rights]
         + [pltpu.VMEM((chips, own, across), BF)] * 3
-        + [dma((len(pairs), 2 * chips)), dma((len(pairs), most)), dma((chips,)), dma((chips,)), dma((chips,))],
+        + [dma((len(pairs), 2 * chips)), dma((len(pairs), most)), dma((chips,)), dma((chips,)), dma((chips,))]
+        + [dma((links_of(size),)), dma((links_of(size),)), dma] * len(more),
         compiler_params=pltpu.CompilerParams(vmem_limit_bytes=VMEM_LIMIT, collective_id=number, has_side_effects=True),
         cost_estimate=pl.CostEstimate(flops=2 * count * width * across, bytes_accessed=60_000_000, transcendentals=0),
         name="rank_sums",
-    )(*lefts, *rights)
+    )(*lefts, *rights, *more)
 
 
 def columns_of(*values):
@@ -1272,18 +1341,14 @@
     half_width = head_width // 2
     hidden_width = gate_weight.shape[1]
 
-    def gather(values, axis):
-        return lax.all_gather(values, "context", axis=axis, tiled=True)
-
     gain_columns = jnp.stack([attention_gain, forward_gain], axis=1)
     gain_columns = jnp.pad(gain_columns, ((0, 0), (0, HD - 2)))
-    w_first = gather(jnp.concatenate([query_weight, key_weight, value_weight, output_weight.T, gain_columns], axis=1), 0)
+    firsts = [query_weight, key_weight, value_weight, output_weight.T, gain_columns]
+    rows, w_first, gate_up_shard, row_shard = start(tokens, firsts, [gate_weight, up_weight], seqs)
     qkv_width = 3 * head_width
     gains = w_first[:, 4 * head_width :]
     gain_attn, gain_feed = gains[:, 0].astype(F32)[None], gains[:, 1].astype(F32)[None]
-    w_gate_up = gather(jnp.concatenate([gate_weight, up_weight], axis=1), 0)
-    query_scaling = query_gain.astype(F32)
-    key_scaling = key_gain.astype(F32)
+    w_gate_up = lax.all_gather(gate_up_shard, "context", axis=0, tiled=True)
 
     chips = s ^ jnp.arange(seqs, dtype=jnp.int32)
     shards = t ^ jnp.arange(columns, dtype=jnp.int32)
@@ -1306,8 +1371,6 @@
     at = (((rank_of % 2) ^ core) * columns + (shard_of ^ t)) * seqs + ((rank_of // 2) ^ s)
     at = (at * piece).astype(jnp.int32)
 
-    row_shard = to_sequences(tokens, s, t)
-    rows = jnp.concatenate(gather_rows(row_shard), axis=0)
     qkv_raw = dot_nn(rows, w_first[:, :qkv_width])
     query_raw = qkv_raw[:, :head_width]
     key_raw = qkv_raw[:, head_width : 2 * head_width]
@@ -1354,17 +1417,16 @@
     def scatter(values):
         return lax.psum_scatter(values, "context", scatter_dimension=0, axis_index_groups=cores, tiled=True)
 
-    down_part = rank_sums(5, [(fed_low, act_low)], own)
+    output_pieces = output_pieces.reshape(shard)
+    split = seqs // 4 * piece
+    down_part, first_rows = rank_sums(5, [(fed_low, act_low)], own, (output_pieces, 0, split))
     down_summed = scatter(down_part)
+    down_grad = down_summed.astype(F32).T
     gate_up_low = act_back(after(fed_low, down_part), w_down, slopes)
-    output_rows = [output_pieces] + [swap(output_pieces, "tensor", k) for k in (order[1:3] if columns == 4 else order[1:])]
-    gate_up_part = rank_sums(6, [(after(hidden_low, *output_rows), gate_up_low)], own)
+    gate_up_part, other_rows = rank_sums(6, [(hidden_low, gate_up_low)], own, (output_pieces, split, shard_rows - split))
+    layer_output = in_place([values.reshape(columns, -1, piece, width) for values in (first_rows, other_rows)], s, t, BF)
     gate_up_summed = scatter(gate_up_part)
-    if columns == 4:
-        passed = [swap(output_rows[1][: seqs // 2], "tensor", 2), swap(output_rows[2][seqs // 2 :], "tensor", 1)]
-        output_rows.append(jnp.concatenate(passed, axis=0))
-    layer_output = in_place(jnp.stack(output_rows), s, t, BF)
-    gate_up_low = after(gate_up_low, gate_up_part, layer_output)
+    gate_up_low = after(gate_up_low, gate_up_part)
     attended_low, hidden_grad, attn_gain_rows = exchange(
         "hidden_grad",
         3,
@@ -1374,6 +1436,7 @@
         [attended, upstream, gain_attn],
         [(shard, F32), ((8, width), F32)],
     )
+    attended_low = after(attended_low, layer_output)
     mixed_grad = dot_nn(attended_low, w_first[:, qkv_width : 4 * head_width]).astype(BF)
     dqkv = attend_back(keep, received, mixed_heads, to_heads(mixed_grad), log, at, piece)
     dqkv_other = swap(dqkv[:, count:], "context", 1)
@@ -1393,16 +1456,15 @@
             (dqkv, 1),
             (dqkv_other, 1),
             (qkv_raw, 0),
-            (columns_of(*factors, *(inner * factors**3 / width)), 0),
+            (after(columns_of(*factors, *(inner * factors**3 / width)), down_grad), 0),
             (scaling, None),
             (cosine, 0),
             (sine, 0),
         ],
         [((count, 3 * head_width), BF, 0)],
     )
-    qkv_part = rank_sums(7, [(rows, qkv_low), (attended_low, mixed_low)], own)
+    (qkv_part,) = rank_sums(7, [(rows, qkv_low), (attended_low, mixed_low)], own)
     qkv_out_summed = scatter(after(qkv_part, gate_up_summed, down_summed))
-    down_grad = down_summed.astype(F32).T
     every, width_gains, head_gains = exchange(
         "tokens_grad",
         4,
@@ -1414,7 +1476,7 @@
         chips=seqs,
         last=True,
     )
-    tokens_grad = in_place(every.reshape(columns, seqs, piece, width), s, t, F32)
+    tokens_grad = in_place([every.reshape(columns, seqs, piece, width)], s, t, F32)
 
     gate_up_summed, qkv_out_summed = gate_up_summed.astype(F32), qkv_out_summed.astype(F32)
     return (

time: 815 us -> 783 us (0.961)
  waiting for transfers between devices: 129 us -> 43 us
  Pallas kernels: 564 us -> 647 us
  local copies, waits for them, and re-layouts: 40.5 us -> 25.8 us
  starting transfers between devices: 21.2 us -> 12.5 us
    pallas_call x3 -> x4, Pallas kernels: 72.9 us -> 176 us  [the longest x1 101 us: start(): pl.pallas_call(functools.partial(start_kernel, size, chips, offsets, len(...]
    ppermute x20 -> x10, waiting for transfers between devices: 99.1 us -> 9.24 us  [swap(): return lax.ppermute(values, axis, [(i, i ^ mask) for i in range(size)])]
    pallas_call x3, Pallas kernels: 262 us -> 242 us  [exchange(): pl.pallas_call(functools.partial(exchange_kernel, size, width, depth, off...]
    reduce_scatter x3, waiting for transfers between devices: 0.04 us -> 17.5 us  [scatter(): lax.psum_scatter(values, 'context', scatter_dimension=0, axis_index_group...]
    all_gather x2 -> x1, waiting for transfers between devices: 30 us -> 16.1 us  [local(): w_gate_up = lax.all_gather(gate_up_shard, 'context', axis=0, tiled=True)]
    unnamed x51 -> x31, local copies, waits for them, and re-layouts: 22.5 us -> 11.2 us
    ppermute x20 -> x10, starting transfers between devices: 21 us -> 12.4 us  [swap(): return lax.ppermute(values, axis, [(i, i ^ mask) for i in range(size)])]
  transfers between devices with their start and end apart: 25 -> 14, of which waited for: 19 -> 9; matrix products, arithmetic and copies ran while one was open for 7% -> 6% of each run, Pallas kernels for 50% -> 50%
where the time goes in v3:
time: 783 us; the launch traced here: 773 us
  Pallas kernels  647 us (83%)
  waiting for transfers between devices  43 us (5%)
  local copies, waits for them, and re-layouts  25.8 us (3%)
  matrix products  15.2 us (2%)
  between operations  14.6 us (2%)
  other arithmetic  14.2 us (2%)
  starting transfers between devices  12.5 us (2%)
    pallas_call x3, Pallas kernels, exchange(): pl.pallas_call(functools.partial(exchange_kernel, size, width, depth, off...  242 us
    pallas_call x1, Pallas kernels, feed(): pl.pallas_call(functools.partial(feed_kernel, size, chips, tile), in_spec...  141 us
    pallas_call x1, Pallas kernels, start(): pl.pallas_call(functools.partial(start_kernel, size, chips, offsets, len(...  101 us
    pallas_call x3, Pallas kernels, rank_sums(): pl.pallas_call(functools.partial(rank_sums_kernel, chips, size, tile, len...  74.8 us
    pallas_call x1, Pallas kernels, attend_back(): pl.pallas_call(functools.partial(attend_back_kernel, piece, 256), grid_sp...  22 us
    pallas_call x3, Pallas kernels, by_rows(): pl.pallas_call(kernel, grid_spec=pltpu.PrefetchScalarGridSpec(num_scalar_...  20.9 us
    reduce_scatter x3, waiting for transfers between devices, scatter(): lax.psum_scatter(values, 'context', scatter_dimension=0, axis_index_group...  17.5 us
    pallas_call x1, Pallas kernels, attend(): pl.pallas_call(functools.partial(attend_kernel, piece, 256), grid_spec=pl...  16.5 us
  transfers between devices with their start and end apart: 14, of which 9 were waited for; matrix products, arithmetic and copies ran while one was open for 6% of the time, Pallas kernels for 50%

profile of v3, /device:TPU:9, one launch (start us, length us, event | category | flops | bytes accessed | tf_op | source)
XLA Modules:
  0.0 772.6 jit_solution(4586009127547304059)
XLA Ops:
  7.2 1.8 copy.50
  9.0 0.7 stack.88
  9.7 0.7 stack.87
  10.5 0.6 pad.13.refs_5_
  11.1 101.4 %start.1 = (bf16[1024,2048]{1,0:T(8,128)(2,1)}, bf16[2048,2176]{1,0:T(8,128)(2,1)}, bf16[256,4096]{1,0:T(8,128)(2,1)}, bf16[256,2048]{1,0:T(8,128)(2,1)}) custom-call(bf16[4,256,2048]{2,1,0:T(8,128)(2,1)} %refs_0_.1, bf16[256,512]{1,0:T(8,128)(2,1)} %refs_1_.1, bf16[256,512]{1,0:T(8,128)(2,1)} %refs_2_.1, bf16[256,512]{1,0:T(8,128)(2,1)} %refs_3_.2, ...), custom_call_target="tpu_custom_call" | custom-call | bytes 300000000 | tf_op jit(solution)/shard_map/start/pallas_call | solution.py:720
  112.6 10.0 %fusion.raw_ref = f32[1024,1536]{1,0:T(8,128)S(1)} fusion(bf16[1024,2048]{1,0:T(8,128)(2,1)} %get-tuple-element.49.refs_0_, bf16[2048,2176]{1,0:T(8,128)(2,1)} %get-tuple-element.50.w_ref), kind=kOutput, calls=%fused_computation | convolution fusion | flops 6442450944 | bytes 16777216 | tf_op jit(solution)/shard_map/dot_general | solution.py:20
  122.6 2.7 copy-done
  125.7 2.1 collective-permute-start.2
  128.8 1.9 fusion.9
  130.8 1.0 pad_maximum_fusion.2.cosine_ref
  131.8 1.0 pad_maximum_fusion.3.sine_ref
  132.8 0.6 maximum_convert_fusion.gain_ref
  133.8 0.8 pad.14.column_ref
  134.7 6.1 turn.1
  140.8 3.9 collective-permute-start.3
  144.8 0.6 add_multiply_fusion.1.at_ref
  145.4 2.6 collective-permute-done.3.other_ref
  148.0 1.1 copy-done.9
  149.1 16.5 %attend.1 = (bf16[2048,256]{1,0:T(8,128)(2,1)}, f32[2,1,2048]{2,1,0:T(1,128)}) custom-call(s32[32]{0:T(128)} %add_multiply_fusion.1.at_ref, bf16[3,1024,256]{2,1,0:T(8,128)(2,1)} %get-tuple-element.51.own_ref, bf16[3,1024,256]{2,1,0:T(8,128)(2,1)} %copy-done.9), custom_call_target="tpu_custom_call" | custom-call | flops 4294967296 | bytes 4194304 | tf_op jit(solution)/shard_map/attend/pallas_call | solution.py:1223
  165.6 1.2 slice.145
  166.8 0.4 collective-permute-start.4
  167.2 1.6 copy.53
  168.8 2.4 convert_reduce_fusion
  171.3 1.1 pad_maximum_fusion.a_ref.refs_3_
  172.4 78.1 %attended.1 = (bf16[1024,2048]{1,0:T(8,128)(2,1)}, f32[256,2048]{1,0:T(8,128)}, f32[256,2048]{1,0:T(8,128)}) custom-call(bf16[1024,512]{1,0:T(8,128)(2,1)} %pad_maximum_fusion.a_ref.refs_3_, bf16[2048,2176]{1,0:T(8,128)(2,1)} %get-tuple-element.50.w_ref, bf16[256,2048]{1,0:T(8,128)(2,1)} %get-tuple-element.54.refs_0_, f32[1,2048]{1,0:T(1,128)} %bitcast.69), custom_call_target="tpu_custom_call" | custom-call | flops 2147483648 | bytes 240000000 | tf_op jit(solution)/shard_map/attended/pallas_call | solution.py:429
  250.5 16.1 %all-gather.2.cloned.1.call-done.refs_1_.w_ref = bf16[2048,4096]{1,0:T(8,128)(2,1)} async-done(((bf16[256,4096]{1,0:T(8,128)(2,1)}), bf16[2048,4096]{1,0:T(8,128)(2,1)}) %all-gather.2.cloned.1.call-update) | async-done | bytes 16777232 | tf_op jit(solution)/shard_map/all_gather | solution.py:1351
  266.7 141.1 %feed.1 = (bf16[1024,2048]{1,0:T(8,128)(2,1)}, bf16[1024,4096]{1,0:T(8,128)(2,1)}, bf16[1024,2048]{1,0:T(8,128)(2,1)}, bf16[2048,2048]{1,0:T(8,128)(2,1)}, bf16[...) custom-call(bf16[1024,2048]{1,0:T(8,128)(2,1)} %get-tuple-element.55.refs_0_, ...), custom_call_target="tpu_custom_call" | custom-call | flops 25769803776 | bytes 400000000 | tf_op jit(solution)/shard_map/feed/pallas_call | solution.py:914
  407.7 19.3 %rank_sums.3 = (bf16[1024,2048]{1,0:T(8,128)(2,1)}, bf16[256,2048]{1,0:T(8,128)(2,1)}) custom-call(bf16[1024,2048]{1,0:T(8,128)(2,1)} %get-tuple-element.63.refs_0_.grad_ref, bf16[1024,2048]{1,0:T(8,128)(2,1)} %get-tuple-element.59.refs_1_, bf16[256,2048]{1,0:T(8,128)(2,1)} %bitcast.83), custom_call_target="tpu_custom_call" | custom-call | flops 8589934592 | bytes 60000000 | tf_op jit(solution)/shard_map/rank_sums/pallas_call | solution.py:1142
  427.2 16.1 %act_back.1.refs_1_.a_ref = bf16[1024,4096]{1,0:T(8,128)(2,1)} custom-call(bf16[1024,2048]{1,0:T(8,128)(2,1)} %get-tuple-element.63.refs_0_.grad_ref, bf16[2048,2048]{1,0:T(8,128)(2,1)} %get-tuple-element.64.w_ref, bf16[1024,4096]{1,0:T(8,128)(2,1)} %get-tuple-element.65.slopes_ref), custom_call_target="tpu_custom_call" | custom-call | flops 8589934592 | bytes 40000000 | tf_op jit(solution)/shard_map/act_back/pallas_call | solution.py:1043
  443.3 34.5 %rank_sums.4 = (bf16[1024,4096]{1,0:T(8,128)(2,1)}, bf16[768,2048]{1,0:T(8,128)(2,1)}) custom-call(bf16[1024,2048]{1,0:T(8,128)(2,1)} %get-tuple-element.55.refs_0_, bf16[1024,4096]{1,0:T(8,128)(2,1)} %act_back.1.refs_1_.a_ref, bf16[256,2048]{1,0:T(8,128)(2,1)} %bitcast.84), custom_call_target="tpu_custom_call" | custom-call | flops 17179869184 | bytes 60000000 | tf_op jit(solution)/shard_map/rank_sums/pallas_call | solution.py:1142
  477.9 0.6 pad_add_fusion.at_ref
  478.4 5.9 place_rows.2
  484.3 81.7 %hidden_grad.1 = (bf16[1024,2048]{1,0:T(8,128)(2,1)}, f32[256,2048]{1,0:T(8,128)}, f32[8,2048]{1,0:T(8,128)}) custom-call(bf16[1024,4096]{1,0:T(8,128)(2,1)} %act_back.1.refs_1_.a_ref, bf16[2048,4096]{1,0:T(8,128)(2,1)} %all-gather.2.cloned.1.call-done.refs_1_.w_ref, f32[256,2048]{1,0:T(8,128)} %get-tuple-element.69.refs_0_, ...), custom_call_target="tpu_custom_call" | custom-call | flops 17179869184 | bytes 240000000 | tf_op jit(solution)/shard_map/hidden_grad/pallas_call | solution.py:429
  566.0 5.2 fusion.6
  571.3 2.2 collective-permute-start.5
  573.5 1.5 collective-permute-done.5
  575.0 1.0 pad_maximum_fusion.1.grad_ref
  576.1 22.0 %attend_back.1.own_ref = bf16[3,2048,256]{2,1,0:T(8,128)(2,1)} custom-call(s32[32]{0:T(128)} %add_multiply_fusion.1.at_ref, bf16[3,1024,256]{2,1,0:T(8,128)(2,1)} %get-tuple-element.51.own_ref, bf16[3,1024,256]{2,1,0:T(8,128)(2,1)} %copy-done.9, bf16[2048,256]{1,0:T(8,128)(2,1)} %get-tuple-element.53.out_ref, bf16[2048,256]{1,0:T(8,128)(2,1)} %pad_maximum_fusion.1.grad_ref, ...), custom_call_target="tpu_custom_call" | custom-call | flops 10737418240 | bytes 8388608 | tf_op jit(solution)/shard_map/attend_back/pallas_call | solution.py:1286
  598.1 1.5 slice.183
  599.6 0.4 collective-permute-start.6
  600.0 3.0 collective-permute-done.6.other_ref
  603.1 1.1 copy-done.3
  604.2 8.0 %inner.1 = (f32[2,8,1024]{2,1,0:T(8,128)}, f32[2,8,512]{2,1,0:T(8,128)}) custom-call(s32[1]{0:T(128)} %bitcast.2.core_ref, bf16[3,2048,256]{2,1,0:T(8,128)(2,1)} %attend_back.1.own_ref, bf16[3,1024,256]{2,1,0:T(8,128)(2,1)} %copy-done.3, f32[1024,1536]{1,0:T(8,128)} %copy-done, f32[1024,8]{1,0:T(8,128)} %pad.14.column_ref, ...), custom_call_target="tpu_custom_call" | custom-call | tf_op jit(solution)/shard_map/inner/pallas_call | solution.py:1017
  612.2 0.9 fusion.28
  613.1 0.8 collective-permute-start.8
  613.9 1.2 collective-permute-start.9
  615.1 0.7 collective-permute-start.7
  616.0 1.2 collective-permute-done.9
  617.3 0.6 collective-permute-done.7
  618.3 0.8 pad.15.column_ref
  619.1 1.5 convert_bitcast_fusion
  620.6 6.8 raw_grad.1.refs_2_.a_ref
  627.4 21.0 %rank_sums.5 = bf16[1024,2048]{1,0:T(8,128)(2,1)} custom-call(bf16[1024,2048]{1,0:T(8,128)(2,1)} %get-tuple-element.49.refs_0_, bf16[1024,2048]{1,0:T(8,128)(2,1)} %get-tuple-element.72.refs_1_, bf16[1024,1536]{1,0:T(8,128)(2,1)} %raw_grad.1.refs_2_.a_ref, bf16[1024,512]{1,0:T(8,128)(2,1)} %pad_maximum_fusion.a_ref.refs_3_), custom_call_target="tpu_custom_call" | custom-call | flops 8589934592 | bytes 60000000 | tf_op jit(solution)/shard_map/rank_sums/pallas_call | solution.py:1142
  648.4 8.7 %reduce-scatter.6.cloned.1.call-done = bf16[256,4096]{1,0:T(8,128)(2,1)} async-done(((bf16[1024,4096]{1,0:T(8,128)(2,1)}), bf16[256,4096]{1,0:T(8,128)(2,1)}) %reduce-scatter.6.cloned.1.call-update) | async-done | bytes 2097168 | tf_op jit(solution)/shard_map/reduce_scatter | solution.py:1418
  657.2 1.8 copy.56
  659.0 82.1 %tokens_grad.1 = (bf16[1024,2048]{1,0:T(8,128)(2,1)}, f32[8,256]{1,0:T(8,128)}, f32[8,512]{1,0:T(8,128)}) custom-call(bf16[1024,1536]{1,0:T(8,128)(2,1)} %raw_grad.1.refs_2_.a_ref, bf16[2048,2176]{1,0:T(8,128)(2,1)} %get-tuple-element.50.w_ref, f32[256,2048]{1,0:T(8,128)} %get-tuple-element.77.refs_0_, f32[8,2048]{1,0:T(8,128)} %get-tuple-element.78.refs_1_, ...), custom_call_target="tpu_custom_call" | custom-call | flops 6442450944 | bytes 240000000 | tf_op jit(solution)/shard_map/tokens_grad/pallas_call | solution.py:429
  741.1 6.8 place_rows.3
  747.9 1.3 fusion.30
  749.2 1.4 fusion.29
  750.6 2.5 fusion.26
  753.1 8.8 %reduce-scatter.8.cloned.1.call-done = bf16[256,2048]{1,0:T(8,128)(2,1)} async-done(((bf16[1024,2048]{1,0:T(8,128)(2,1)}), bf16[256,2048]{1,0:T(8,128)(2,1)}) %reduce-scatter.8.cloned.1.call-update) | async-done | bytes 1048592 | tf_op jit(solution)/shard_map/reduce_scatter | solution.py:1418
  761.9 1.5 convert_element_type.60
  763.5 1.0 copy.55
  764.5 1.2 fusion.27
  (82 shorter events, 3.1 us)
Async XLA Ops:
  7.2 259.5 %all-gather.2.cloned.1.call-start = ((), (), s32[]{:S(2)}) async-start(), calls=%async_computation.3 | async-start | bytes 18874368 | tf_op jit(solution)/shard_map/all_gather | solution.py:1351
  112.5 506.6 %reduce-scatter.4.cloned.1.call-start = ((), (), s32[]{:S(2)}) async-start(), calls=%async_computation.4 | async-start | bytes 5242880 | tf_op jit(solution)/shard_map/reduce_scatter | solution.py:1418
  122.6 2.7 copy-start
  125.3 3.1 copy-start.6
  125.3 3.1 copy-start.7
  125.3 3.4 copy-start.8
  125.7 7.7 collective-permute-start.2
  127.8 5.6 collective-permute-start.1
  128.0 5.5 collective-permute-start
  140.8 7.2 collective-permute-start.3
  148.0 1.1 copy-start.9
  149.1 18.1 %copy-start.5 = (bf16[2048,256]{1,0:T(8,128)(2,1)S(1)}, bf16[2048,256]{1,0:T(8,128)(2,1)}, u32[]{:S(2)}) copy-start(bf16[2048,256]{1,0:T(8,128)(2,1)} %param.22) | copy-start | bytes 3145732
  165.6 5.6 copy-start.4
  166.8 4.5 collective-permute-start.4
  427.1 230.1 %reduce-scatter.6.cloned.1.call-start = ((), (), s32[]{:S(2)}) async-start(), calls=%async_computation.5 | async-start | bytes 10485760 | tf_op jit(solution)/shard_map/reduce_scatter | solution.py:1418
  477.8 284.1 %reduce-scatter.8.cloned.1.call-start = ((), (), s32[]{:S(2)}) async-start(), calls=%async_computation.6 | async-start | bytes 5242880 | tf_op jit(solution)/shard_map/reduce_scatter | solution.py:1418
  571.3 3.7 collective-permute-start.5
  599.6 3.5 collective-permute-start.6
  603.1 1.1 copy-start.3
  613.1 3.0 collective-permute-start.8
  613.9 3.4 collective-permute-start.9
  615.1 2.9 collective-permute-start.7
  741.1 9.5 %copy-start.1 = (bf16[256,4096]{1,0:T(8,128)(2,1)S(1)}, bf16[256,4096]{1,0:T(8,128)(2,1)}, u32[]{:S(2)}) copy-start(bf16[256,4096]{1,0:T(8,128)(2,1)} %reduce-scatter.6.cloned.1.call-done) | copy-start | bytes 6291460
  761.9 2.6 copy-start.2
Sparse Core Ops, SparseCore 0:
  112.7 153.9 all-gather.1
  427.2 82.6 reduce-scatter.3
  512.4 144.6 reduce-scatter.5
  659.4 102.4 reduce-scatter.7

commit v4 on v3

--- a/solution.py
+++ b/solution.py
@@ -503,16 +503,21 @@
         self.c = lax.axis_index("context")
         self.s, self.core = self.c // 2, self.c % 2
 
-    def rows(self, chip):
-        return pl.ds(pl.multiple_of((2 * chip + self.core) * self.own, self.own), self.own)
-
-    def hop(self, k, way, chip):
-        part = self.buf.at[self.rows(chip), :]
-        return remote(part, part, self.sems[way], k, {"context": self.c + 2 * way})
-
-    def cross(self, k, way, chip):
-        part = self.buf.at[self.rows(chip), :]
-        return remote(part, part, self.core_sems, 0 if k < 0 else 1 + 2 * k + (way < 0), {"context": flip(self.c, 1)})
+    def rows(self, chip, part=None):
+        base = (2 * chip + self.core) * self.own
+        if part is None:
+            return pl.ds(pl.multiple_of(base, self.own), self.own)
+        half = self.own // 2
+        return pl.ds(pl.multiple_of(base + part * half, half), half)
+
+    def hop(self, k, way, chip, part):
+        ref = self.buf.at[self.rows(chip, part), :]
+        return remote(ref, ref, self.sems[way], 2 * k + part, {"context": self.c + 2 * way})
+
+    def cross(self, k, way, chip, part):
+        ref = self.buf.at[self.rows(chip, part), :]
+        slot = 0 if k < 0 else 1 + 2 * k + (way < 0)
+        return remote(ref, ref, self.core_sems, 2 * slot + part, {"context": flip(self.c, 1)})
 
     def sends(self, k, way):
         if way > 0:
@@ -526,39 +531,44 @@
         for way in (1, -1):
             pl.when(test(k, way))(functools.partial(act, k, way))
 
-    def start(self, k):
-        self.each(self.sends, k, lambda k, way: self.hop(k, way, self.s - way * k).start())
+    def start(self, k, part):
+        self.each(self.sends, k, lambda k, way: self.hop(k, way, self.s - way * k, part).start())
 
     def begin(self):
-        self.start(0)
-        self.cross(-1, 1, self.s).start()
-
-    def advance(self, k):
-        def got(k, way):
-            chip = self.s - way * (k + 1)
-            self.hop(k, way, chip).wait_recv()
-            self.cross(k, way, chip).start()
-
-        self.each(self.gets, k, got)
-        if k + 1 < self.chips - 1:
-            self.start(k + 1)
+        for part in range(2):
+            self.start(0, part)
+            self.cross(-1, 1, self.s, part).start()
+
+    def advance(self, k, parts=(0, 1)):
+        for part in parts:
+
+            def got(k, way):
+                chip = self.s - way * (k + 1)
+                self.hop(k, way, chip, part).wait_recv()
+                self.cross(k, way, chip, part).start()
+
+            self.each(self.gets, k, got)
+            if k + 1 < self.chips - 1:
+                self.start(k + 1, part)
 
     def other_core(self, k):
-        if k < 0:
-            self.cross(-1, 1, self.s).wait_recv()
-        else:
-            self.each(self.gets, k, lambda k, way: self.cross(k, way, self.s - way * (k + 1)).wait_recv())
+        for part in range(2):
+            if k < 0:
+                self.cross(-1, 1, self.s, part).wait_recv()
+            else:
+                self.each(self.gets, k, lambda k, way: self.cross(k, way, self.s - way * (k + 1), part).wait_recv())
 
     def end(self):
-        self.cross(-1, 1, self.s).wait_send()
-        for k in range(self.chips - 1):
-            self.each(self.sends, k, lambda k, way: self.hop(k, way, self.s - way * k).wait_send())
-            self.each(self.gets, k, lambda k, way: self.cross(k, way, self.s - way * (k + 1)).wait_send())
+        for part in range(2):
+            self.cross(-1, 1, self.s, part).wait_send()
+            for k in range(self.chips - 1):
+                self.each(self.sends, k, lambda k, way: self.hop(k, way, self.s - way * k, part).wait_send())
+                self.each(self.gets, k, lambda k, way: self.cross(k, way, self.s - way * (k + 1), part).wait_send())
 
 
 def line_sems(chips):
     dma = pltpu.SemaphoreType.DMA
-    return [dma((chips - 1,))] * 4 + [dma((2 * chips - 1,))] * 2
+    return [dma((2 * (chips - 1),))] * 4 + [dma((2 * (2 * chips - 1),))] * 2
 
 
 class Sums:
@@ -654,9 +664,10 @@
 
 
 def start_kernel(size, chips, offsets, n_pair, *refs):
-    tokens_ref, firsts, pair, refs = refs[0], refs[1 : 1 + len(offsets)], refs[1 + len(offsets) :][:n_pair], refs[1 + len(offsets) + n_pair :]
-    every, whole, both, shard = refs[:4]
-    line_refs, gather, coming, own_sem, keep_sem = refs[4:10], refs[10:12], refs[12:14], refs[14], refs[15]
+    tokens_ref, firsts, refs = refs[0], refs[1 : 1 + len(offsets)], refs[1 + len(offsets) :]
+    turned_ref, gains_ref, pair, refs = refs[0], refs[1], refs[2 : 2 + n_pair], refs[2 + n_pair :]
+    every, out, both, shard = refs[:4]
+    line_refs, gather, coming, own_sem, keep_sem, whole, turned, out_sem = refs[4:10], refs[10:12], refs[12:14], *refs[14:19]
     t, c = lax.axis_index("tensor"), lax.axis_index("context")
     s = c // 2
     rows = shard.shape[0]
@@ -672,8 +683,15 @@
     kept += [
         pltpu.make_async_copy(part, both.at[:, pl.ds(i * across, across)], keep_sem.at[len(offsets) + i]) for i, part in enumerate(pair)
     ]
-    for copy in kept:
+    turned_copy = pltpu.make_async_copy(turned_ref, turned, keep_sem.at[len(offsets) + n_pair])
+    for copy in [turned_copy, *kept]:
         copy.start()
+    after_firsts = sum(first.shape[1] for first in firsts)
+    height = turned.shape[0]
+    turned_copy.wait()
+    whole[line.rows(s), after_firsts : after_firsts + height] = turned[...].astype(F32).T.astype(BF)
+    gains = jnp.concatenate([gains_ref[...].astype(F32), jnp.zeros((HD - gains_ref.shape[0], own), F32)], axis=0)
+    whole[line.rows(s), after_firsts + height :] = gains.T.astype(BF)
     arrivals = [
         (tokens_ref.at[flip(s, j), pl.ds(pl.multiple_of(t * piece, piece), piece), :], shard.at[pl.ds(j * piece, piece), :])
         for j in range(chips)
@@ -692,20 +710,34 @@
     share = Gather(size, t, shard, every, gather, own_sem)
     share.start(0)
     share.start(1)
+
+    def write(k, way, chip):
+        at = pl.ds(pl.multiple_of(chip * 2 * own, 2 * own), 2 * own)
+        return pltpu.make_async_copy(whole.at[at, :], out.at[at, :], out_sem.at[0 if k < 0 else 1 + 2 * k + (way < 0)])
+
+    def keep(k):
+        line.other_core(k)
+        line.each(line.gets, k, lambda k, way: write(k, way, s - way * (k + 1)).start())
+
     line.advance(0)
+    line.other_core(-1)
+    write(-1, 1, s).start()
     share.pass_on()
     for k in range(1, chips - 1):
         line.advance(k)
+        keep(k - 1)
     share.wait()
-    for k in range(-1, chips - 1):
-        line.other_core(k)
+    keep(chips - 2)
     line.end()
     share.end()
     for copy in others:
         copy.wait_send()
-
-
-def start(tokens, firsts, pair, chips):
+    write(-1, 1, s).wait()
+    for k in range(chips - 1):
+        line.each(line.gets, k, lambda k, way: write(k, way, s - way * (k + 1)).wait())
+
+
+def start(tokens, firsts, turned, gains, pair, chips):
     size = lax.axis_size("tensor")
     seqs, local_len, width = tokens.shape
     rows = seqs * local_len // size
@@ -714,13 +746,14 @@
     for first in firsts:
         offsets.append(across)
         across += first.shape[1]
+    across += turned.shape[0] + HD
     dma = pltpu.SemaphoreType.DMA
-    anywhere = pl.BlockSpec(memory_space=pl.ANY)
+    anywhere, in_vmem = pl.BlockSpec(memory_space=pl.ANY), pl.BlockSpec(memory_space=pltpu.VMEM)
     shape = jax.ShapeDtypeStruct
     return pl.pallas_call(
         functools.partial(start_kernel, size, chips, offsets, len(pair)),
-        in_specs=[anywhere] * (1 + len(firsts) + len(pair)),
-        out_specs=[anywhere] + [pl.BlockSpec(memory_space=pltpu.VMEM)] * 3,
+        in_specs=[anywhere] * (2 + len(firsts)) + [in_vmem] + [anywhere] * len(pair),
+        out_specs=[anywhere] * 2 + [in_vmem] * 2,
         out_shape=[
             shape((size * rows, width), BF),
             shape((2 * chips * own, across), BF),
@@ -730,11 +763,12 @@
         scratch_shapes=line_sems(chips)
         + [dma((links_of(size),))] * 2
         + [dma((chips,))] * 2
-        + [dma, dma((len(firsts) + len(pair),))],
+        + [dma, dma((len(firsts) + len(pair) + 1,))]
+        + [pltpu.VMEM((2 * chips * own, across), BF), pltpu.VMEM(turned.shape, BF), dma((2 * chips - 1,))],
         compiler_params=pltpu.CompilerParams(vmem_limit_bytes=VMEM_LIMIT, collective_id=8, has_side_effects=True),
         cost_estimate=pl.CostEstimate(flops=0, bytes_accessed=300_000_000, transcendentals=0),
         name="start",
-    )(tokens, *firsts, *pair)
+    )(tokens, *firsts, turned, gains, *pair)
 
 
 def feed_kernel(size, chips, tile, *refs):
@@ -808,6 +842,10 @@
             return carry
 
         lax.fori_loop(0, tiles, step, 0)
+        if n + 1 == size // 2:
+            line.advance(0, (0,))
+        if n + 1 == size * 3 // 4:
+            line.advance(0, (1,))
     for slot in range(2):
         for i in range(2):
             stage_copy(slot, i, 0, 0).wait()
@@ -829,7 +867,6 @@
                 total[:, at] = value
         rounds.append(group)
 
-    line.advance(0)
     line.other_core(-1)
     fed_round(0)
     line.other_core(0)
@@ -1095,35 +1132,39 @@
         share = Gather(size, t, part, every_ref, (sent_out, got_out), own_sem)
         share.start(0)
         share.start(1)
-    sends = [remote(passed.at[j], got.at[j], (sent_sem, got_sem), j, {"context": flip(c, 1)}) for j in range(chips)]
-    writes = [pltpu.make_async_copy(out.at[j], out_ref.at[pl.ds(j * own, own), :], out_sem.at[j]) for j in range(chips)]
-    for at, (j, core_at) in enumerate(blocks):
+    def send(j):
+        return remote(passed.at[j], got.at[j], (sent_sem, got_sem), j, {"context": flip(c, 1)})
+
+    def write(j):
+        return pltpu.make_async_copy(out.at[j], out_ref.at[pl.ds(pl.multiple_of(j * own, own), own), :], out_sem.at[j])
+
+    def block(core_at, j, carry):
         base = 0
         if core_at == 0:
-            sends[j].wait_recv()
+            send(j).wait_recv()
         for i in range(count):
             left_copy(i, j, core_at).wait()
-            left = left_bufs[i][core_at * chips + j].astype(F32).T.astype(BF)
-
-            def step(n, carry):
-                if at == 0:
-                    right_copy(i, n).wait()
-                part = dot_nn(left, right_bufs[i][:, pl.ds(pl.multiple_of(n * tile, tile), tile)])
-                to = pl.ds(pl.multiple_of(base + n * tile, tile), tile)
+            left = left_bufs[i][core_at * chips + j].T
+            for n in range(tiles[i]):
+                if core_at:
+                    pl.when(j == 0)(right_copy(i, n).wait)
+                to = slice(base + n * tile, base + (n + 1) * tile)
+                part = dot_nn(left, right_bufs[i][:, n * tile : (n + 1) * tile])
                 if core_at:
                     passed[j, :, to] = part.astype(BF)
                 else:
                     out[j, :, to] = (part + got[j, :, to].astype(F32)).astype(BF)
-                return carry
-
-            lax.fori_loop(0, tiles[i], step, 0)
             base += tiles[i] * tile
-        (sends if core_at else writes)[j].start()
-        if carries and at == len(blocks) - 3:
-            share.pass_on()
+        (send if core_at else write)(j).start()
+        if carries and core_at == 0:
+            pl.when(j == 1)(share.pass_on)
+        return carry
+
+    lax.fori_loop(0, chips, functools.partial(block, 1), 0)
+    lax.fori_loop(0, chips, functools.partial(block, 0), 0)
     for j in range(chips):
-        sends[j].wait_send()
-        writes[j].wait()
+        send(j).wait_send()
+        write(j).wait()
     if carries:
         share.wait()
         share.end()
@@ -1341,10 +1382,14 @@
     half_width = head_width // 2
     hidden_width = gate_weight.shape[1]
 
-    gain_columns = jnp.stack([attention_gain, forward_gain], axis=1)
-    gain_columns = jnp.pad(gain_columns, ((0, 0), (0, HD - 2)))
-    firsts = [query_weight, key_weight, value_weight, output_weight.T, gain_columns]
-    rows, w_first, gate_up_shard, row_shard = start(tokens, firsts, [gate_weight, up_weight], seqs)
+    rows, w_first, gate_up_shard, row_shard = start(
+        tokens,
+        [query_weight, key_weight, value_weight],
+        output_weight,
+        jnp.stack([attention_gain, forward_gain]),
+        [gate_weight, up_weight],
+        seqs,
+    )
     qkv_width = 3 * head_width
     gains = w_first[:, 4 * head_width :]
     gain_attn, gain_feed = gains[:, 0].astype(F32)[None], gains[:, 1].astype(F32)[None]

time: 783 us -> 770 us (0.983)
  Pallas kernels: 647 us -> 630 us
where the time goes in v4:
time: 770 us; the launch traced here: 759 us
  Pallas kernels  630 us (82%)
  waiting for transfers between devices  50.5 us (7%)
  local copies, waits for them, and re-layouts  23.3 us (3%)
  matrix products  15.3 us (2%)
  other arithmetic  14.7 us (2%)
  between operations  14.4 us (2%)
  starting transfers between devices  11.2 us (1%)
    pallas_call x3, Pallas kernels, exchange(): pl.pallas_call(functools.partial(exchange_kernel, size, width, depth, off...  240 us
    pallas_call x1, Pallas kernels, feed(): pl.pallas_call(functools.partial(feed_kernel, size, chips, tile), in_spec...  141 us
    pallas_call x1, Pallas kernels, start(): pl.pallas_call(functools.partial(start_kernel, size, chips, offsets, len(...  93.7 us
    pallas_call x3, Pallas kernels, rank_sums(): pl.pallas_call(functools.partial(rank_sums_kernel, chips, size, tile, len...  67.2 us
    reduce_scatter x3, waiting for transfers between devices, scatter(): lax.psum_scatter(values, 'context', scatter_dimension=0, axis_index_group...  23.5 us
    pallas_call x1, Pallas kernels, attend_back(): pl.pallas_call(functools.partial(attend_back_kernel, piece, 256), grid_sp...  22.2 us
    pallas_call x3, Pallas kernels, by_rows(): pl.pallas_call(kernel, grid_spec=pltpu.PrefetchScalarGridSpec(num_scalar_...  20.9 us
    all_gather x1, waiting for transfers between devices, local(): w_gate_up = lax.all_gather(gate_up_shard, 'context', axis=0, tiled=True)  16.8 us
  transfers between devices with their start and end apart: 14, of which 9 were waited for; matrix products, arithmetic and copies ran while one was open for 6% of the time, Pallas kernels for 50%

profile of v4, /device:TPU:9, one launch (start us, length us, event | category | flops | bytes accessed | tf_op | source)
XLA Modules:
  0.0 759.5 jit_solution(12586266823541398540)
XLA Ops:
  7.2 0.7 stack.88
  7.9 0.7 stack.87
  8.5 0.6 pad_maximum_fusion.6.refs_5_
  9.1 93.7 %start.1 = (bf16[1024,2048]{1,0:T(8,128)(2,1)}, bf16[2048,2176]{1,0:T(8,128)(2,1)}, bf16[256,4096]{1,0:T(8,128)(2,1)}, bf16[256,2048]{1,0:T(8,128)(2,1)}) custom-call(bf16[4,256,2048]{2,1,0:T(8,128)(2,1)} %refs_0_.1, bf16[256,512]{1,0:T(8,128)(2,1)} %refs_1_.1, bf16[256,512]{1,0:T(8,128)(2,1)} %refs_2_.1, bf16[256,512]{1,0:T(8,128)(2,1)} %refs_3_.2, ...), custom_call_target="tpu_custom_call" | custom-call | bytes 300000000 | tf_op jit(solution)/shard_map/start/pallas_call | solution.py:753
  102.9 10.0 %fusion.raw_ref = f32[1024,1536]{1,0:T(8,128)S(1)} fusion(bf16[1024,2048]{1,0:T(8,128)(2,1)} %get-tuple-element.49.refs_0_, bf16[2048,2176]{1,0:T(8,128)(2,1)} %get-tuple-element.50.w_ref), kind=kOutput, calls=%fused_computation | convolution fusion | flops 6442450944 | bytes 16777216 | tf_op jit(solution)/shard_map/dot_general | solution.py:20
  113.0 2.7 copy-done
  115.6 0.3 fusion.2
  116.0 3.4 collective-permute-start.2
  119.5 0.2 collective-permute-start.1
  120.3 1.9 fusion.9
  122.2 1.0 pad_maximum_fusion.2.cosine_ref
  123.2 1.0 pad_maximum_fusion.3.sine_ref
  124.2 0.6 maximum_convert_fusion.gain_ref
  125.2 0.8 pad.9.column_ref
  126.1 6.1 turn.1
  132.2 1.6 collective-permute-start.3
  133.9 0.6 add_multiply_fusion.1.at_ref
  134.5 2.6 collective-permute-done.3.other_ref
  137.1 1.1 copy-done.9
  138.2 16.5 %attend.1 = (bf16[2048,256]{1,0:T(8,128)(2,1)}, f32[2,1,2048]{2,1,0:T(1,128)}) custom-call(s32[32]{0:T(128)} %add_multiply_fusion.1.at_ref, bf16[3,1024,256]{2,1,0:T(8,128)(2,1)} %get-tuple-element.51.own_ref, bf16[3,1024,256]{2,1,0:T(8,128)(2,1)} %copy-done.9), custom_call_target="tpu_custom_call" | custom-call | flops 4294967296 | bytes 4194304 | tf_op jit(solution)/shard_map/attend/pallas_call | solution.py:1264
  154.7 1.2 slice.145
  155.9 0.5 collective-permute-start.4
  156.3 1.6 copy.45
  157.9 2.4 convert_reduce_fusion
  160.4 1.1 pad_maximum_fusion.a_ref.refs_3_
  161.5 77.9 %attended.1 = (bf16[1024,2048]{1,0:T(8,128)(2,1)}, f32[256,2048]{1,0:T(8,128)}, f32[256,2048]{1,0:T(8,128)}) custom-call(bf16[1024,512]{1,0:T(8,128)(2,1)} %pad_maximum_fusion.a_ref.refs_3_, bf16[2048,2176]{1,0:T(8,128)(2,1)} %get-tuple-element.50.w_ref, bf16[256,2048]{1,0:T(8,128)(2,1)} %get-tuple-element.54.refs_0_, f32[1,2048]{1,0:T(1,128)} %bitcast.67), custom_call_target="tpu_custom_call" | custom-call | flops 2147483648 | bytes 240000000 | tf_op jit(solution)/shard_map/attended/pallas_call | solution.py:429
  239.5 16.8 %all-gather.2.cloned.1.call-done.refs_1_.w_ref = bf16[2048,4096]{1,0:T(8,128)(2,1)} async-done(((bf16[256,4096]{1,0:T(8,128)(2,1)}), bf16[2048,4096]{1,0:T(8,128)(2,1)}) %all-gather.2.cloned.1.call-update) | async-done | bytes 16777232 | tf_op jit(solution)/shard_map/all_gather | solution.py:1396
  256.3 140.6 %feed.1 = (bf16[1024,2048]{1,0:T(8,128)(2,1)}, bf16[1024,4096]{1,0:T(8,128)(2,1)}, bf16[1024,2048]{1,0:T(8,128)(2,1)}, bf16[2048,2048]{1,0:T(8,128)(2,1)}, bf16[...) custom-call(bf16[1024,2048]{1,0:T(8,128)(2,1)} %get-tuple-element.55.refs_0_, ...), custom_call_target="tpu_custom_call" | custom-call | flops 25769803776 | bytes 400000000 | tf_op jit(solution)/shard_map/feed/pallas_call | solution.py:951
  396.9 16.2 %rank_sums.3 = (bf16[1024,2048]{1,0:T(8,128)(2,1)}, bf16[256,2048]{1,0:T(8,128)(2,1)}) custom-call(bf16[1024,2048]{1,0:T(8,128)(2,1)} %get-tuple-element.63.refs_0_.grad_ref, bf16[1024,2048]{1,0:T(8,128)(2,1)} %get-tuple-element.59.refs_1_, bf16[256,2048]{1,0:T(8,128)(2,1)} %bitcast.81), custom_call_target="tpu_custom_call" | custom-call | flops 8589934592 | bytes 60000000 | tf_op jit(solution)/shard_map/rank_sums/pallas_call | solution.py:1183
  413.2 16.3 %act_back.1.refs_1_.a_ref = bf16[1024,4096]{1,0:T(8,128)(2,1)} custom-call(bf16[1024,2048]{1,0:T(8,128)(2,1)} %get-tuple-element.63.refs_0_.grad_ref, bf16[2048,2048]{1,0:T(8,128)(2,1)} %get-tuple-element.64.w_ref, bf16[1024,4096]{1,0:T(8,128)(2,1)} %get-tuple-element.65.slopes_ref), custom_call_target="tpu_custom_call" | custom-call | flops 8589934592 | bytes 40000000 | tf_op jit(solution)/shard_map/act_back/pallas_call | solution.py:1080
  429.5 32.2 %rank_sums.4 = (bf16[1024,4096]{1,0:T(8,128)(2,1)}, bf16[768,2048]{1,0:T(8,128)(2,1)}) custom-call(bf16[1024,2048]{1,0:T(8,128)(2,1)} %get-tuple-element.55.refs_0_, bf16[1024,4096]{1,0:T(8,128)(2,1)} %act_back.1.refs_1_.a_ref, bf16[256,2048]{1,0:T(8,128)(2,1)} %bitcast.82), custom_call_target="tpu_custom_call" | custom-call | flops 17179869184 | bytes 60000000 | tf_op jit(solution)/shard_map/rank_sums/pallas_call | solution.py:1183
  461.8 0.6 pad_add_fusion.at_ref
  462.4 5.5 place_rows.2
  467.8 80.4 %hidden_grad.1 = (bf16[1024,2048]{1,0:T(8,128)(2,1)}, f32[256,2048]{1,0:T(8,128)}, f32[8,2048]{1,0:T(8,128)}) custom-call(bf16[1024,4096]{1,0:T(8,128)(2,1)} %act_back.1.refs_1_.a_ref, bf16[2048,4096]{1,0:T(8,128)(2,1)} %all-gather.2.cloned.1.call-done.refs_1_.w_ref, f32[256,2048]{1,0:T(8,128)} %get-tuple-element.69.refs_0_, ...), custom_call_target="tpu_custom_call" | custom-call | flops 17179869184 | bytes 240000000 | tf_op jit(solution)/shard_map/hidden_grad/pallas_call | solution.py:429
  548.3 5.3 fusion.6
  553.6 1.7 collective-permute-start.5
  555.3 1.5 collective-permute-done.5
  556.8 1.0 pad_maximum_fusion.1.grad_ref
  557.8 22.2 %attend_back.1.own_ref = bf16[3,2048,256]{2,1,0:T(8,128)(2,1)} custom-call(s32[32]{0:T(128)} %add_multiply_fusion.1.at_ref, bf16[3,1024,256]{2,1,0:T(8,128)(2,1)} %get-tuple-element.51.own_ref, bf16[3,1024,256]{2,1,0:T(8,128)(2,1)} %copy-done.9, bf16[2048,256]{1,0:T(8,128)(2,1)} %get-tuple-element.53.out_ref, bf16[2048,256]{1,0:T(8,128)(2,1)} %pad_maximum_fusion.1.grad_ref, ...), custom_call_target="tpu_custom_call" | custom-call | flops 10737418240 | bytes 8388608 | tf_op jit(solution)/shard_map/attend_back/pallas_call | solution.py:1327
  580.0 1.5 slice.183
  581.5 0.3 collective-permute-start.6
  581.8 3.2 collective-permute-done.6.other_ref
  585.0 1.1 copy-done.3
  586.1 8.0 %inner.1 = (f32[2,8,1024]{2,1,0:T(8,128)}, f32[2,8,512]{2,1,0:T(8,128)}) custom-call(s32[1]{0:T(128)} %bitcast.2.core_ref, bf16[3,2048,256]{2,1,0:T(8,128)(2,1)} %attend_back.1.own_ref, bf16[3,1024,256]{2,1,0:T(8,128)(2,1)} %copy-done.3, f32[1024,1536]{1,0:T(8,128)} %copy-done, f32[1024,8]{1,0:T(8,128)} %pad.9.column_ref, ...), custom_call_target="tpu_custom_call" | custom-call | tf_op jit(solution)/shard_map/inner/pallas_call | solution.py:1054
  594.1 0.9 fusion.28
  595.0 1.8 collective-permute-start.8
  596.8 1.4 collective-permute-start.9
  598.3 1.9 collective-permute-done.9
  600.3 0.8 collective-permute-done.7
  601.5 0.8 pad.10.column_ref
  602.3 1.5 convert_bitcast_fusion
  603.8 6.8 raw_grad.1.refs_2_.a_ref
  610.6 18.8 %rank_sums.5 = bf16[1024,2048]{1,0:T(8,128)(2,1)} custom-call(bf16[1024,2048]{1,0:T(8,128)(2,1)} %get-tuple-element.49.refs_0_, bf16[1024,2048]{1,0:T(8,128)(2,1)} %get-tuple-element.72.refs_1_, bf16[1024,1536]{1,0:T(8,128)(2,1)} %raw_grad.1.refs_2_.a_ref, bf16[1024,512]{1,0:T(8,128)(2,1)} %pad_maximum_fusion.a_ref.refs_3_), custom_call_target="tpu_custom_call" | custom-call | flops 8589934592 | bytes 60000000 | tf_op jit(solution)/shard_map/rank_sums/pallas_call | solution.py:1183
  629.4 14.7 %reduce-scatter.6.cloned.1.call-done = bf16[256,4096]{1,0:T(8,128)(2,1)} async-done(((bf16[1024,4096]{1,0:T(8,128)(2,1)}), bf16[256,4096]{1,0:T(8,128)(2,1)}) %reduce-scatter.6.cloned.1.call-update) | async-done | bytes 2097168 | tf_op jit(solution)/shard_map/reduce_scatter | solution.py:1463
  644.1 2.0 copy.48
  646.0 82.1 %tokens_grad.1 = (bf16[1024,2048]{1,0:T(8,128)(2,1)}, f32[8,256]{1,0:T(8,128)}, f32[8,512]{1,0:T(8,128)}) custom-call(bf16[1024,1536]{1,0:T(8,128)(2,1)} %raw_grad.1.refs_2_.a_ref, bf16[2048,2176]{1,0:T(8,128)(2,1)} %get-tuple-element.50.w_ref, f32[256,2048]{1,0:T(8,128)} %get-tuple-element.77.refs_0_, f32[8,2048]{1,0:T(8,128)} %get-tuple-element.78.refs_1_, ...), custom_call_target="tpu_custom_call" | custom-call | flops 6442450944 | bytes 240000000 | tf_op jit(solution)/shard_map/tokens_grad/pallas_call | solution.py:429
  728.2 6.8 place_rows.3
  734.9 1.3 fusion.30
  736.3 1.4 fusion.29
  737.7 2.5 fusion.26
  740.2 8.8 %reduce-scatter.8.cloned.1.call-done = bf16[256,2048]{1,0:T(8,128)(2,1)} async-done(((bf16[1024,2048]{1,0:T(8,128)(2,1)}), bf16[256,2048]{1,0:T(8,128)(2,1)}) %reduce-scatter.8.cloned.1.call-update) | async-done | bytes 1048592 | tf_op jit(solution)/shard_map/reduce_scatter | solution.py:1463
  749.0 1.5 convert_element_type.58
  750.6 1.0 copy.47
  751.6 1.2 fusion.27
  (79 shorter events, 1.9 us)
Async XLA Ops:
  7.2 249.1 %all-gather.2.cloned.1.call-start = ((), (), s32[]{:S(2)}) async-start(), calls=%async_computation.3 | async-start | bytes 18874368 | tf_op jit(solution)/shard_map/all_gather | solution.py:1396
  102.8 499.5 %reduce-scatter.4.cloned.1.call-start = ((), (), s32[]{:S(2)}) async-start(), calls=%async_computation.4 | async-start | bytes 5242880 | tf_op jit(solution)/shard_map/reduce_scatter | solution.py:1463
  112.9 2.7 copy-start
  115.6 4.2 copy-start.6
  115.6 4.2 copy-start.7
  115.6 4.5 copy-start.8
  116.0 8.8 %collective-permute-start.2 = (f32[2,4,256]{2,1,0:T(4,128)S(1)}, f32[2,4,256]{2,1,0:T(4,128)S(1)}, u32[]{:S(2)}, u32[]{:S(2)}) collective-permute-start(f32[2,4,256]{2,1,0:T(4,128)S(1)} %constant_dynamic-update-slice_fusion), channel_id=1, source_target_pairs={{0,3},{1,2},{2,1},{3,0},{4,7},{5,6},{6,5},{7,4},{8,11},{9,10},{10,... | collective-permute-start | bytes 24584 | tf_op jit(solution)/shard_map/ppermute | solution.py:33
  119.5 5.3 collective-permute-start.1
  119.7 5.2 collective-permute-start
  132.2 4.9 collective-permute-start.3
  137.1 1.1 copy-start.9
  138.2 18.1 %copy-start.5 = (bf16[2048,256]{1,0:T(8,128)(2,1)S(1)}, bf16[2048,256]{1,0:T(8,128)(2,1)}, u32[]{:S(2)}) copy-start(bf16[2048,256]{1,0:T(8,128)(2,1)} %param.22) | copy-start | bytes 3145732
  154.7 5.7 copy-start.4
  155.9 4.5 collective-permute-start.4
  413.2 230.9 %reduce-scatter.6.cloned.1.call-start = ((), (), s32[]{:S(2)}) async-start(), calls=%async_computation.5 | async-start | bytes 10485760 | tf_op jit(solution)/shard_map/reduce_scatter | solution.py:1463
  461.7 287.3 %reduce-scatter.8.cloned.1.call-start = ((), (), s32[]{:S(2)}) async-start(), calls=%async_computation.6 | async-start | bytes 5242880 | tf_op jit(solution)/shard_map/reduce_scatter | solution.py:1463
  553.6 3.2 collective-permute-start.5
  581.5 3.5 collective-permute-start.6
  585.0 1.1 copy-start.3
  595.0 3.3 collective-permute-start.8
  596.8 3.4 collective-permute-start.9
  598.2 2.9 collective-permute-start.7
  728.2 9.5 %copy-start.1 = (bf16[256,4096]{1,0:T(8,128)(2,1)S(1)}, bf16[256,4096]{1,0:T(8,128)(2,1)}, u32[]{:S(2)}) copy-start(bf16[256,4096]{1,0:T(8,128)(2,1)} %reduce-scatter.6.cloned.1.call-done) | copy-start | bytes 6291460
  749.0 2.6 copy-start.2
Sparse Core Ops, SparseCore 0:
  103.0 153.2 all-gather.1
  413.3 83.5 reduce-scatter.3
  499.3 144.6 reduce-scatter.5
  646.3 102.6 reduce-scatter.7

commit v5 on v4

--- a/solution.py
+++ b/solution.py
@@ -867,25 +867,30 @@
                 total[:, at] = value
         rounds.append(group)
 
+    if chips > 2:
+        line.advance(1, (0,))
     line.other_core(-1)
     fed_round(0)
     line.other_core(0)
     fed_round(1)
+    if chips > 2:
+        line.advance(1, (1,))
     rounds[0].pass_on()
     rounds[1].pass_on()
+    arrivals = [
+        (cotangent_ref.at[flip(s, j), pl.ds(pl.multiple_of(t * piece, piece), piece), :], upstream.at[pl.ds(j * piece, piece), :])
+        for j in range(chips)
+    ]
+    first = pltpu.make_async_copy(*arrivals[0], coming[0].at[0])
+    others = [remote(*arrivals[j], coming, j, {"context": flip(c, 2 * j)}) for j in range(1, chips)]
     for k in range(1, chips - 1):
-        line.advance(k)
+        if k > 1:
+            line.advance(k)
+        if k + 1 == chips - 1:
+            for copy in [first, *others]:
+                copy.start()
         line.other_core(k)
         fed_round(k + 1)
-        if k + 1 == chips - 1:
-            arrivals = [
-                (cotangent_ref.at[flip(s, j), pl.ds(pl.multiple_of(t * piece, piece), piece), :], upstream.at[pl.ds(j * piece, piece), :])
-                for j in range(chips)
-            ]
-            first = pltpu.make_async_copy(*arrivals[0], coming[0].at[0])
-            others = [remote(*arrivals[j], coming, j, {"context": flip(c, 2 * j)}) for j in range(1, chips)]
-            for copy in [first, *others]:
-                copy.start()
         rounds[k + 1].pass_on()
     down_out = pltpu.make_async_copy(down, down_all_ref, keep_sem.at[2])
     down_out.start()

time: 770 us -> 760 us (0.987)
  Pallas kernels: 630 us -> 620 us
    pallas_call x1, Pallas kernels: 141 us -> 128 us  [feed(): pl.pallas_call(functools.partial(feed_kernel, size, chips, tile), in_spec...]
where the time goes in v5:
time: 760 us; the launch traced here: 750 us
  Pallas kernels  620 us (82%)
  waiting for transfers between devices  50.2 us (7%)
  local copies, waits for them, and re-layouts  23.3 us (3%)
  matrix products  15.3 us (2%)
  other arithmetic  14.7 us (2%)
  between operations  14.4 us (2%)
  starting transfers between devices  11.8 us (2%)
    pallas_call x3, Pallas kernels, exchange(): pl.pallas_call(functools.partial(exchange_kernel, size, width, depth, off...  238 us
    pallas_call x1, Pallas kernels, feed(): pl.pallas_call(functools.partial(feed_kernel, size, chips, tile), in_spec...  128 us
    pallas_call x1, Pallas kernels, start(): pl.pallas_call(functools.partial(start_kernel, size, chips, offsets, len(...  93.7 us
    pallas_call x3, Pallas kernels, rank_sums(): pl.pallas_call(functools.partial(rank_sums_kernel, chips, size, tile, len...  71.8 us
    reduce_scatter x3, waiting for transfers between devices, scatter(): lax.psum_scatter(values, 'context', scatter_dimension=0, axis_index_group...  23.9 us
    pallas_call x1, Pallas kernels, attend_back(): pl.pallas_call(functools.partial(attend_back_kernel, piece, 256), grid_sp...  22.2 us
    pallas_call x3, Pallas kernels, by_rows(): pl.pallas_call(kernel, grid_spec=pltpu.PrefetchScalarGridSpec(num_scalar_...  20.9 us
    pallas_call x1, Pallas kernels, act_back(): pl.pallas_call(functools.partial(act_back_kernel, 512), grid=(count // ro...  16.8 us
  transfers between devices with their start and end apart: 14, of which 9 were waited for; matrix products, arithmetic and copies ran while one was open for 6% of the time, Pallas kernels for 50%

profile of v5, /device:TPU:9, one launch (start us, length us, event | category | flops | bytes accessed | tf_op | source)
XLA Modules:
  0.0 749.9 jit_solution(4958752425302233095)
XLA Ops:
  7.2 0.7 stack.88
  7.9 0.7 stack.87
  8.5 0.6 pad_maximum_fusion.6.refs_5_
  9.1 93.7 %start.1 = (bf16[1024,2048]{1,0:T(8,128)(2,1)}, bf16[2048,2176]{1,0:T(8,128)(2,1)}, bf16[256,4096]{1,0:T(8,128)(2,1)}, bf16[256,2048]{1,0:T(8,128)(2,1)}) custom-call(bf16[4,256,2048]{2,1,0:T(8,128)(2,1)} %refs_0_.1, bf16[256,512]{1,0:T(8,128)(2,1)} %refs_1_.1, bf16[256,512]{1,0:T(8,128)(2,1)} %refs_2_.1, bf16[256,512]{1,0:T(8,128)(2,1)} %refs_3_.2, ...), custom_call_target="tpu_custom_call" | custom-call | bytes 300000000 | tf_op jit(solution)/shard_map/start/pallas_call | solution.py:753
  102.9 10.0 %fusion.raw_ref = f32[1024,1536]{1,0:T(8,128)S(1)} fusion(bf16[1024,2048]{1,0:T(8,128)(2,1)} %get-tuple-element.49.refs_0_, bf16[2048,2176]{1,0:T(8,128)(2,1)} %get-tuple-element.50.w_ref), kind=kOutput, calls=%fused_computation | convolution fusion | flops 6442450944 | bytes 16777216 | tf_op jit(solution)/shard_map/dot_general | solution.py:20
  113.0 2.7 copy-done
  115.6 0.3 fusion.2
  116.0 3.4 collective-permute-start.2
  120.3 1.9 fusion.9
  122.2 1.0 pad_maximum_fusion.2.cosine_ref
  123.2 1.0 pad_maximum_fusion.3.sine_ref
  124.2 0.6 maximum_convert_fusion.gain_ref
  125.2 0.8 pad.9.column_ref
  126.1 6.1 turn.1
  132.2 1.6 collective-permute-start.3
  133.9 0.6 add_multiply_fusion.1.at_ref
  134.5 2.6 collective-permute-done.3.other_ref
  137.1 1.1 copy-done.9
  138.2 16.5 %attend.1 = (bf16[2048,256]{1,0:T(8,128)(2,1)}, f32[2,1,2048]{2,1,0:T(1,128)}) custom-call(s32[32]{0:T(128)} %add_multiply_fusion.1.at_ref, bf16[3,1024,256]{2,1,0:T(8,128)(2,1)} %get-tuple-element.51.own_ref, bf16[3,1024,256]{2,1,0:T(8,128)(2,1)} %copy-done.9), custom_call_target="tpu_custom_call" | custom-call | flops 4294967296 | bytes 4194304 | tf_op jit(solution)/shard_map/attend/pallas_call | solution.py:1269
  154.7 1.2 slice.145
  155.9 0.5 collective-permute-start.4
  156.3 1.6 copy.45
  157.9 2.4 convert_reduce_fusion
  160.4 1.1 pad_maximum_fusion.a_ref.refs_3_
  161.5 77.9 %attended.1 = (bf16[1024,2048]{1,0:T(8,128)(2,1)}, f32[256,2048]{1,0:T(8,128)}, f32[256,2048]{1,0:T(8,128)}) custom-call(bf16[1024,512]{1,0:T(8,128)(2,1)} %pad_maximum_fusion.a_ref.refs_3_, bf16[2048,2176]{1,0:T(8,128)(2,1)} %get-tuple-element.50.w_ref, bf16[256,2048]{1,0:T(8,128)(2,1)} %get-tuple-element.54.refs_0_, f32[1,2048]{1,0:T(1,128)} %bitcast.67), custom_call_target="tpu_custom_call" | custom-call | flops 2147483648 | bytes 240000000 | tf_op jit(solution)/shard_map/attended/pallas_call | solution.py:429
  239.5 16.8 %all-gather.2.cloned.1.call-done.refs_1_.w_ref = bf16[2048,4096]{1,0:T(8,128)(2,1)} async-done(((bf16[256,4096]{1,0:T(8,128)(2,1)}), bf16[2048,4096]{1,0:T(8,128)(2,1)}) %all-gather.2.cloned.1.call-update) | async-done | bytes 16777232 | tf_op jit(solution)/shard_map/all_gather | solution.py:1401
  256.3 127.6 %feed.1 = (bf16[1024,2048]{1,0:T(8,128)(2,1)}, bf16[1024,4096]{1,0:T(8,128)(2,1)}, bf16[1024,2048]{1,0:T(8,128)(2,1)}, bf16[2048,2048]{1,0:T(8,128)(2,1)}, bf16[...) custom-call(bf16[1024,2048]{1,0:T(8,128)(2,1)} %get-tuple-element.55.refs_0_, ...), custom_call_target="tpu_custom_call" | custom-call | flops 25769803776 | bytes 400000000 | tf_op jit(solution)/shard_map/feed/pallas_call | solution.py:956
  383.9 21.7 %rank_sums.3 = (bf16[1024,2048]{1,0:T(8,128)(2,1)}, bf16[256,2048]{1,0:T(8,128)(2,1)}) custom-call(bf16[1024,2048]{1,0:T(8,128)(2,1)} %get-tuple-element.63.refs_0_.grad_ref, bf16[1024,2048]{1,0:T(8,128)(2,1)} %get-tuple-element.59.refs_1_, bf16[256,2048]{1,0:T(8,128)(2,1)} %bitcast.81), custom_call_target="tpu_custom_call" | custom-call | flops 8589934592 | bytes 60000000 | tf_op jit(solution)/shard_map/rank_sums/pallas_call | solution.py:1188
  405.8 16.8 %act_back.1.refs_1_.a_ref = bf16[1024,4096]{1,0:T(8,128)(2,1)} custom-call(bf16[1024,2048]{1,0:T(8,128)(2,1)} %get-tuple-element.63.refs_0_.grad_ref, bf16[2048,2048]{1,0:T(8,128)(2,1)} %get-tuple-element.64.w_ref, bf16[1024,4096]{1,0:T(8,128)(2,1)} %get-tuple-element.65.slopes_ref), custom_call_target="tpu_custom_call" | custom-call | flops 8589934592 | bytes 40000000 | tf_op jit(solution)/shard_map/act_back/pallas_call | solution.py:1085
  422.6 31.2 %rank_sums.4 = (bf16[1024,4096]{1,0:T(8,128)(2,1)}, bf16[768,2048]{1,0:T(8,128)(2,1)}) custom-call(bf16[1024,2048]{1,0:T(8,128)(2,1)} %get-tuple-element.55.refs_0_, bf16[1024,4096]{1,0:T(8,128)(2,1)} %act_back.1.refs_1_.a_ref, bf16[256,2048]{1,0:T(8,128)(2,1)} %bitcast.82), custom_call_target="tpu_custom_call" | custom-call | flops 17179869184 | bytes 60000000 | tf_op jit(solution)/shard_map/rank_sums/pallas_call | solution.py:1188
  453.9 0.6 pad_add_fusion.at_ref
  454.5 5.4 place_rows.2
  459.9 78.4 %hidden_grad.1 = (bf16[1024,2048]{1,0:T(8,128)(2,1)}, f32[256,2048]{1,0:T(8,128)}, f32[8,2048]{1,0:T(8,128)}) custom-call(bf16[1024,4096]{1,0:T(8,128)(2,1)} %act_back.1.refs_1_.a_ref, bf16[2048,4096]{1,0:T(8,128)(2,1)} %all-gather.2.cloned.1.call-done.refs_1_.w_ref, f32[256,2048]{1,0:T(8,128)} %get-tuple-element.69.refs_0_, ...), custom_call_target="tpu_custom_call" | custom-call | flops 17179869184 | bytes 240000000 | tf_op jit(solution)/shard_map/hidden_grad/pallas_call | solution.py:429
  538.3 5.3 fusion.6
  543.6 2.6 collective-permute-start.5
  546.2 1.5 collective-permute-done.5
  547.8 1.0 pad_maximum_fusion.1.grad_ref
  548.8 22.2 %attend_back.1.own_ref = bf16[3,2048,256]{2,1,0:T(8,128)(2,1)} custom-call(s32[32]{0:T(128)} %add_multiply_fusion.1.at_ref, bf16[3,1024,256]{2,1,0:T(8,128)(2,1)} %get-tuple-element.51.own_ref, bf16[3,1024,256]{2,1,0:T(8,128)(2,1)} %copy-done.9, bf16[2048,256]{1,0:T(8,128)(2,1)} %get-tuple-element.53.out_ref, bf16[2048,256]{1,0:T(8,128)(2,1)} %pad_maximum_fusion.1.grad_ref, ...), custom_call_target="tpu_custom_call" | custom-call | flops 10737418240 | bytes 8388608 | tf_op jit(solution)/shard_map/attend_back/pallas_call | solution.py:1332
  571.0 1.5 slice.183
  572.5 0.4 collective-permute-start.6
  573.0 3.0 collective-permute-done.6.other_ref
  576.0 1.1 copy-done.3
  577.1 8.0 %inner.1 = (f32[2,8,1024]{2,1,0:T(8,128)}, f32[2,8,512]{2,1,0:T(8,128)}) custom-call(s32[1]{0:T(128)} %bitcast.2.core_ref, bf16[3,2048,256]{2,1,0:T(8,128)(2,1)} %attend_back.1.own_ref, bf16[3,1024,256]{2,1,0:T(8,128)(2,1)} %copy-done.3, f32[1024,1536]{1,0:T(8,128)} %copy-done, f32[1024,8]{1,0:T(8,128)} %pad.9.column_ref, ...), custom_call_target="tpu_custom_call" | custom-call | tf_op jit(solution)/shard_map/inner/pallas_call | solution.py:1059
  585.2 0.9 fusion.28
  586.1 0.3 collective-permute-start.8
  586.4 1.8 collective-permute-start.9
  588.1 0.6 collective-permute-start.7
  589.0 0.7 collective-permute-done.9
  589.8 1.2 collective-permute-done.7
  591.4 0.8 pad.10.column_ref
  592.2 1.5 convert_bitcast_fusion
  593.7 6.8 raw_grad.1.refs_2_.a_ref
  600.5 18.8 %rank_sums.5 = bf16[1024,2048]{1,0:T(8,128)(2,1)} custom-call(bf16[1024,2048]{1,0:T(8,128)(2,1)} %get-tuple-element.49.refs_0_, bf16[1024,2048]{1,0:T(8,128)(2,1)} %get-tuple-element.72.refs_1_, bf16[1024,1536]{1,0:T(8,128)(2,1)} %raw_grad.1.refs_2_.a_ref, bf16[1024,512]{1,0:T(8,128)(2,1)} %pad_maximum_fusion.a_ref.refs_3_), custom_call_target="tpu_custom_call" | custom-call | flops 8589934592 | bytes 60000000 | tf_op jit(solution)/shard_map/rank_sums/pallas_call | solution.py:1188
  619.3 15.1 %reduce-scatter.6.cloned.1.call-done = bf16[256,4096]{1,0:T(8,128)(2,1)} async-done(((bf16[1024,4096]{1,0:T(8,128)(2,1)}), bf16[256,4096]{1,0:T(8,128)(2,1)}) %reduce-scatter.6.cloned.1.call-update) | async-done | bytes 2097168 | tf_op jit(solution)/shard_map/reduce_scatter | solution.py:1468
  634.4 2.0 copy.48
  636.4 82.1 %tokens_grad.1 = (bf16[1024,2048]{1,0:T(8,128)(2,1)}, f32[8,256]{1,0:T(8,128)}, f32[8,512]{1,0:T(8,128)}) custom-call(bf16[1024,1536]{1,0:T(8,128)(2,1)} %raw_grad.1.refs_2_.a_ref, bf16[2048,2176]{1,0:T(8,128)(2,1)} %get-tuple-element.50.w_ref, f32[256,2048]{1,0:T(8,128)} %get-tuple-element.77.refs_0_, f32[8,2048]{1,0:T(8,128)} %get-tuple-element.78.refs_1_, ...), custom_call_target="tpu_custom_call" | custom-call | flops 6442450944 | bytes 240000000 | tf_op jit(solution)/shard_map/tokens_grad/pallas_call | solution.py:429
  718.5 6.8 place_rows.3
  725.3 1.3 fusion.30
  726.6 1.4 fusion.29
  728.0 2.5 fusion.26
  730.6 8.8 %reduce-scatter.8.cloned.1.call-done = bf16[256,2048]{1,0:T(8,128)(2,1)} async-done(((bf16[1024,2048]{1,0:T(8,128)(2,1)}), bf16[256,2048]{1,0:T(8,128)(2,1)}) %reduce-scatter.8.cloned.1.call-update) | async-done | bytes 1048592 | tf_op jit(solution)/shard_map/reduce_scatter | solution.py:1468
  739.4 1.5 convert_element_type.58
  741.0 1.0 copy.47
  742.0 1.2 fusion.27
  (79 shorter events, 2.3 us)
Async XLA Ops:
  7.2 249.1 %all-gather.2.cloned.1.call-start = ((), (), s32[]{:S(2)}) async-start(), calls=%async_computation.3 | async-start | bytes 18874368 | tf_op jit(solution)/shard_map/all_gather | solution.py:1401
  102.8 489.4 %reduce-scatter.4.cloned.1.call-start = ((), (), s32[]{:S(2)}) async-start(), calls=%async_computation.4 | async-start | bytes 5242880 | tf_op jit(solution)/shard_map/reduce_scatter | solution.py:1468
  112.9 2.7 copy-start
  115.6 4.2 copy-start.6
  115.6 4.2 copy-start.7
  115.6 4.5 copy-start.8
  116.0 8.8 %collective-permute-start.2 = (f32[2,4,256]{2,1,0:T(4,128)S(1)}, f32[2,4,256]{2,1,0:T(4,128)S(1)}, u32[]{:S(2)}, u32[]{:S(2)}) collective-permute-start(f32[2,4,256]{2,1,0:T(4,128)S(1)} %constant_dynamic-update-slice_fusion), channel_id=1, source_target_pairs={{0,3},{1,2},{2,1},{3,0},{4,7},{5,6},{6,5},{7,4},{8,11},{9,10},{10,... | collective-permute-start | bytes 24584 | tf_op jit(solution)/shard_map/ppermute | solution.py:33
  119.5 5.3 collective-permute-start.1
  119.7 5.2 collective-permute-start
  132.2 4.9 collective-permute-start.3
  137.1 1.1 copy-start.9
  138.2 18.1 %copy-start.5 = (bf16[2048,256]{1,0:T(8,128)(2,1)S(1)}, bf16[2048,256]{1,0:T(8,128)(2,1)}, u32[]{:S(2)}) copy-start(bf16[2048,256]{1,0:T(8,128)(2,1)} %param.22) | copy-start | bytes 3145732
  154.7 5.7 copy-start.4
  155.9 4.5 collective-permute-start.4
  405.7 228.7 %reduce-scatter.6.cloned.1.call-start = ((), (), s32[]{:S(2)}) async-start(), calls=%async_computation.5 | async-start | bytes 10485760 | tf_op jit(solution)/shard_map/reduce_scatter | solution.py:1468
  453.8 285.6 %reduce-scatter.8.cloned.1.call-start = ((), (), s32[]{:S(2)}) async-start(), calls=%async_computation.6 | async-start | bytes 5242880 | tf_op jit(solution)/shard_map/reduce_scatter | solution.py:1468
  543.6 4.1 collective-permute-start.5
  572.5 3.5 collective-permute-start.6
  576.0 1.1 copy-start.3
  586.1 3.0 collective-permute-start.8
  586.4 3.4 collective-permute-start.9
  588.1 2.9 collective-permute-start.7
  718.5 9.5 %copy-start.1 = (bf16[256,4096]{1,0:T(8,128)(2,1)S(1)}, bf16[256,4096]{1,0:T(8,128)(2,1)}, u32[]{:S(2)}) copy-start(bf16[256,4096]{1,0:T(8,128)(2,1)} %reduce-scatter.6.cloned.1.call-done) | copy-start | bytes 6291460
  739.4 2.6 copy-start.2
Sparse Core Ops, SparseCore 0:
  103.0 153.2 all-gather.1
  405.8 81.4 reduce-scatter.3
  489.8 144.6 reduce-scatter.5
  636.7 102.6 reduce-scatter.7

commit v6 on v5

--- a/solution.py
+++ b/solution.py
@@ -896,10 +896,6 @@
     down_out.start()
     for group in rounds:
         group.wait()
-    first.wait()
-    for copy in others:
-        copy.wait_recv()
-
     used = 2 if size == 4 else size - 1
 
     def finish_rows(side):
@@ -918,8 +914,13 @@
         lax.fori_loop(0, rows // 32, step, 0)
 
     share = Gather(size, t, mine, every, gather, own_sem)
+    first.wait()
+    for copy in others[: chips // 2 - 1]:
+        copy.wait_recv()
     finish_rows(0)
     share.start(0)
+    for copy in others[chips // 2 - 1 :]:
+        copy.wait_recv()
     finish_rows(1)
     share.start(1)
     kept = pltpu.make_async_copy(output.at[pl.ds(0, piece), :], pieces.at[0], going[0].at[0])

time: 760 us -> 758 us (level)
  no operation moved by 1% of the time
where the time goes in v6:
time: 758 us; the launch traced here: 748 us
  Pallas kernels  613 us (81%)
  waiting for transfers between devices  55.6 us (7%)
  local copies, waits for them, and re-layouts  23.3 us (3%)
  matrix products  15.3 us (2%)
  other arithmetic  14.7 us (2%)
  between operations  14.4 us (2%)
  starting transfers between devices  12 us (2%)
    pallas_call x3, Pallas kernels, exchange(): pl.pallas_call(functools.partial(exchange_kernel, size, width, depth, off...  238 us
    pallas_call x1, Pallas kernels, feed(): pl.pallas_call(functools.partial(feed_kernel, size, chips, tile), in_spec...  125 us
    pallas_call x1, Pallas kernels, start(): pl.pallas_call(functools.partial(start_kernel, size, chips, offsets, len(...  93.7 us
    pallas_call x3, Pallas kernels, rank_sums(): pl.pallas_call(functools.partial(rank_sums_kernel, chips, size, tile, len...  68.4 us
    reduce_scatter x3, waiting for transfers between devices, scatter(): lax.psum_scatter(values, 'context', scatter_dimension=0, axis_index_group...  29.7 us
    pallas_call x1, Pallas kernels, attend_back(): pl.pallas_call(functools.partial(attend_back_kernel, piece, 256), grid_sp...  22 us
    pallas_call x3, Pallas kernels, by_rows(): pl.pallas_call(kernel, grid_spec=pltpu.PrefetchScalarGridSpec(num_scalar_...  20.9 us
    all_gather x1, waiting for transfers between devices, local(): w_gate_up = lax.all_gather(gate_up_shard, 'context', axis=0, tiled=True)  16.8 us
  transfers between devices with their start and end apart: 14, of which 9 were waited for; matrix products, arithmetic and copies ran while one was open for 6% of the time, Pallas kernels for 50%

profile of v6, /device:TPU:9, one launch (start us, length us, event | category | flops | bytes accessed | tf_op | source)
XLA Modules:
  0.0 748.2 jit_solution(9592779601385348793)
XLA Ops:
  7.2 0.7 stack.88
  7.9 0.7 stack.87
  8.5 0.6 pad_maximum_fusion.6.refs_5_
  9.1 93.7 %start.1 = (bf16[1024,2048]{1,0:T(8,128)(2,1)}, bf16[2048,2176]{1,0:T(8,128)(2,1)}, bf16[256,4096]{1,0:T(8,128)(2,1)}, bf16[256,2048]{1,0:T(8,128)(2,1)}) custom-call(bf16[4,256,2048]{2,1,0:T(8,128)(2,1)} %refs_0_.1, bf16[256,512]{1,0:T(8,128)(2,1)} %refs_1_.1, bf16[256,512]{1,0:T(8,128)(2,1)} %refs_2_.1, bf16[256,512]{1,0:T(8,128)(2,1)} %refs_3_.2, ...), custom_call_target="tpu_custom_call" | custom-call | bytes 300000000 | tf_op jit(solution)/shard_map/start/pallas_call | solution.py:753
  102.9 10.0 %fusion.raw_ref = f32[1024,1536]{1,0:T(8,128)S(1)} fusion(bf16[1024,2048]{1,0:T(8,128)(2,1)} %get-tuple-element.49.refs_0_, bf16[2048,2176]{1,0:T(8,128)(2,1)} %get-tuple-element.50.w_ref), kind=kOutput, calls=%fused_computation | convolution fusion | flops 6442450944 | bytes 16777216 | tf_op jit(solution)/shard_map/dot_general | solution.py:20
  113.0 2.7 copy-done
  115.6 0.3 fusion.2
  116.0 3.4 collective-permute-start.2
  120.3 1.9 fusion.9
  122.2 1.0 pad_maximum_fusion.2.cosine_ref
  123.2 1.0 pad_maximum_fusion.3.sine_ref
  124.2 0.6 maximum_convert_fusion.gain_ref
  125.2 0.8 pad.9.column_ref
  126.1 6.1 turn.1
  132.2 1.6 collective-permute-start.3
  133.9 0.6 add_multiply_fusion.1.at_ref
  134.5 2.6 collective-permute-done.3.other_ref
  137.1 1.1 copy-done.9
  138.2 16.5 %attend.1 = (bf16[2048,256]{1,0:T(8,128)(2,1)}, f32[2,1,2048]{2,1,0:T(1,128)}) custom-call(s32[32]{0:T(128)} %add_multiply_fusion.1.at_ref, bf16[3,1024,256]{2,1,0:T(8,128)(2,1)} %get-tuple-element.51.own_ref, bf16[3,1024,256]{2,1,0:T(8,128)(2,1)} %copy-done.9), custom_call_target="tpu_custom_call" | custom-call | flops 4294967296 | bytes 4194304 | tf_op jit(solution)/shard_map/attend/pallas_call | solution.py:1270
  154.7 1.2 slice.145
  155.9 0.5 collective-permute-start.4
  156.3 1.6 copy.45
  157.9 2.4 convert_reduce_fusion
  160.4 1.1 pad_maximum_fusion.a_ref.refs_3_
  161.5 77.9 %attended.1 = (bf16[1024,2048]{1,0:T(8,128)(2,1)}, f32[256,2048]{1,0:T(8,128)}, f32[256,2048]{1,0:T(8,128)}) custom-call(bf16[1024,512]{1,0:T(8,128)(2,1)} %pad_maximum_fusion.a_ref.refs_3_, bf16[2048,2176]{1,0:T(8,128)(2,1)} %get-tuple-element.50.w_ref, bf16[256,2048]{1,0:T(8,128)(2,1)} %get-tuple-element.54.refs_0_, f32[1,2048]{1,0:T(1,128)} %bitcast.67), custom_call_target="tpu_custom_call" | custom-call | flops 2147483648 | bytes 240000000 | tf_op jit(solution)/shard_map/attended/pallas_call | solution.py:429
  239.5 16.8 %all-gather.2.cloned.1.call-done.refs_1_.w_ref = bf16[2048,4096]{1,0:T(8,128)(2,1)} async-done(((bf16[256,4096]{1,0:T(8,128)(2,1)}), bf16[2048,4096]{1,0:T(8,128)(2,1)}) %all-gather.2.cloned.1.call-update) | async-done | bytes 16777232 | tf_op jit(solution)/shard_map/all_gather | solution.py:1402
  256.3 124.8 %feed.1 = (bf16[1024,2048]{1,0:T(8,128)(2,1)}, bf16[1024,4096]{1,0:T(8,128)(2,1)}, bf16[1024,2048]{1,0:T(8,128)(2,1)}, bf16[2048,2048]{1,0:T(8,128)(2,1)}, bf16[...) custom-call(bf16[1024,2048]{1,0:T(8,128)(2,1)} %get-tuple-element.55.refs_0_, ...), custom_call_target="tpu_custom_call" | custom-call | flops 25769803776 | bytes 400000000 | tf_op jit(solution)/shard_map/feed/pallas_call | solution.py:957
  381.1 18.0 %rank_sums.3 = (bf16[1024,2048]{1,0:T(8,128)(2,1)}, bf16[256,2048]{1,0:T(8,128)(2,1)}) custom-call(bf16[1024,2048]{1,0:T(8,128)(2,1)} %get-tuple-element.63.refs_0_.grad_ref, bf16[1024,2048]{1,0:T(8,128)(2,1)} %get-tuple-element.59.refs_1_, bf16[256,2048]{1,0:T(8,128)(2,1)} %bitcast.81), custom_call_target="tpu_custom_call" | custom-call | flops 8589934592 | bytes 60000000 | tf_op jit(solution)/shard_map/rank_sums/pallas_call | solution.py:1189
  399.2 16.3 %act_back.1.refs_1_.a_ref = bf16[1024,4096]{1,0:T(8,128)(2,1)} custom-call(bf16[1024,2048]{1,0:T(8,128)(2,1)} %get-tuple-element.63.refs_0_.grad_ref, bf16[2048,2048]{1,0:T(8,128)(2,1)} %get-tuple-element.64.w_ref, bf16[1024,4096]{1,0:T(8,128)(2,1)} %get-tuple-element.65.slopes_ref), custom_call_target="tpu_custom_call" | custom-call | flops 8589934592 | bytes 40000000 | tf_op jit(solution)/shard_map/act_back/pallas_call | solution.py:1086
  415.5 31.5 %rank_sums.4 = (bf16[1024,4096]{1,0:T(8,128)(2,1)}, bf16[768,2048]{1,0:T(8,128)(2,1)}) custom-call(bf16[1024,2048]{1,0:T(8,128)(2,1)} %get-tuple-element.55.refs_0_, bf16[1024,4096]{1,0:T(8,128)(2,1)} %act_back.1.refs_1_.a_ref, bf16[256,2048]{1,0:T(8,128)(2,1)} %bitcast.82), custom_call_target="tpu_custom_call" | custom-call | flops 17179869184 | bytes 60000000 | tf_op jit(solution)/shard_map/rank_sums/pallas_call | solution.py:1189
  447.1 0.6 pad_add_fusion.at_ref
  447.7 5.5 place_rows.2
  453.2 77.9 %hidden_grad.1 = (bf16[1024,2048]{1,0:T(8,128)(2,1)}, f32[256,2048]{1,0:T(8,128)}, f32[8,2048]{1,0:T(8,128)}) custom-call(bf16[1024,4096]{1,0:T(8,128)(2,1)} %act_back.1.refs_1_.a_ref, bf16[2048,4096]{1,0:T(8,128)(2,1)} %all-gather.2.cloned.1.call-done.refs_1_.w_ref, f32[256,2048]{1,0:T(8,128)} %get-tuple-element.69.refs_0_, ...), custom_call_target="tpu_custom_call" | custom-call | flops 17179869184 | bytes 240000000 | tf_op jit(solution)/shard_map/hidden_grad/pallas_call | solution.py:429
  531.1 5.3 fusion.6
  536.4 2.8 collective-permute-start.5
  539.2 1.5 collective-permute-done.5
  540.8 1.0 pad_maximum_fusion.1.grad_ref
  541.8 22.0 %attend_back.1.own_ref = bf16[3,2048,256]{2,1,0:T(8,128)(2,1)} custom-call(s32[32]{0:T(128)} %add_multiply_fusion.1.at_ref, bf16[3,1024,256]{2,1,0:T(8,128)(2,1)} %get-tuple-element.51.own_ref, bf16[3,1024,256]{2,1,0:T(8,128)(2,1)} %copy-done.9, bf16[2048,256]{1,0:T(8,128)(2,1)} %get-tuple-element.53.out_ref, bf16[2048,256]{1,0:T(8,128)(2,1)} %pad_maximum_fusion.1.grad_ref, ...), custom_call_target="tpu_custom_call" | custom-call | flops 10737418240 | bytes 8388608 | tf_op jit(solution)/shard_map/attend_back/pallas_call | solution.py:1333
  563.8 1.5 slice.183
  565.4 0.4 collective-permute-start.6
  565.8 3.0 collective-permute-done.6.other_ref
  568.8 1.1 copy-done.3
  570.0 8.0 %inner.1 = (f32[2,8,1024]{2,1,0:T(8,128)}, f32[2,8,512]{2,1,0:T(8,128)}) custom-call(s32[1]{0:T(128)} %bitcast.2.core_ref, bf16[3,2048,256]{2,1,0:T(8,128)(2,1)} %attend_back.1.own_ref, bf16[3,1024,256]{2,1,0:T(8,128)(2,1)} %copy-done.3, f32[1024,1536]{1,0:T(8,128)} %copy-done, f32[1024,8]{1,0:T(8,128)} %pad.9.column_ref, ...), custom_call_target="tpu_custom_call" | custom-call | tf_op jit(solution)/shard_map/inner/pallas_call | solution.py:1060
  578.0 0.9 fusion.28
  578.9 0.8 collective-permute-start.8
  579.6 1.1 collective-permute-start.9
  580.7 0.9 collective-permute-start.7
  581.9 1.2 collective-permute-done.9
  583.2 0.5 collective-permute-done.7
  584.0 0.8 pad.10.column_ref
  584.8 1.5 convert_bitcast_fusion
  586.3 6.8 raw_grad.1.refs_2_.a_ref
  593.0 18.8 %rank_sums.5 = bf16[1024,2048]{1,0:T(8,128)(2,1)} custom-call(bf16[1024,2048]{1,0:T(8,128)(2,1)} %get-tuple-element.49.refs_0_, bf16[1024,2048]{1,0:T(8,128)(2,1)} %get-tuple-element.72.refs_1_, bf16[1024,1536]{1,0:T(8,128)(2,1)} %raw_grad.1.refs_2_.a_ref, bf16[1024,512]{1,0:T(8,128)(2,1)} %pad_maximum_fusion.a_ref.refs_3_), custom_call_target="tpu_custom_call" | custom-call | flops 8589934592 | bytes 60000000 | tf_op jit(solution)/shard_map/rank_sums/pallas_call | solution.py:1189
  611.9 20.9 %reduce-scatter.6.cloned.1.call-done = bf16[256,4096]{1,0:T(8,128)(2,1)} async-done(((bf16[1024,4096]{1,0:T(8,128)(2,1)}), bf16[256,4096]{1,0:T(8,128)(2,1)}) %reduce-scatter.6.cloned.1.call-update) | async-done | bytes 2097168 | tf_op jit(solution)/shard_map/reduce_scatter | solution.py:1469
  632.8 2.0 copy.48
  634.8 82.1 %tokens_grad.1 = (bf16[1024,2048]{1,0:T(8,128)(2,1)}, f32[8,256]{1,0:T(8,128)}, f32[8,512]{1,0:T(8,128)}) custom-call(bf16[1024,1536]{1,0:T(8,128)(2,1)} %raw_grad.1.refs_2_.a_ref, bf16[2048,2176]{1,0:T(8,128)(2,1)} %get-tuple-element.50.w_ref, f32[256,2048]{1,0:T(8,128)} %get-tuple-element.77.refs_0_, f32[8,2048]{1,0:T(8,128)} %get-tuple-element.78.refs_1_, ...), custom_call_target="tpu_custom_call" | custom-call | flops 6442450944 | bytes 240000000 | tf_op jit(solution)/shard_map/tokens_grad/pallas_call | solution.py:429
  716.9 6.8 place_rows.3
  723.7 1.3 fusion.30
  725.0 1.4 fusion.29
  726.4 2.5 fusion.26
  728.9 8.8 %reduce-scatter.8.cloned.1.call-done = bf16[256,2048]{1,0:T(8,128)(2,1)} async-done(((bf16[1024,2048]{1,0:T(8,128)(2,1)}), bf16[256,2048]{1,0:T(8,128)(2,1)}) %reduce-scatter.8.cloned.1.call-update) | async-done | bytes 1048592 | tf_op jit(solution)/shard_map/reduce_scatter | solution.py:1469
  737.7 1.5 convert_element_type.58
  739.3 1.0 copy.47
  740.3 1.2 fusion.27
  (79 shorter events, 2.3 us)
Async XLA Ops:
  7.2 249.1 %all-gather.2.cloned.1.call-start = ((), (), s32[]{:S(2)}) async-start(), calls=%async_computation.3 | async-start | bytes 18874368 | tf_op jit(solution)/shard_map/all_gather | solution.py:1402
  102.8 482.0 %reduce-scatter.4.cloned.1.call-start = ((), (), s32[]{:S(2)}) async-start(), calls=%async_computation.4 | async-start | bytes 5242880 | tf_op jit(solution)/shard_map/reduce_scatter | solution.py:1469
  112.9 2.7 copy-start
  115.6 4.2 copy-start.6
  115.6 4.2 copy-start.7
  115.6 4.5 copy-start.8
  116.0 8.8 %collective-permute-start.2 = (f32[2,4,256]{2,1,0:T(4,128)S(1)}, f32[2,4,256]{2,1,0:T(4,128)S(1)}, u32[]{:S(2)}, u32[]{:S(2)}) collective-permute-start(f32[2,4,256]{2,1,0:T(4,128)S(1)} %constant_dynamic-update-slice_fusion), channel_id=1, source_target_pairs={{0,3},{1,2},{2,1},{3,0},{4,7},{5,6},{6,5},{7,4},{8,11},{9,10},{10,... | collective-permute-start | bytes 24584 | tf_op jit(solution)/shard_map/ppermute | solution.py:33
  119.5 5.3 collective-permute-start.1
  119.7 5.2 collective-permute-start
  132.2 4.9 collective-permute-start.3
  137.1 1.1 copy-start.9
  138.2 18.1 %copy-start.5 = (bf16[2048,256]{1,0:T(8,128)(2,1)S(1)}, bf16[2048,256]{1,0:T(8,128)(2,1)}, u32[]{:S(2)}) copy-start(bf16[2048,256]{1,0:T(8,128)(2,1)} %param.22) | copy-start | bytes 3145732
  154.7 5.7 copy-start.4
  155.9 4.5 collective-permute-start.4
  399.2 233.6 %reduce-scatter.6.cloned.1.call-start = ((), (), s32[]{:S(2)}) async-start(), calls=%async_computation.5 | async-start | bytes 10485760 | tf_op jit(solution)/shard_map/reduce_scatter | solution.py:1469
  447.0 290.7 %reduce-scatter.8.cloned.1.call-start = ((), (), s32[]{:S(2)}) async-start(), calls=%async_computation.6 | async-start | bytes 5242880 | tf_op jit(solution)/shard_map/reduce_scatter | solution.py:1469
  536.4 4.4 collective-permute-start.5
  565.4 3.5 collective-permute-start.6
  568.8 1.1 copy-start.3
  578.9 3.0 collective-permute-start.8
  579.6 3.4 collective-permute-start.9
  580.7 2.9 collective-permute-start.7
  716.9 9.5 %copy-start.1 = (bf16[256,4096]{1,0:T(8,128)(2,1)S(1)}, bf16[256,4096]{1,0:T(8,128)(2,1)}, u32[]{:S(2)}) copy-start(bf16[256,4096]{1,0:T(8,128)(2,1)} %reduce-scatter.6.cloned.1.call-done) | copy-start | bytes 6291460
  737.7 2.6 copy-start.2
Sparse Core Ops, SparseCore 0:
  103.0 153.2 all-gather.1
  399.3 86.2 reduce-scatter.3
  488.0 144.6 reduce-scatter.5
  635.0 102.6 reduce-scatter.7
